TPU v7x, 256 devices: a whole 4x4x8 slice. The times are simulated.
256 devices in a mesh: gx: 32 (over z_lo, y, core), gy: 8 (over z_hi, x).
Axes of the slice: x: 4, y: 4, z: 8 (z_hi: 2, z_lo: 4; z = z_hi * 4 + z_lo), core: 2. Of those that a mesh axis runs over, the one named last changes fastest.
Arguments:
- tsdf: float32 [256, 1024, 1024], P('gx', None, 'gy'), may hold values from -6 to 6
- shift_x: int32 [256], P('gx'), may hold values from -1 to 0
- shift_y: int32 [256], P('gx'), may hold values from -1 to 0
- frac_x: float32 [256], P('gx'), may hold values from 0 to 1
- frac_y: float32 [256], P('gx'), may hold values from 0 to 1
- extinction: float32 [256], P('gx'), may hold values from 0.00390625 to 0.015625
- color_slope: float32 [3], replicated, may hold values from -4 to 4
- color_offset: float32 [3], replicated, may hold values from -3 to 3
- view_mask: int32 [1], replicated, may hold values from 0 to 31
Outputs:
- frame: float32 [4, 1024, 1024], P(None, None, 'gy')
Inputs may be any that keep to these rules, and one draw needn't show every extreme that they name: `shift_x`: each entry is -1 or 0. `shift_y`: each entry is -1 or 0.
All inputs are finite; a program needn't handle non-finite values.
Results may differ from a plain program's by a relative error of at most 0.0003.
Values sent between devices are 32-bit elements; how exact they have to be, the bound alone decides.
No kernel may reach another device: no remote copies, remote signals or barrier semaphores. Data moves between devices by JAX's collectives and lax.ppermute only.
A program may use at most 128 MiB of HBM per device.

v0:
```python
import jax
import jax.numpy as jnp
from jax import lax
from jax.sharding import PartitionSpec as P


def with_halo(cells, sides, width):
    for axis, dim in sides:
        count = lax.axis_size(axis)
        ends = count - 1
        head = lax.slice_in_dim(cells, 0, width, axis=dim)
        tail = lax.slice_in_dim(cells, cells.shape[dim] - width, cells.shape[dim], axis=dim)
        cells = jnp.concatenate(
            [
                lax.ppermute(tail, axis, [(i, (i + 1) % count) for i in range(ends)]),
                cells,
                lax.ppermute(head, axis, [((i + 1) % count, i) for i in range(ends)]),
            ],
            axis=dim,
        )
    return cells


def from_partner(block, axis, distance):
    count = lax.axis_size(axis)
    route = []
    for low in range(count):
        high = low | 1 << distance
        if high != low and high < count:
            route += [(low, high), (high, low)]
    return lax.ppermute(block, axis, route)


def sample_slice(slab, row_shift, col_shift, row_frac, col_frac):
    row_count = slab.shape[0] - 2
    col_count = slab.shape[1] - 2
    window = lax.dynamic_slice(slab, (row_shift + 1, col_shift + 1), (row_count + 1, col_count + 1))
    blended = window[:-1] * (1.0 - row_frac) + window[1:] * row_frac
    return blended[:, :-1] * (1.0 - col_frac) + blended[:, 1:] * col_frac


def render(padded, shift_x, shift_y, frac_x, frac_y, extinction, color_slope, color_offset):
    values = jax.vmap(sample_slice)(padded, shift_x, shift_y, frac_x, frac_y)
    density = jnp.exp(-values * values)
    opacity_step = 1.0 - jnp.exp(-extinction[:, None, None] * density)
    transmit = jnp.cumprod(1.0 - opacity_step, axis=0)
    before = jnp.concatenate([jnp.ones_like(transmit[:1]), transmit[:-1]], axis=0)
    weight = before * opacity_step
    channels = []
    for channel in range(3):
        colour = jax.nn.sigmoid(color_slope[channel] * values + color_offset[channel])
        channels.append(jnp.sum(weight * colour, axis=0))
    channels.append(1.0 - transmit[-1])
    return jnp.stack(channels)


def composite(front, back):
    return front + (1.0 - front[3:4]) * back


def body(tsdf, shift_x, shift_y, frac_x, frac_y, extinction, color_slope, color_offset, view_mask):
    widened = with_halo(tsdf, (("gy", 2),), 1)
    padded = jnp.pad(widened, ((0, 0), (1, 1), (0, 0)))
    partial_value = render(
        padded, shift_x, shift_y, frac_x, frac_y, extinction, color_slope, color_offset
    )
    row_count = partial_value.shape[1]
    col_count = partial_value.shape[2]
    count_x = lax.axis_size("gx")
    index_x = lax.axis_index("gx")
    mask_x = view_mask[0]
    tile = row_count * col_count // count_x
    image = partial_value.reshape(4, count_x, tile)
    for bit in range(count_x.bit_length() - 1):
        halves = image.reshape(4, image.shape[1] // 2, 2, tile)
        own_bit = index_x >> bit & 1
        kept = jnp.where(own_bit == 0, halves[:, :, 0], halves[:, :, 1])
        handed = jnp.where(own_bit == 0, halves[:, :, 1], halves[:, :, 0])
        partner = from_partner(handed, "gx", bit)
        self_front = own_bit ^ mask_x >> bit & 1 == 0
        image = jnp.where(self_front, composite(kept, partner), composite(partner, kept))
    final_tile = image[:, 0]
    band = lax.all_gather(final_tile, "gx", axis=1, tiled=True)
    return band.reshape(4, row_count, col_count)


def solution(mesh):
    in_specs = (P("gx", None, "gy"), P("gx"), P("gx"), P("gx"), P("gx"), P("gx"), P(), P(), P())
    out_specs = P(None, None, "gy")
    return jax.shard_map(body, mesh=mesh, in_specs=in_specs, out_specs=out_specs, check_vma=False)
```

profile of v0, /device:TPU:5, one launch (start us, length us, event | category | flops | bytes accessed | tf_op | source)
XLA Modules:
  0.0 243.1 jit_solution(12761710436557226671)
XLA Ops:
  6.5 7.9 %fusion.28 = (f32[8,1024,1]{2,1,0:T(8,128)}, f32[8,1024,1]{2,1,0:T(8,128)}) fusion(f32[8,1024,128]{2,1,0:T(8,128)} %param.9), kind=kLoop, calls=%fused_computation.89 | loop fusion | bytes 131072 | tf_op jit(solution)/shard_map/slice | solution.py:12
  14.5 2.9 %copy.104 = f32[8,1024,1]{1,0,2:T(8,128)S(1)} copy(f32[8,1024,1]{2,1,0:T(8,128)} %get-tuple-element.27) | data formatting | bytes 65536
  17.4 2.8 %collective-permute-start = (f32[8,1024,1]{1,0,2:T(8,128)S(1)}, f32[8,1024,1]{1,0,2:T(8,128)S(1)}, u32[]{:S(2)}, u32[]{:S(2)}) collective-permute-start(f32[8,1024,1]{1,0,2:T(8,128)S(1)} %copy.104), channel_id=1, source_target_pairs={{0,1},{1,2},{2,3},{3,4},{4,5},{5,6},{6,7},{8,9},{9,10},{10,11},{11... | collective-permute-start | bytes 98312 | tf_op jit(solution)/shard_map/ppermute | solution.py:15
  20.2 2.9 %copy.105 = f32[8,1024,1]{1,0,2:T(8,128)S(1)} copy(f32[8,1024,1]{2,1,0:T(8,128)} %get-tuple-element.28) | data formatting | bytes 65536
  35.7 8.8 %select_maximum_fusion = f32[8,1026,130]{2,1,0:T(8,128)} fusion(f32[8,1024,1]{2,1,0:T(8,128)} %copy.79, f32[8,1024,128]{2,1,0:T(8,128)} %param.9, f32[8,1024,1]{2,1,0:T(8,128)} %copy.78), kind=kLoop, calls=%fused_computation.4 | loop fusion | flops 8536320 | bytes 8528000 | tf_op jit(solution)/shard_map/concatenate | solution.py:13
  44.5 40.3 %while.1 = (s32[]{:T(128)}, f32[8,1026,130]{2,1,0:T(8,128)}, s32[8,3]{0,1:T(4,128)S(1)}, f32[8,1025,129]{2,1,0:T(8,128)}, s32[]{:T(128)}) while((s32[]{:T(128)}, f32[8,1026,130]{2,1,0:T(8,128)}, s32[8,3]{0,1:T(4,128)S(1)}, f32[8,1025,129]{2,1,0:T(8,128)}, s32[]{:T(128)}) %tuple.31), condition=%wide.while_cond, body=%wide.while_body.sunk | while | flops 2 | bytes 2115697 | solution.py:37
  45.2 4.5 %dynamic-slice_dynamic-update-slice_fusion.2 = f32[8,1025,129]{2,1,0:T(8,128)} fusion(f32[8,1025,129]{2,1,0:T(8,128)} %get-tuple-element.81, s32[]{:T(128)} %get-tuple-element.78, f32[8,1026,130]{2,1,0:T(8,128)} %get-tuple-element.84, s32[]{:T(128)} %bitcast.150, s32[]{:T(128)} %bitcast.151, s32[]{:T(128)} %bitcast.152), kind=kLoop, calls=%fused_computation.clone.1 | loop fusion | bytes 2115584 | tf_op jit(solution)/shard_map/vmap()/gather
  50.3 4.4 %dynamic-slice_dynamic-update-slice_fusion.2 = f32[8,1025,129]{2,1,0:T(8,128)} fusion(f32[8,1025,129]{2,1,0:T(8,128)} %get-tuple-element.81, s32[]{:T(128)} %get-tuple-element.78, f32[8,1026,130]{2,1,0:T(8,128)} %get-tuple-element.84, s32[]{:T(128)} %bitcast.150, s32[]{:T(128)} %bitcast.151, s32[]{:T(128)} %bitcast.152), kind=kLoop, calls=%fused_computation.clone.1 | loop fusion | bytes 2115584 | tf_op jit(solution)/shard_map/vmap()/gather
  55.3 4.4 %dynamic-slice_dynamic-update-slice_fusion.2 = f32[8,1025,129]{2,1,0:T(8,128)} fusion(f32[8,1025,129]{2,1,0:T(8,128)} %get-tuple-element.81, s32[]{:T(128)} %get-tuple-element.78, f32[8,1026,130]{2,1,0:T(8,128)} %get-tuple-element.84, s32[]{:T(128)} %bitcast.150, s32[]{:T(128)} %bitcast.151, s32[]{:T(128)} %bitcast.152), kind=kLoop, calls=%fused_computation.clone.1 | loop fusion | bytes 2115584 | tf_op jit(solution)/shard_map/vmap()/gather
  60.3 4.4 %dynamic-slice_dynamic-update-slice_fusion.2 = f32[8,1025,129]{2,1,0:T(8,128)} fusion(f32[8,1025,129]{2,1,0:T(8,128)} %get-tuple-element.81, s32[]{:T(128)} %get-tuple-element.78, f32[8,1026,130]{2,1,0:T(8,128)} %get-tuple-element.84, s32[]{:T(128)} %bitcast.150, s32[]{:T(128)} %bitcast.151, s32[]{:T(128)} %bitcast.152), kind=kLoop, calls=%fused_computation.clone.1 | loop fusion | bytes 2115584 | tf_op jit(solution)/shard_map/vmap()/gather
  65.4 4.5 %dynamic-slice_dynamic-update-slice_fusion.2 = f32[8,1025,129]{2,1,0:T(8,128)} fusion(f32[8,1025,129]{2,1,0:T(8,128)} %get-tuple-element.81, s32[]{:T(128)} %get-tuple-element.78, f32[8,1026,130]{2,1,0:T(8,128)} %get-tuple-element.84, s32[]{:T(128)} %bitcast.150, s32[]{:T(128)} %bitcast.151, s32[]{:T(128)} %bitcast.152), kind=kLoop, calls=%fused_computation.clone.1 | loop fusion | bytes 2115584 | tf_op jit(solution)/shard_map/vmap()/gather
  70.4 4.4 %dynamic-slice_dynamic-update-slice_fusion.2 = f32[8,1025,129]{2,1,0:T(8,128)} fusion(f32[8,1025,129]{2,1,0:T(8,128)} %get-tuple-element.81, s32[]{:T(128)} %get-tuple-element.78, f32[8,1026,130]{2,1,0:T(8,128)} %get-tuple-element.84, s32[]{:T(128)} %bitcast.150, s32[]{:T(128)} %bitcast.151, s32[]{:T(128)} %bitcast.152), kind=kLoop, calls=%fused_computation.clone.1 | loop fusion | bytes 2115584 | tf_op jit(solution)/shard_map/vmap()/gather
  75.5 4.4 %dynamic-slice_dynamic-update-slice_fusion.2 = f32[8,1025,129]{2,1,0:T(8,128)} fusion(f32[8,1025,129]{2,1,0:T(8,128)} %get-tuple-element.81, s32[]{:T(128)} %get-tuple-element.78, f32[8,1026,130]{2,1,0:T(8,128)} %get-tuple-element.84, s32[]{:T(128)} %bitcast.150, s32[]{:T(128)} %bitcast.151, s32[]{:T(128)} %bitcast.152), kind=kLoop, calls=%fused_computation.clone.1 | loop fusion | bytes 2115584 | tf_op jit(solution)/shard_map/vmap()/gather
  80.5 4.4 %dynamic-slice_dynamic-update-slice_fusion.2 = f32[8,1025,129]{2,1,0:T(8,128)} fusion(f32[8,1025,129]{2,1,0:T(8,128)} %get-tuple-element.81, s32[]{:T(128)} %get-tuple-element.78, f32[8,1026,130]{2,1,0:T(8,128)} %get-tuple-element.84, s32[]{:T(128)} %bitcast.150, s32[]{:T(128)} %bitcast.151, s32[]{:T(128)} %bitcast.152), kind=kLoop, calls=%fused_computation.clone.1 | loop fusion | bytes 2115584 | tf_op jit(solution)/shard_map/vmap()/gather
  84.9 10.1 %multiply_add_fusion = f32[8,1024,129]{2,1,0:T(8,128)} fusion(f32[8,1025,129]{2,1,0:T(8,128)} %get-tuple-element.12, f32[8]{0:T(128)S(1)} %copy-done.4, f32[8]{0:T(128)S(1)} %broadcast_subtract_fusion.1), kind=kLoop, calls=%fused_computation.7 | loop fusion | flops 3170304 | bytes 12681280 | tf_op jit(solution)/shard_map/vmap()/add | solution.py:38
  94.9 8.6 %fusion.6 = f32[8,1024,128]{2,1,0:T(8,128)} fusion(f32[8]{0:T(128)S(1)} %neg.16, f32[8,1024,129]{2,1,0:T(8,128)} %multiply_add_fusion, f32[8]{0:T(128)S(1)} %copy-done.3, f32[8]{0:T(128)S(1)} %broadcast_subtract_fusion), kind=kOutput, calls=%fused_computation.20 | output fusion | flops 15728640 | bytes 8421472 | tf_op jit(solution)/shard_map/jit(cumprod)/reduce_window | solution.py:46
  108.2 9.3 %multiply_reduce_fusion = (f32[1024,128]{1,0:T(8,128)S(1)}, f32[1024,128]{1,0:T(8,128)S(1)}, f32[1024,128]{1,0:T(8,128)S(1)}) fusion(f32[7,1024,128]{2,1,0:T(8,128)S(1)} %slice.167, f32[]{:T(128)} %bitcast.12, f32[]{:T(128)} %bitcast.11, f32[8]{0:T(128)S(1)} %neg.16, f32[]{:T(128)} %bitcast.10, f32[]{:T(128)} %bitcast.9, f32[]{:T(128)} %bitcast.8, ...), kind=kLoop, calls=%fused_computation.16 | loop fusion | flops 30015488 | bytes 13631608 | tf_op jit(solution)/shard_map/reduce_sum | solution.py:52
  134.0 11.6 %collective-permute-done.3 = f32[4,8,4096]{2,0,1:T(4,128)S(1)} collective-permute-done((f32[4,8,4096]{2,0,1:T(4,128)S(1)}, f32[4,8,4096]{2,0,1:T(4,128)S(1)}, u32[]{:S(2)}, u32[]{:S(2)}) %collective-permute-start.3) | collective-permute-done | bytes 524320 | tf_op jit(solution)/shard_map/ppermute | solution.py:31
  146.3 3.0 %collective-permute-start.4 = (f32[4,4,4096]{2,0,1:T(4,128)S(1)}, f32[4,4,4096]{2,0,1:T(4,128)S(1)}, u32[]{:S(2)}, u32[]{:S(2)}) collective-permute-start(f32[4,4,4096]{2,0,1:T(4,128)S(1)} %select_bitcast_fusion.1), channel_id=1, source_target_pairs={{0,32},{32,0},{8,40},{40,8},{16,48},{48,16},{24,56},{56,24},{64,96... | collective-permute-start | bytes 786440 | tf_op jit(solution)/shard_map/ppermute | solution.py:31
  149.5 5.0 %collective-permute-done.4 = f32[4,4,4096]{2,0,1:T(4,128)S(1)} collective-permute-done((f32[4,4,4096]{2,0,1:T(4,128)S(1)}, f32[4,4,4096]{2,0,1:T(4,128)S(1)}, u32[]{:S(2)}, u32[]{:S(2)}) %collective-permute-start.4) | collective-permute-done | bytes 262176 | tf_op jit(solution)/shard_map/ppermute | solution.py:31
  155.8 3.0 %collective-permute-done.5 = f32[4,2,4096]{2,0,1:T(4,128)S(1)} collective-permute-done((f32[4,2,4096]{2,0,1:T(4,128)S(1)}, f32[4,2,4096]{2,0,1:T(4,128)S(1)}, u32[]{:S(2)}, u32[]{:S(2)}) %collective-permute-start.5) | collective-permute-done | bytes 131104 | tf_op jit(solution)/shard_map/ppermute | solution.py:31
  160.3 3.5 %collective-permute-done.6 = f32[4,1,4096]{2,0,1:T(4,128)S(1)} collective-permute-done((f32[4,1,4096]{2,0,1:T(4,128)S(1)}, f32[4,1,4096]{2,0,1:T(4,128)S(1)}, u32[]{:S(2)}, u32[]{:S(2)}) %collective-permute-start.6) | collective-permute-done | bytes 65568 | tf_op jit(solution)/shard_map/ppermute | solution.py:31
  164.6 68.7 %all-gather.3.cloned.1.call-done = f32[4,1,131072]{2,0,1:T(4,128)} async-done(((f32[4,1,4096]{2,0,1:T(4,128)}), f32[4,1,131072]{2,0,1:T(4,128)}) %all-gather.3.cloned.1.call-update) | async-done | bytes 2097168 | tf_op jit(solution)/shard_map/all_gather | solution.py:83
  233.2 3.0 %copy.121 = f32[1,4,1024,128]{3,2,1,0:T(8,128)} copy(f32[1,4,1024,128]{3,1,2,0:T(4,128)} %bitcast.162) | data formatting | bytes 4194304
  (95 shorter events, 42.3 us)
Async XLA Ops:
  6.5 226.7 %all-gather.3.cloned.1.call-start = ((), (), s32[]{:S(2)}) async-start(), calls=%async_computation | async-start | bytes 2162688 | tf_op jit(solution)/shard_map/all_gather | solution.py:83
  14.4 11.3 %copy-start.4 = (f32[8]{0:T(128)S(1)}, f32[8]{0:T(128)}, u32[]{:S(2)}) copy-start(f32[8]{0:T(128)} %param.12) | copy-start | bytes 100
  14.4 11.3 %copy-start.3 = (f32[8]{0:T(128)S(1)}, f32[8]{0:T(128)}, u32[]{:S(2)}) copy-start(f32[8]{0:T(128)} %param.13) | copy-start | bytes 100
  14.4 11.3 %copy-start.1 = (f32[3]{0:T(128)S(1)}, f32[3]{0:T(128)}, u32[]{:S(2)}) copy-start(f32[3]{0:T(128)} %param.16) | copy-start | bytes 40
  14.4 12.0 %copy-start.2 = (f32[3]{0:T(128)S(1)}, f32[3]{0:T(128)}, u32[]{:S(2)}) copy-start(f32[3]{0:T(128)} %param.15) | copy-start | bytes 40
  14.4 12.6 %copy-start.5 = (s32[8]{0:T(128)S(1)}, s32[8]{0:T(128)}, u32[]{:S(2)}) copy-start(s32[8]{0:T(128)} %param.10) | copy-start | bytes 100
  14.4 12.6 %copy-start.6 = (s32[8]{0:T(128)S(1)}, s32[8]{0:T(128)}, u32[]{:S(2)}) copy-start(s32[8]{0:T(128)} %param.11) | copy-start | bytes 100
  14.5 12.6 %copy-start.7 = (f32[8]{0:T(128)S(1)}, f32[8]{0:T(128)}, u32[]{:S(2)}) copy-start(f32[8]{0:T(128)} %param.14) | copy-start | bytes 100
  17.4 10.4 %collective-permute-start = (f32[8,1024,1]{1,0,2:T(8,128)S(1)}, f32[8,1024,1]{1,0,2:T(8,128)S(1)}, u32[]{:S(2)}, u32[]{:S(2)}) collective-permute-start(f32[8,1024,1]{1,0,2:T(8,128)S(1)} %copy.104), channel_id=1, source_target_pairs={{0,1},{1,2},{2,3},{3,4},{4,5},{5,6},{6,7},{8,9},{9,10},{10,11},{11... | collective-permute-start | bytes 98312 | tf_op jit(solution)/shard_map/ppermute | solution.py:15
  23.0 10.0 %collective-permute-start.1 = (f32[8,1024,1]{1,0,2:T(8,128)S(1)}, f32[8,1024,1]{1,0,2:T(8,128)S(1)}, u32[]{:S(2)}, u32[]{:S(2)}) collective-permute-start(f32[8,1024,1]{1,0,2:T(8,128)S(1)} %copy.105), channel_id=1, source_target_pairs={{1,0},{2,1},{3,2},{4,3},{5,4},{6,5},{7,6},{9,8},{10,9},{11,10},{12... | collective-permute-start | bytes 98312 | tf_op jit(solution)/shard_map/ppermute | solution.py:17
  103.5 4.7 %copy-start = (f32[8,1024,129]{2,1,0:T(8,128)S(1)}, f32[8,1024,129]{2,1,0:T(8,128)}, u32[]{:S(2)}) copy-start(f32[8,1024,129]{2,1,0:T(8,128)} %multiply_add_fusion) | copy-start | bytes 12681220
  126.8 4.4 %collective-permute-start.2 = (f32[4,16,4096]{2,1,0:T(8,128)S(1)}, f32[4,16,4096]{2,1,0:T(8,128)S(1)}, u32[]{:S(2)}, u32[]{:S(2)}) collective-permute-start(f32[4,16,4096]{2,1,0:T(8,128)S(1)} %bitcast.163), channel_id=1, source_target_pairs={{0,8},{8,0},{16,24},{24,16},{32,40},{40,32},{48,56},{56,48},{64,72... | collective-permute-start | bytes 3145736 | tf_op jit(solution)/shard_map/ppermute | solution.py:31
  132.4 13.2 %collective-permute-start.3 = (f32[4,8,4096]{2,0,1:T(4,128)S(1)}, f32[4,8,4096]{2,0,1:T(4,128)S(1)}, u32[]{:S(2)}, u32[]{:S(2)}) collective-permute-start(f32[4,8,4096]{2,0,1:T(4,128)S(1)} %select_bitcast_fusion), channel_id=1, source_target_pairs={{0,16},{16,0},{8,24},{24,8},{32,48},{48,32},{40,56},{56,40},{64,80... | collective-permute-start | bytes 1572872 | tf_op jit(solution)/shard_map/ppermute | solution.py:31
  146.3 8.2 %collective-permute-start.4 = (f32[4,4,4096]{2,0,1:T(4,128)S(1)}, f32[4,4,4096]{2,0,1:T(4,128)S(1)}, u32[]{:S(2)}, u32[]{:S(2)}) collective-permute-start(f32[4,4,4096]{2,0,1:T(4,128)S(1)} %select_bitcast_fusion.1), channel_id=1, source_target_pairs={{0,32},{32,0},{8,40},{40,8},{16,48},{48,16},{24,56},{56,24},{64,96... | collective-permute-start | bytes 786440 | tf_op jit(solution)/shard_map/ppermute | solution.py:31
  154.9 3.9 %collective-permute-start.5 = (f32[4,2,4096]{2,0,1:T(4,128)S(1)}, f32[4,2,4096]{2,0,1:T(4,128)S(1)}, u32[]{:S(2)}, u32[]{:S(2)}) collective-permute-start(f32[4,2,4096]{2,0,1:T(4,128)S(1)} %select_bitcast_fusion.2), channel_id=1, source_target_pairs={{0,64},{64,0},{8,72},{72,8},{16,80},{80,16},{24,88},{88,24},{32,96... | collective-permute-start | bytes 393224 | tf_op jit(solution)/shard_map/ppermute | solution.py:31
  159.0 4.8 %collective-permute-start.6 = (f32[4,1,4096]{2,0,1:T(4,128)S(1)}, f32[4,1,4096]{2,0,1:T(4,128)S(1)}, u32[]{:S(2)}, u32[]{:S(2)}) collective-permute-start(f32[4,1,4096]{2,0,1:T(4,128)S(1)} %get-tuple-element.32), channel_id=1, source_target_pairs={{0,128},{128,0},{8,136},{136,8},{16,144},{144,16},{24,152},{152,24... | collective-permute-start | bytes 196616 | tf_op jit(solution)/shard_map/ppermute | solution.py:31
Sparse Core Ops, SparseCore 0:
  164.7 68.5 all-gather.2
where the time goes:
time: 245 us; the launch traced here: 243 us
  waiting for transfers between devices  95 us (39%)
  local copies, waits for them, and re-layouts  73.7 us (30%)
  other arithmetic  45.8 us (19%)
  between operations  14.5 us (6%)
  starting transfers between devices  14.1 us (6%)
    all_gather x1, waiting for transfers between devices, body(): band = lax.all_gather(final_tile, 'gx', axis=1, tiled=True)  68.7 us
    gather x24, local copies, waits for them, and re-layouts  40.3 us
    ppermute x5, waiting for transfers between devices, from_partner(): return lax.ppermute(block, axis, route)  23.7 us
    unnamed x30, local copies, waits for them, and re-layouts  12 us
    add x1, other arithmetic, sample_slice(): blended = window[:-1] * (1.0 - row_frac) + window[1:] * row_frac  10.1 us
    reduce_sum x1, other arithmetic, render(): channels.append(jnp.sum(weight * colour, axis=0))  9.27 us
    concatenate x1, other arithmetic, with_halo(): jnp.concatenate([lax.ppermute(tail, axis, [(i, (i + 1) % count) for i in...  8.83 us
    ppermute x5, starting transfers between devices, from_partner(): return lax.ppermute(block, axis, route)  8.62 us
  transfers between devices with their start and end apart: 8, of which 7 were waited for; matrix products, arithmetic and copies ran while one was open for 4% of the time, Pallas kernels for 0%

commit v1 on v0

v1 whole, which is shorter than its diff:
```python
import functools
import math

import jax
import jax.numpy as jnp
from jax import lax
from jax.experimental import pallas as pl
from jax.experimental.pallas import tpu as pltpu
from jax.sharding import PartitionSpec as P

F32 = jnp.float32
SLICES, ROWS, COLS = 8, 1024, 128
HALF, QUARTER, TILE = 512, 128, 32
STEP = 32
LOG2E = math.log2(math.e)
VMEM = pl.BlockSpec(memory_space=pltpu.VMEM)
SMEM = pl.BlockSpec(memory_space=pltpu.SMEM)
ANY = pl.BlockSpec(memory_space=pl.ANY)
BIG = 48 << 20


def call(kernel, outs, ins, args, scratch=(), cost=1 << 20):
    return pl.pallas_call(
        kernel,
        out_shape=outs,
        in_specs=ins,
        out_specs=jax.tree.map(lambda _: VMEM, outs),
        scratch_shapes=scratch,
        compiler_params=pltpu.CompilerParams(vmem_limit_bytes=BIG),
        cost_estimate=pl.CostEstimate(flops=cost, bytes_accessed=cost, transcendentals=0),
    )(*args)


def image(*shape):
    return jax.ShapeDtypeStruct(shape, F32)


def over(front, back):
    clear = 1.0 - front[3]
    return [front[c] + clear * back[c] for c in range(4)]


def edges_kernel(cells, first, last):
    for k in range(SLICES):
        for r in range(0, 256, 128):
            turned = jnp.transpose(cells[k, r : r + 128, :])
            first[k : k + 1, r : r + 128] = turned[0:1]
            last[k : k + 1, r : r + 128] = turned[127:128]


def edges(tsdf):
    columns = pl.BlockSpec((SLICES, 256), lambda i: (0, i))
    return pl.pallas_call(
        edges_kernel,
        grid=(ROWS // 256,),
        out_shape=[image(SLICES, ROWS)] * 2,
        in_specs=[pl.BlockSpec((SLICES, 256, COLS), lambda i: (0, i, 0))],
        out_specs=[columns, columns],
        compiler_params=pltpu.CompilerParams(vmem_limit_bytes=BIG),
    )(tsdf)


def render_kernel(
    partner, tsdf, left, right, shift_x, shift_y, frac_x, frac_y, extinction, slope, offset, out, cells, side, sems
):
    core = lax.axis_index("gx") & 1
    half = core ^ 1 if partner else core
    base = pl.multiple_of(half * HALF, HALF)
    copies = []
    for c in range(4):
        copies.append(
            pltpu.make_async_copy(
                tsdf.at[:, pl.ds(pl.multiple_of(base + c * 128, 128), 128), :],
                cells.at[:, pl.ds(8 + c * 128, 128), :],
                sems.at[c],
            )
        )
    above = pltpu.make_async_copy(tsdf.at[:, pl.ds(HALF - 8, 8), :], cells.at[:, pl.ds(0, 8), :], sems.at[4])
    below = pltpu.make_async_copy(tsdf.at[:, pl.ds(HALF, 8), :], cells.at[:, pl.ds(HALF + 8, 8), :], sems.at[4])

    @pl.when(half == 1)
    def _():
        above.start()
        cells[:, HALF + 8 :, :] = jnp.zeros((SLICES, 8, COLS), F32)

    @pl.when(half == 0)
    def _():
        below.start()
        cells[:, 0:8, :] = jnp.zeros((SLICES, 8, COLS), F32)

    for copy in copies:
        copy.start()

    row = lax.broadcasted_iota(jnp.int32, (SLICES, ROWS), 1)
    which = lax.broadcasted_iota(jnp.int32, (SLICES, 1), 0)

    def per_slice(ref):
        vec = jnp.zeros((SLICES, 1), F32)
        for k in range(SLICES):
            vec = jnp.where(which == k, ref[k].astype(F32), vec)
        return vec

    sx = per_slice(shift_x)
    sy = per_slice(shift_y)
    fx = per_slice(frac_x)
    mid = jnp.where(sy < -0.5, left[...], right[...])
    prev = jnp.where(row == 0, 0.0, pltpu.roll(mid, 1, 1))
    after = jnp.where(row == ROWS - 1, 0.0, pltpu.roll(mid, ROWS - 1, 1))
    up = sx < -0.5
    blended = jnp.where(up, prev, mid) * (1.0 - fx) + jnp.where(up, mid, after) * fx

    @pl.when(half == 0)
    def _():
        for r in range(0, HALF, 128):
            side[r : r + 128, 0:SLICES] = jnp.transpose(blended[:, r : r + 128])

    @pl.when(half == 1)
    def _():
        for r in range(0, HALF, 128):
            side[r : r + 128, 0:SLICES] = jnp.transpose(blended[:, HALF + r : HALF + r + 128])

    lane = lax.broadcasted_iota(jnp.int32, (STEP, COLS), 1)
    scale = [0.5 * slope[c] for c in range(3)]
    bias = [0.5 * offset[c] for c in range(3)]

    def step(i, carry):
        r = pl.multiple_of(i * STEP, STEP)
        beyond = side[pl.ds(r, STEP), :]
        transmit = jnp.ones((STEP, COLS), F32)
        total = [jnp.zeros((STEP, COLS), F32) for _ in range(3)]
        for k in range(SLICES):
            at = r + 8 + shift_x[k]
            upper = cells[k, pl.ds(at, STEP), :]
            lower = cells[k, pl.ds(at + 1, STEP), :]
            down = frac_x[k]
            mixed = upper * (1.0 - down) + lower * down
            back = shift_y[k] == -1
            turn = jnp.where(back, 1, COLS - 1)
            edge = jnp.where(back, 0, COLS - 1)
            moved = pltpu.roll(mixed, turn, 1)
            moved = jnp.where(lane == edge, beyond[:, k : k + 1], moved)
            far = jnp.where(back, 1.0 - frac_y[k], frac_y[k])
            value = mixed * (1.0 - far) + moved * far
            density = jnp.exp2(value * value * (-LOG2E))
            after = transmit * jnp.exp2(density * (extinction[k] * (-LOG2E)))
            weight = transmit - after
            transmit = after
            for c in range(3):
                total[c] = total[c] + weight * jnp.tanh(value * scale[c] + bias[c])
        alpha = 1.0 - transmit
        for c in range(3):
            out[c, pl.ds(r, STEP), :] = 0.5 * (alpha + total[c])
        out[3, pl.ds(r, STEP), :] = alpha
        return carry

    @pl.when(half == 1)
    def _():
        above.wait()

    @pl.when(half == 0)
    def _():
        below.wait()

    copies[0].wait()
    per = 128 // STEP
    for c in range(4):
        if c < 3:
            copies[c + 1].wait()
        lax.fori_loop(c * per, (c + 1) * per, step, 0)


def render(partner, tsdf, left, right, scalars):
    return call(
        functools.partial(render_kernel, partner),
        image(4, HALF, COLS),
        [ANY, VMEM, VMEM] + [SMEM] * 7,
        (tsdf, left, right, *scalars),
        [
            pltpu.VMEM((SLICES, HALF + 16, COLS), F32),
            pltpu.VMEM((HALF, COLS), F32),
            pltpu.SemaphoreType.DMA((5,)),
        ],
        cost=8 << 20,
    )


def pair_kernel(mask, own, other, here, plus, minus, far):
    index = lax.axis_index("gx")
    y = index >> 1 & 3
    front = (index ^ mask[0]) & 1 == 0
    for away, dest in ((0, here), (1, plus), (3, minus), (2, far)):
        begin = pl.multiple_of(((y + away) & 3) * QUARTER, QUARTER)

        def run(first, second):
            @pl.loop(0, QUARTER, step=TILE)
            def _(r):
                r = pl.multiple_of(r, TILE)
                rows = pl.ds(pl.multiple_of(begin + r, TILE), TILE)
                done = over([first[c, rows, :] for c in range(4)], [second[c, rows, :] for c in range(4)])
                for c in range(4):
                    dest[c, pl.ds(r, TILE), :] = done[c]

        pl.when(front)(functools.partial(run, own, other))
        pl.when(jnp.logical_not(front))(functools.partial(run, other, own))


def pair(mask, own, other):
    return call(
        pair_kernel, [image(4, QUARTER, COLS)] * 4, [SMEM, VMEM, VMEM], (mask, own, other), cost=1 << 20
    )


def in_order(parts, ranks, rows):
    loaded = [[part[c, rows, :] for c in range(4)] for part in parts]
    image_so_far = None
    for place in range(4):
        chosen = loaded[0]
        for part in range(1, 4):
            here = ranks[part] == place
            chosen = [jnp.where(here, loaded[part][c], chosen[c]) for c in range(4)]
        image_so_far = chosen if image_so_far is None else over(image_so_far, chosen)
    return image_so_far


def quarter_kernel(mask, own, plus, minus, far, here, one, two, three):
    index = lax.axis_index("gx")
    y = index >> 1 & 3
    z = index >> 3
    key = mask[0] >> 1 & 3
    ranks = [((y + away) & 3) ^ key for away in (0, 3, 1, 2)]
    for flip, dest in enumerate((here, one, two, three)):
        rows = pl.ds(pl.multiple_of((z ^ flip) * TILE, TILE), TILE)
        done = in_order((own, plus, minus, far), ranks, rows)
        for c in range(4):
            dest[c, :, :] = done[c]


def quarter(mask, parts):
    return call(quarter_kernel, [image(4, TILE, COLS)] * 4, [SMEM] + [VMEM] * 4, (mask, *parts), cost=1 << 19)


def tile_kernel(mask, own, one, two, three, out):
    z = lax.axis_index("gx") >> 3
    key = mask[0] >> 3 & 3
    ranks = [(z ^ flip) ^ key for flip in range(4)]
    done = in_order((own, one, two, three), ranks, pl.ds(0, TILE))
    for c in range(4):
        out[c, :, :] = done[c]


def tile(mask, parts):
    return call(tile_kernel, image(4, TILE, COLS), [SMEM] + [VMEM] * 4, (mask, *parts), cost=1 << 18)


def join_kernel(own, one, two, three, out):
    z = lax.axis_index("gx") >> 3
    for flip, part in enumerate((own, one, two, three)):
        out[:, pl.ds(pl.multiple_of((z ^ flip) * TILE, TILE), TILE), :] = part[...]


def join(parts):
    return call(join_kernel, image(4, QUARTER, COLS), [VMEM] * 4, parts, cost=1 << 19)


def frame_kernel(*refs):
    parts, out, sems = refs[:8], refs[8], refs[9]
    index = lax.axis_index("gx")
    copies = []
    for n, part in enumerate(parts):
        half = index & 1 ^ (n >> 2)
        y = (index >> 1) + (0, 3, 1, 2)[n & 3] & 3
        rows = pl.ds(pl.multiple_of(half * HALF + y * QUARTER, QUARTER), QUARTER)
        copies.append(pltpu.make_async_copy(part, out.at[:, rows, :], sems.at[n]))
    for copy in copies:
        copy.start()
    for copy in copies:
        copy.wait()


def frame(parts):
    return pl.pallas_call(
        frame_kernel,
        out_shape=image(4, ROWS, COLS),
        in_specs=[ANY] * 8,
        out_specs=ANY,
        scratch_shapes=[pltpu.SemaphoreType.DMA((8,))],
    )(*parts)


def send(block, target):
    return lax.ppermute(block, "gx", [(i, target(i)) for i in range(32)])


def flip(bits):
    return lambda i: i ^ bits


def along_y(step):
    return lambda i: i & ~6 | ((i >> 1) + step & 3) << 1


def to_quarters(plus, minus, far):
    return send(plus, along_y(1)), send(minus, along_y(3)), send(far, along_y(2))


def body(tsdf, shift_x, shift_y, frac_x, frac_y, extinction, color_slope, color_offset, view_mask):
    scalars = (shift_x, shift_y, frac_x, frac_y, extinction, color_slope, color_offset)
    first, last = edges(tsdf)
    left = lax.ppermute(last, "gy", [(i, i + 1) for i in range(7)])
    right = lax.ppermute(first, "gy", [(i + 1, i) for i in range(7)])
    given = render(True, tsdf, left, right, scalars)
    other = send(given, flip(1))
    own = render(False, tsdf, left, right, scalars)
    here, plus, minus, far = pair(view_mask, own, other)
    here, one, two, three = quarter(view_mask, (here, *to_quarters(plus, minus, far)))
    mine = tile(view_mask, (here, send(one, flip(8)), send(two, flip(16)), send(three, flip(24))))
    block = join((mine, send(mine, flip(8)), send(mine, flip(16)), send(mine, flip(24))))
    blocks = (block, *to_quarters(block, block, block))
    return frame(blocks + tuple(send(b, flip(1)) for b in blocks))


def solution(mesh):
    in_specs = (P("gx", None, "gy"), P("gx"), P("gx"), P("gx"), P("gx"), P("gx"), P(), P(), P())
    out_specs = P(None, None, "gy")
    return jax.shard_map(body, mesh=mesh, in_specs=in_specs, out_specs=out_specs, check_vma=False)
```

time: 245 us -> 149 us (0.61)
  the two profiles are of different devices: /device:TPU:5 before, /device:TPU:7 now
where the time goes in v1:
time: 149 us
  Pallas kernels  75.7 us (51%)
  starting transfers between devices  40.6 us (27%)
  waiting for transfers between devices  28.9 us (19%)
  local copies, waits for them, and re-layouts  2.93 us (2%)
    pallas_call x1, Pallas kernels, frame(): pl.pallas_call(frame_kernel, out_shape=image(4, ROWS, COLS), in_specs=[AN...  64.7 us
    ppermute x17, starting transfers between devices, send(): return lax.ppermute(block, 'gx', [(i, target(i)) for i in range(32)])  30 us
    ppermute x17, waiting for transfers between devices, send(): return lax.ppermute(block, 'gx', [(i, target(i)) for i in range(32)])  20.1 us
    pallas_call x6, Pallas kernels, call(): pl.pallas_call(kernel, out_shape=outs, in_specs=ins, out_specs=jax.tree.m...  9.35 us
    ppermute x1, waiting for transfers between devices, body(): right = lax.ppermute(first, 'gy', [(i + 1, i) for i in range(7)])  8.74 us
    ppermute x1, starting transfers between devices, body(): left = lax.ppermute(last, 'gy', [(i, i + 1) for i in range(7)])  8.73 us
  transfers between devices with their start and end apart: 19, of which 9 were waited for; matrix products, arithmetic and copies ran while one was open for 0% of the time, Pallas kernels for 3%

profile of v1, /device:TPU:7, one launch (start us, length us, event | category | flops | bytes accessed | tf_op | source)
XLA Modules:
  0.0 149.0 jit_solution(7503332268302365254)
XLA Ops:
  0.0 2.2 %copy-done = f32[8,1024,128]{2,1,0:T(8,128)S(1)} copy-done((f32[8,1024,128]{2,1,0:T(8,128)S(1)}, f32[8,1024,128]{2,1,0:T(8,128)}, u32[]{:S(2)}) %copy-start) | copy-done | bytes 4194328
  2.2 1.7 %shard_map.91 = (f32[8,1024]{1,0:T(8,128)S(1)}, f32[8,1024]{1,0:T(8,128)S(1)}) custom-call(f32[8,1024,128]{2,1,0:T(8,128)S(1)} %copy-done), custom_call_target="tpu_custom_call" | custom-call | tf_op jit(solution)/shard_map/pallas_call | solution.py:53
  3.9 8.7 %collective-permute-start = (f32[8,1024]{1,0:T(8,128)S(1)}, f32[8,1024]{1,0:T(8,128)S(1)}, u32[]{:S(2)}, u32[]{:S(2)}) collective-permute-start(f32[8,1024]{1,0:T(8,128)S(1)} %get-tuple-element.15), channel_id=1, source_target_pairs={{0,1},{1,2},{2,3},{3,4},{4,5},{5,6},{6,7},{8,9},{9,10},{10,11},{11... | collective-permute-start | bytes 98312 | tf_op jit(solution)/shard_map/ppermute | solution.py:309
  12.6 1.9 %collective-permute-start.1 = (f32[8,1024]{1,0:T(8,128)S(1)}, f32[8,1024]{1,0:T(8,128)S(1)}, u32[]{:S(2)}, u32[]{:S(2)}) collective-permute-start(f32[8,1024]{1,0:T(8,128)S(1)} %get-tuple-element.16), channel_id=1, source_target_pairs={{1,0},{2,1},{3,2},{4,3},{5,4},{6,5},{7,6},{9,8},{10,9},{11,10},{12... | collective-permute-start | bytes 98312 | tf_op jit(solution)/shard_map/ppermute | solution.py:310
  14.6 8.7 %collective-permute-done.1.right = f32[8,1024]{1,0:T(8,128)S(1)} collective-permute-done((f32[8,1024]{1,0:T(8,128)S(1)}, f32[8,1024]{1,0:T(8,128)S(1)}, u32[]{:S(2)}, u32[]{:S(2)}) %collective-permute-start.1) | collective-permute-done | bytes 32800 | tf_op jit(solution)/shard_map/ppermute | solution.py:310
  23.4 4.4 %shard_map.93 = f32[4,512,128]{2,1,0:T(8,128)S(1)} custom-call(f32[8,1024,128]{2,1,0:T(8,128)S(1)} %copy-done, f32[8,1024]{1,0:T(8,128)S(1)} %collective-permute-done.left, f32[8,1024]{1,0:T(8,128)S(1)} %collective-permute-done.1.right, s32[8]{0:T(128)S(1)} %copy-done.2, s32[8]{0:T(128)S(1)} %copy-done.3, f32[8]{0:T(128)S(1)} %copy-done.4, f32[8]{0:T(128)S(1)} %copy-done.5, ...), custom_call_target="tpu_custom_call" | custom-call | flops 8388608 | bytes 8388608 | tf_op jit(solution)/shard_map/pallas_call | solution.py:23
  27.8 2.2 %collective-permute-start.2 = (f32[4,512,128]{2,1,0:T(8,128)S(1)}, f32[4,512,128]{2,1,0:T(8,128)S(1)}, u32[]{:S(2)}, u32[]{:S(2)}) collective-permute-start(f32[4,512,128]{2,1,0:T(8,128)S(1)} %shard_map.93), channel_id=1, source_target_pairs={{0,8},{8,0},{16,24},{24,16},{32,40},{40,32},{48,56},{56,48},{64,72... | collective-permute-start | bytes 3145736 | tf_op jit(solution)/shard_map/ppermute | solution.py:291
  30.7 4.4 %shard_map.92.own = f32[4,512,128]{2,1,0:T(8,128)S(1)} custom-call(f32[8,1024,128]{2,1,0:T(8,128)S(1)} %copy-done, f32[8,1024]{1,0:T(8,128)S(1)} %collective-permute-done.left, f32[8,1024]{1,0:T(8,128)S(1)} %collective-permute-done.1.right, s32[8]{0:T(128)S(1)} %copy-done.2, s32[8]{0:T(128)S(1)} %copy-done.3, f32[8]{0:T(128)S(1)} %copy-done.4, ...), custom_call_target="tpu_custom_call" | custom-call | flops 8388608 | bytes 8388608 | tf_op jit(solution)/shard_map/pallas_call | solution.py:23
  36.8 1.5 %collective-permute-start.4 = (f32[4,128,128]{2,1,0:T(8,128)S(1)}, f32[4,128,128]{2,1,0:T(8,128)S(1)}, u32[]{:S(2)}, u32[]{:S(2)}) collective-permute-start(f32[4,128,128]{2,1,0:T(8,128)S(1)} %get-tuple-element.19), channel_id=1, source_target_pairs={{0,48},{8,56},{16,0},{24,8},{32,16},{40,24},{48,32},{56,40},{64,11... | collective-permute-start | bytes 786440 | tf_op jit(solution)/shard_map/ppermute | solution.py:291
  38.3 1.6 %collective-permute-start.5 = (f32[4,128,128]{2,1,0:T(8,128)S(1)}, f32[4,128,128]{2,1,0:T(8,128)S(1)}, u32[]{:S(2)}, u32[]{:S(2)}) collective-permute-start(f32[4,128,128]{2,1,0:T(8,128)S(1)} %get-tuple-element.20), channel_id=1, source_target_pairs={{0,32},{8,40},{16,48},{24,56},{32,0},{40,8},{48,16},{56,24},{64,96... | collective-permute-start | bytes 786440 | tf_op jit(solution)/shard_map/ppermute | solution.py:291
  39.8 4.9 %collective-permute-done.3.plus = f32[4,128,128]{2,1,0:T(8,128)S(1)} collective-permute-done((f32[4,128,128]{2,1,0:T(8,128)S(1)}, f32[4,128,128]{2,1,0:T(8,128)S(1)}, u32[]{:S(2)}, u32[]{:S(2)}) %collective-permute-start.3) | collective-permute-done | bytes 262176 | tf_op jit(solution)/shard_map/ppermute | solution.py:291
  44.8 6.7 %collective-permute-done.5.far = f32[4,128,128]{2,1,0:T(8,128)S(1)} collective-permute-done((f32[4,128,128]{2,1,0:T(8,128)S(1)}, f32[4,128,128]{2,1,0:T(8,128)S(1)}, u32[]{:S(2)}, u32[]{:S(2)}) %collective-permute-start.5) | collective-permute-done | bytes 262176 | tf_op jit(solution)/shard_map/ppermute | solution.py:291
  53.7 1.6 %collective-permute-start.8 = (f32[4,32,128]{2,1,0:T(8,128)S(1)}, f32[4,32,128]{2,1,0:T(8,128)S(1)}, u32[]{:S(2)}, u32[]{:S(2)}) collective-permute-start(f32[4,32,128]{2,1,0:T(8,128)S(1)} %get-tuple-element.24), channel_id=1, source_target_pairs={{0,192},{8,200},{16,208},{24,216},{32,224},{40,232},{48,240},{56,2... | collective-permute-start | bytes 196616 | tf_op jit(solution)/shard_map/ppermute | solution.py:291
  55.3 1.5 collective-permute-done.7.two
  56.7 2.4 %collective-permute-done.8.three = f32[4,32,128]{2,1,0:T(8,128)S(1)} collective-permute-done((f32[4,32,128]{2,1,0:T(8,128)S(1)}, f32[4,32,128]{2,1,0:T(8,128)S(1)}, u32[]{:S(2)}, u32[]{:S(2)}) %collective-permute-start.8) | collective-permute-done | bytes 65568 | tf_op jit(solution)/shard_map/ppermute | solution.py:291
  59.2 1.7 %collective-permute-start.11 = (f32[4,32,128]{2,1,0:T(8,128)S(1)}, f32[4,32,128]{2,1,0:T(8,128)S(1)}, u32[]{:S(2)}, u32[]{:S(2)}) collective-permute-start(f32[4,32,128]{2,1,0:T(8,128)S(1)} %shard_map.96.own), channel_id=1, source_target_pairs={{0,192},{8,200},{16,208},{24,216},{32,224},{40,232},{48,240},{56,2... | collective-permute-start | bytes 196616 | tf_op jit(solution)/shard_map/ppermute | solution.py:291
  61.2 1.6 %collective-permute-start.9 = (f32[4,32,128]{2,1,0:T(8,128)S(1)}, f32[4,32,128]{2,1,0:T(8,128)S(1)}, u32[]{:S(2)}, u32[]{:S(2)}) collective-permute-start(f32[4,32,128]{2,1,0:T(8,128)S(1)} %shard_map.96.own), channel_id=1, source_target_pairs={{0,64},{8,72},{16,80},{24,88},{32,96},{40,104},{48,112},{56,120},{... | collective-permute-start | bytes 196616 | tf_op jit(solution)/shard_map/ppermute | solution.py:291
  62.9 1.4 collective-permute-done.11.three
  64.3 1.9 %collective-permute-done.10.two = f32[4,32,128]{2,1,0:T(8,128)S(1)} collective-permute-done((f32[4,32,128]{2,1,0:T(8,128)S(1)}, f32[4,32,128]{2,1,0:T(8,128)S(1)}, u32[]{:S(2)}, u32[]{:S(2)}) %collective-permute-start.10) | collective-permute-done | bytes 65568 | tf_op jit(solution)/shard_map/ppermute | solution.py:291
  67.1 2.6 %collective-permute-start.13 = (f32[4,128,128]{2,1,0:T(8,128)S(1)}, f32[4,128,128]{2,1,0:T(8,128)S(1)}, u32[]{:S(2)}, u32[]{:S(2)}) collective-permute-start(f32[4,128,128]{2,1,0:T(8,128)S(1)} %shard_map.97.refs_0_), channel_id=1, source_target_pairs={{0,48},{8,56},{16,0},{24,8},{32,16},{40,24},{48,32},{56,40},{64,11... | collective-permute-start | bytes 786440 | tf_op jit(solution)/shard_map/ppermute | solution.py:291
  69.7 3.1 %collective-permute-start.15 = (f32[4,128,128]{2,1,0:T(8,128)S(1)}, f32[4,128,128]{2,1,0:T(8,128)S(1)}, u32[]{:S(2)}, u32[]{:S(2)}) collective-permute-start(f32[4,128,128]{2,1,0:T(8,128)S(1)} %shard_map.97.refs_0_), channel_id=1, source_target_pairs={{0,8},{8,0},{16,24},{24,16},{32,40},{40,32},{48,56},{56,48},{64,72... | collective-permute-start | bytes 786440 | tf_op jit(solution)/shard_map/ppermute | solution.py:291
  73.0 6.4 %collective-permute-start.18 = (f32[4,128,128]{2,1,0:T(8,128)S(1)}, f32[4,128,128]{2,1,0:T(8,128)S(1)}, u32[]{:S(2)}, u32[]{:S(2)}) collective-permute-start(f32[4,128,128]{2,1,0:T(8,128)S(1)} %collective-permute-done.14.refs_3_), channel_id=1, source_target_pairs={{0,8},{8,0},{16,24},{24,16},{32,40},{40,32},{48,56},{56,48},{64,72... | collective-permute-start | bytes 786440 | tf_op jit(solution)/shard_map/ppermute | solution.py:291
  80.3 2.2 %collective-permute-start.16 = (f32[4,128,128]{2,1,0:T(8,128)S(1)}, f32[4,128,128]{2,1,0:T(8,128)S(1)}, u32[]{:S(2)}, u32[]{:S(2)}) collective-permute-start(f32[4,128,128]{2,1,0:T(8,128)S(1)} %collective-permute-done.12.refs_1_), channel_id=1, source_target_pairs={{0,8},{8,0},{16,24},{24,16},{32,40},{40,32},{48,56},{56,48},{64,72... | collective-permute-start | bytes 786440 | tf_op jit(solution)/shard_map/ppermute | solution.py:291
  84.3 64.7 %shard_map.98 = f32[4,1024,128]{2,1,0:T(8,128)} custom-call(f32[4,128,128]{2,1,0:T(8,128)} %copy-done.1, f32[4,128,128]{2,1,0:T(8,128)} %copy-done.11, f32[4,128,128]{2,1,0:T(8,128)} %copy-done.10, f32[4,128,128]{2,1,0:T(8,128)} %copy-done.9, f32[4,128,128]{2,1,0:T(8,128)} %copy-done.12, f32[4,128,128]{2,1,0:T(8,128)} %copy-done.15, ...), custom_call_target="tpu_custom_call" | custom-call | tf_op jit(solution)/shard_map/pallas_call | solution.py:281
  (54 shorter events, 8.0 us)
Async XLA Ops:
  2.2 21.1 %copy-start.4 = (f32[8]{0:T(128)S(1)}, f32[8]{0:T(128)}, u32[]{:S(2)}) copy-start(f32[8]{0:T(128)} %frac_x.3) | copy-start | bytes 100
  2.2 21.1 %copy-start.5 = (f32[8]{0:T(128)S(1)}, f32[8]{0:T(128)}, u32[]{:S(2)}) copy-start(f32[8]{0:T(128)} %frac_y.3) | copy-start | bytes 100
  2.2 21.1 %copy-start.6 = (f32[8]{0:T(128)S(1)}, f32[8]{0:T(128)}, u32[]{:S(2)}) copy-start(f32[8]{0:T(128)} %extinction.3) | copy-start | bytes 100
  2.2 21.1 %copy-start.7 = (f32[3]{0:T(128)S(1)}, f32[3]{0:T(128)}, u32[]{:S(2)}) copy-start(f32[3]{0:T(128)} %slope.3) | copy-start | bytes 40
  2.2 21.1 %copy-start.8 = (f32[3]{0:T(128)S(1)}, f32[3]{0:T(128)}, u32[]{:S(2)}) copy-start(f32[3]{0:T(128)} %offset.3) | copy-start | bytes 40
  3.9 10.7 %collective-permute-start = (f32[8,1024]{1,0:T(8,128)S(1)}, f32[8,1024]{1,0:T(8,128)S(1)}, u32[]{:S(2)}, u32[]{:S(2)}) collective-permute-start(f32[8,1024]{1,0:T(8,128)S(1)} %get-tuple-element.15), channel_id=1, source_target_pairs={{0,1},{1,2},{2,3},{3,4},{4,5},{5,6},{6,7},{8,9},{9,10},{10,11},{11... | collective-permute-start | bytes 98312 | tf_op jit(solution)/shard_map/ppermute | solution.py:309
  12.6 10.7 %collective-permute-start.1 = (f32[8,1024]{1,0:T(8,128)S(1)}, f32[8,1024]{1,0:T(8,128)S(1)}, u32[]{:S(2)}, u32[]{:S(2)}) collective-permute-start(f32[8,1024]{1,0:T(8,128)S(1)} %get-tuple-element.16), channel_id=1, source_target_pairs={{1,0},{2,1},{3,2},{4,3},{5,4},{6,5},{7,6},{9,8},{10,9},{11,10},{12... | collective-permute-start | bytes 98312 | tf_op jit(solution)/shard_map/ppermute | solution.py:310
  27.8 7.3 %collective-permute-start.2 = (f32[4,512,128]{2,1,0:T(8,128)S(1)}, f32[4,512,128]{2,1,0:T(8,128)S(1)}, u32[]{:S(2)}, u32[]{:S(2)}) collective-permute-start(f32[4,512,128]{2,1,0:T(8,128)S(1)} %shard_map.93), channel_id=1, source_target_pairs={{0,8},{8,0},{16,24},{24,16},{32,40},{40,32},{48,56},{56,48},{64,72... | collective-permute-start | bytes 3145736 | tf_op jit(solution)/shard_map/ppermute | solution.py:291
  35.4 9.4 %collective-permute-start.3 = (f32[4,128,128]{2,1,0:T(8,128)S(1)}, f32[4,128,128]{2,1,0:T(8,128)S(1)}, u32[]{:S(2)}, u32[]{:S(2)}) collective-permute-start(f32[4,128,128]{2,1,0:T(8,128)S(1)} %get-tuple-element.18), channel_id=1, source_target_pairs={{0,16},{8,24},{16,32},{24,40},{32,48},{40,56},{48,0},{56,8},{64,80... | collective-permute-start | bytes 786440 | tf_op jit(solution)/shard_map/ppermute | solution.py:291
  36.8 8.0 %collective-permute-start.4 = (f32[4,128,128]{2,1,0:T(8,128)S(1)}, f32[4,128,128]{2,1,0:T(8,128)S(1)}, u32[]{:S(2)}, u32[]{:S(2)}) collective-permute-start(f32[4,128,128]{2,1,0:T(8,128)S(1)} %get-tuple-element.19), channel_id=1, source_target_pairs={{0,48},{8,56},{16,0},{24,8},{32,16},{40,24},{48,32},{56,40},{64,11... | collective-permute-start | bytes 786440 | tf_op jit(solution)/shard_map/ppermute | solution.py:291
  38.3 13.2 %collective-permute-start.5 = (f32[4,128,128]{2,1,0:T(8,128)S(1)}, f32[4,128,128]{2,1,0:T(8,128)S(1)}, u32[]{:S(2)}, u32[]{:S(2)}) collective-permute-start(f32[4,128,128]{2,1,0:T(8,128)S(1)} %get-tuple-element.20), channel_id=1, source_target_pairs={{0,32},{8,40},{16,48},{24,56},{32,0},{40,8},{48,16},{56,24},{64,96... | collective-permute-start | bytes 786440 | tf_op jit(solution)/shard_map/ppermute | solution.py:291
  51.6 3.6 %collective-permute-start.6 = (f32[4,32,128]{2,1,0:T(8,128)S(1)}, f32[4,32,128]{2,1,0:T(8,128)S(1)}, u32[]{:S(2)}, u32[]{:S(2)}) collective-permute-start(f32[4,32,128]{2,1,0:T(8,128)S(1)} %get-tuple-element.22), channel_id=1, source_target_pairs={{0,64},{8,72},{16,80},{24,88},{32,96},{40,104},{48,112},{56,120},{... | collective-permute-start | bytes 196616 | tf_op jit(solution)/shard_map/ppermute | solution.py:291
  52.4 4.3 %collective-permute-start.7 = (f32[4,32,128]{2,1,0:T(8,128)S(1)}, f32[4,32,128]{2,1,0:T(8,128)S(1)}, u32[]{:S(2)}, u32[]{:S(2)}) collective-permute-start(f32[4,32,128]{2,1,0:T(8,128)S(1)} %get-tuple-element.23), channel_id=1, source_target_pairs={{0,128},{8,136},{16,144},{24,152},{32,160},{40,168},{48,176},{56,1... | collective-permute-start | bytes 196616 | tf_op jit(solution)/shard_map/ppermute | solution.py:291
  53.7 5.5 %collective-permute-start.8 = (f32[4,32,128]{2,1,0:T(8,128)S(1)}, f32[4,32,128]{2,1,0:T(8,128)S(1)}, u32[]{:S(2)}, u32[]{:S(2)}) collective-permute-start(f32[4,32,128]{2,1,0:T(8,128)S(1)} %get-tuple-element.24), channel_id=1, source_target_pairs={{0,192},{8,200},{16,208},{24,216},{32,224},{40,232},{48,240},{56,2... | collective-permute-start | bytes 196616 | tf_op jit(solution)/shard_map/ppermute | solution.py:291
  59.2 5.0 %collective-permute-start.11 = (f32[4,32,128]{2,1,0:T(8,128)S(1)}, f32[4,32,128]{2,1,0:T(8,128)S(1)}, u32[]{:S(2)}, u32[]{:S(2)}) collective-permute-start(f32[4,32,128]{2,1,0:T(8,128)S(1)} %shard_map.96.own), channel_id=1, source_target_pairs={{0,192},{8,200},{16,208},{24,216},{32,224},{40,232},{48,240},{56,2... | collective-permute-start | bytes 196616 | tf_op jit(solution)/shard_map/ppermute | solution.py:291
  61.0 5.2 %collective-permute-start.10 = (f32[4,32,128]{2,1,0:T(8,128)S(1)}, f32[4,32,128]{2,1,0:T(8,128)S(1)}, u32[]{:S(2)}, u32[]{:S(2)}) collective-permute-start(f32[4,32,128]{2,1,0:T(8,128)S(1)} %shard_map.96.own), channel_id=1, source_target_pairs={{0,128},{8,136},{16,144},{24,152},{32,160},{40,168},{48,176},{56,1... | collective-permute-start | bytes 196616 | tf_op jit(solution)/shard_map/ppermute | solution.py:291
  61.2 4.9 %collective-permute-start.9 = (f32[4,32,128]{2,1,0:T(8,128)S(1)}, f32[4,32,128]{2,1,0:T(8,128)S(1)}, u32[]{:S(2)}, u32[]{:S(2)}) collective-permute-start(f32[4,32,128]{2,1,0:T(8,128)S(1)} %shard_map.96.own), channel_id=1, source_target_pairs={{0,64},{8,72},{16,80},{24,88},{32,96},{40,104},{48,112},{56,120},{... | collective-permute-start | bytes 196616 | tf_op jit(solution)/shard_map/ppermute | solution.py:291
  66.2 6.8 %collective-permute-start.14 = (f32[4,128,128]{2,1,0:T(8,128)S(1)}, f32[4,128,128]{2,1,0:T(8,128)S(1)}, u32[]{:S(2)}, u32[]{:S(2)}) collective-permute-start(f32[4,128,128]{2,1,0:T(8,128)S(1)} %shard_map.97.refs_0_), channel_id=1, source_target_pairs={{0,32},{8,40},{16,48},{24,56},{32,0},{40,8},{48,16},{56,24},{64,96... | collective-permute-start | bytes 786440 | tf_op jit(solution)/shard_map/ppermute | solution.py:291
  67.1 12.4 %collective-permute-start.13 = (f32[4,128,128]{2,1,0:T(8,128)S(1)}, f32[4,128,128]{2,1,0:T(8,128)S(1)}, u32[]{:S(2)}, u32[]{:S(2)}) collective-permute-start(f32[4,128,128]{2,1,0:T(8,128)S(1)} %shard_map.97.refs_0_), channel_id=1, source_target_pairs={{0,48},{8,56},{16,0},{24,8},{32,16},{40,24},{48,32},{56,40},{64,11... | collective-permute-start | bytes 786440 | tf_op jit(solution)/shard_map/ppermute | solution.py:291
  69.7 10.6 %collective-permute-start.12 = (f32[4,128,128]{2,1,0:T(8,128)S(1)}, f32[4,128,128]{2,1,0:T(8,128)S(1)}, u32[]{:S(2)}, u32[]{:S(2)}) collective-permute-start(f32[4,128,128]{2,1,0:T(8,128)S(1)} %shard_map.97.refs_0_), channel_id=1, source_target_pairs={{0,16},{8,24},{16,32},{24,40},{32,48},{40,56},{48,0},{56,8},{64,80... | collective-permute-start | bytes 786440 | tf_op jit(solution)/shard_map/ppermute | solution.py:291
  69.7 12.7 %collective-permute-start.15 = (f32[4,128,128]{2,1,0:T(8,128)S(1)}, f32[4,128,128]{2,1,0:T(8,128)S(1)}, u32[]{:S(2)}, u32[]{:S(2)}) collective-permute-start(f32[4,128,128]{2,1,0:T(8,128)S(1)} %shard_map.97.refs_0_), channel_id=1, source_target_pairs={{0,8},{8,0},{16,24},{24,16},{32,40},{40,32},{48,56},{56,48},{64,72... | collective-permute-start | bytes 786440 | tf_op jit(solution)/shard_map/ppermute | solution.py:291
  73.0 9.4 %collective-permute-start.18 = (f32[4,128,128]{2,1,0:T(8,128)S(1)}, f32[4,128,128]{2,1,0:T(8,128)S(1)}, u32[]{:S(2)}, u32[]{:S(2)}) collective-permute-start(f32[4,128,128]{2,1,0:T(8,128)S(1)} %collective-permute-done.14.refs_3_), channel_id=1, source_target_pairs={{0,8},{8,0},{16,24},{24,16},{32,40},{40,32},{48,56},{56,48},{64,72... | collective-permute-start | bytes 786440 | tf_op jit(solution)/shard_map/ppermute | solution.py:291
  79.4 3.0 %collective-permute-start.17 = (f32[4,128,128]{2,1,0:T(8,128)S(1)}, f32[4,128,128]{2,1,0:T(8,128)S(1)}, u32[]{:S(2)}, u32[]{:S(2)}) collective-permute-start(f32[4,128,128]{2,1,0:T(8,128)S(1)} %collective-permute-done.13.refs_2_), channel_id=1, source_target_pairs={{0,8},{8,0},{16,24},{24,16},{32,40},{40,32},{48,56},{56,48},{64,72... | collective-permute-start | bytes 786440 | tf_op jit(solution)/shard_map/ppermute | solution.py:291
  80.3 3.3 %collective-permute-start.16 = (f32[4,128,128]{2,1,0:T(8,128)S(1)}, f32[4,128,128]{2,1,0:T(8,128)S(1)}, u32[]{:S(2)}, u32[]{:S(2)}) collective-permute-start(f32[4,128,128]{2,1,0:T(8,128)S(1)} %collective-permute-done.12.refs_1_), channel_id=1, source_target_pairs={{0,8},{8,0},{16,24},{24,16},{32,40},{40,32},{48,56},{56,48},{64,72... | collective-permute-start | bytes 786440 | tf_op jit(solution)/shard_map/ppermute | solution.py:291
  (11 other events, 84.1 us)

commit v2 on v1

v2 whole, which is shorter than its diff:
```python
import functools
import math

import jax
import jax.numpy as jnp
from jax import lax
from jax.experimental import pallas as pl
from jax.experimental.pallas import tpu as pltpu
from jax.sharding import PartitionSpec as P

F32 = jnp.float32
SLICES, ROWS, COLS = 8, 1024, 128
HALF, QUARTER, TILE = 512, 128, 32
STEP = 64
CHUNK = 128
AHEAD = 8
PAD = 8
LOG2E = math.log2(math.e)
VMEM = pl.BlockSpec(memory_space=pltpu.VMEM)
SMEM = pl.BlockSpec(memory_space=pltpu.SMEM)
ANY = pl.BlockSpec(memory_space=pl.ANY)
HBM = pl.BlockSpec(memory_space=pltpu.HBM)
BIG = 24 << 20


def call(kernel, outs, ins, args, scratch=(), cost=1 << 20, limit=24 << 20):
    return pl.pallas_call(
        kernel,
        out_shape=outs,
        in_specs=ins,
        out_specs=jax.tree.map(lambda _: VMEM, outs),
        scratch_shapes=scratch,
        compiler_params=pltpu.CompilerParams(vmem_limit_bytes=limit),
        cost_estimate=pl.CostEstimate(flops=cost << 8, bytes_accessed=cost, transcendentals=0),
    )(*args)


def image(*shape):
    return jax.ShapeDtypeStruct(shape, F32)


def over(front, back):
    clear = 1.0 - front[3]
    return [front[c] + clear * back[c] for c in range(4)]


def per_slice(ref):
    which = lax.broadcasted_iota(jnp.int32, (SLICES, 1), 0)
    vec = jnp.zeros((SLICES, 1), F32)
    for k in range(SLICES):
        vec = jnp.where(which == k, ref[k].astype(F32), vec)
    return vec


def edges_kernel(tsdf, cells, columns, to_odd, to_even, block, sems):
    copies = []
    for n in range(ROWS // CHUNK):
        copies.append(
            pltpu.make_async_copy(
                tsdf.at[:, pl.ds(n * CHUNK, CHUNK), :], cells.at[:, pl.ds(PAD + n * CHUNK, CHUNK), :], sems.at[n]
            )
        )
    for copy in copies[:AHEAD]:
        copy.start()
    for r in (0, PAD + ROWS):
        cells[:, r : r + PAD, :] = jnp.zeros((SLICES, PAD, COLS), F32)
    lane = lax.broadcasted_iota(jnp.int32, (128, COLS), 1)
    for n, copy in enumerate(copies):
        copy.wait()
        if n + AHEAD < len(copies):
            copies[n + AHEAD].start()
        for r in range(n * CHUNK, (n + 1) * CHUNK, 128):
            rows = pl.ds(PAD + r, 128)
            packed = pltpu.roll(cells[0, rows, :], 2, 1)
            for k in range(1, SLICES):
                turned = pltpu.roll(cells[k, rows, :], 4 * k + 2, 1)
                packed = jnp.where(lane >= 4 * k, turned, packed)
            block[r // 128] = jnp.transpose(packed)[: 4 * SLICES]
            for j in range(4):
                columns[j, :, r : r + 128] = block[r // 128, pl.ds(j, SLICES, stride=4), :]
    even = lax.axis_index("gy") & 1 == 0
    last, first = columns[1], columns[2]
    to_odd[...] = jnp.where(even, first, last)
    to_even[...] = jnp.where(even, last, first)


def edges(tsdf):
    return call(
        edges_kernel,
        [pltpu.VMEM((SLICES, ROWS + 2 * PAD, COLS), F32), image(4, SLICES, ROWS), image(SLICES, ROWS), image(SLICES, ROWS)],
        [HBM],
        (pltpu.with_memory_space_constraint(tsdf, pltpu.HBM),),
        [
            pltpu.VMEM((ROWS // 128, 4 * SLICES, 128), F32),
            pltpu.SemaphoreType.DMA((ROWS // CHUNK,)),
        ],
        cost=4 << 20,
    )


def border_kernel(
    columns, by_odd, by_even, shift_x, shift_y, frac_x, frac_y, extinction, slope, offset, mine, theirs, whole
):
    even = lax.axis_index("gy") & 1 == 0
    left = jnp.where(even, by_odd[...], by_even[...])
    right = jnp.where(even, by_even[...], by_odd[...])
    row = lax.broadcasted_iota(jnp.int32, (SLICES, ROWS), 1)
    depth = lax.broadcasted_iota(jnp.int32, (SLICES, ROWS), 0)
    up = per_slice(shift_x) < -0.5
    back = per_slice(shift_y) < -0.5
    fx, fy = per_slice(frac_x), per_slice(frac_y)
    optical = per_slice(extinction) * (-LOG2E)
    third, fourth, first, second = (columns[n] for n in range(4))
    pairs = (
        (jnp.where(back, left, first), jnp.where(back, first, second)),
        (jnp.where(back, third, fourth), jnp.where(back, fourth, right)),
    )
    for n, (one, two) in enumerate(pairs):
        mixed = one * (1.0 - fy) + two * fy
        prev = jnp.where(row == 0, 0.0, pltpu.roll(mixed, 1, 1))
        after = jnp.where(row == ROWS - 1, 0.0, pltpu.roll(mixed, ROWS - 1, 1))
        value = jnp.where(up, prev, mixed) * (1.0 - fx) + jnp.where(up, mixed, after) * fx
        passed = jnp.exp2(jnp.exp2(value * value * (-LOG2E)) * optical)
        for far in (1, 2, 4):
            passed = passed * jnp.where(depth >= far, pltpu.roll(passed, far, 0), 1.0)
        weight = jnp.where(depth >= 1, pltpu.roll(passed, 1, 0), 1.0) - passed
        alpha = 1.0 - passed[SLICES - 1 :]
        for c in range(3):
            colour = weight * jnp.tanh(value * (0.5 * slope[c]) + 0.5 * offset[c])
            whole[4 * n + c : 4 * n + c + 1, :] = 0.5 * (alpha + jnp.sum(colour, axis=0, keepdims=True))
        whole[4 * n + 3 : 4 * n + 4, :] = alpha
    core = lax.axis_index("gx") & 1
    mine[...] = whole[:, pl.ds(pl.multiple_of(core * HALF, HALF), HALF)]
    theirs[...] = whole[:, pl.ds(pl.multiple_of((core ^ 1) * HALF, HALF), HALF)]


def border(columns, by_odd, by_even, scalars):
    return call(
        border_kernel,
        [image(8, HALF)] * 2,
        [VMEM] * 3 + [SMEM] * 7,
        (columns, by_odd, by_even, *scalars),
        [pltpu.VMEM((8, ROWS), F32)],
        cost=256 << 20,
    )


def render_kernel(cells, shift_x, shift_y, frac_x, frac_y, extinction, slope, offset, given, own):
    core = lax.axis_index("gx") & 1
    scale = [0.5 * slope[c] for c in range(3)]
    bias = [0.5 * offset[c] for c in range(3)]
    scalars = []
    for k in range(SLICES):
        back = shift_y[k] == -1
        far = jnp.where(back, 1.0 - frac_y[k], frac_y[k])
        near = jnp.where(back, frac_y[k], 1.0 - frac_y[k])
        turn = jnp.where(back, 1, COLS - 1)
        scalars.append((PAD + shift_x[k], 1.0 - frac_x[k], frac_x[k], turn, near, far, extinction[k] * (-LOG2E)))

    def step(out, base, i):
        r = pl.multiple_of(i * STEP, STEP)
        transmit = jnp.ones((STEP, COLS), F32)
        total = [jnp.zeros((STEP, COLS), F32) for _ in range(3)]
        for k in range(SLICES):
            begin, stay, down, turn, near, far, optical = scalars[k]
            upper = cells[k, pl.ds(base + r + begin, STEP), :]
            lower = cells[k, pl.ds(base + r + begin + 1, STEP), :]
            mixed = upper * stay + lower * down
            value = mixed * near + pltpu.roll(mixed, turn, 1) * far
            density = jnp.exp2(value * value * (-LOG2E))
            after = transmit * jnp.exp2(density * optical)
            weight = transmit - after
            transmit = after
            for c in range(3):
                total[c] = total[c] + weight * jnp.tanh(value * scale[c] + bias[c])
        alpha = 1.0 - transmit
        for c in range(3):
            out[c, pl.ds(r, STEP), :] = 0.5 * (alpha + total[c])
        out[3, pl.ds(r, STEP), :] = alpha

    for out, half in ((given, core ^ 1), (own, core)):
        pl.loop(0, HALF // STEP)(functools.partial(step, out, pl.multiple_of(half * HALF, HALF)))


def render(cells, scalars):
    return call(
        render_kernel,
        [image(4, HALF, COLS)] * 2,
        [VMEM] + [SMEM] * 7,
        (cells, *scalars),
        cost=20 << 20,
    )


def pair_kernel(mask, own, other, own_border, other_border, here, plus, minus, far, side):
    index = lax.axis_index("gx")
    y = index >> 1 & 3
    front = (index ^ mask[0]) & 1 == 0
    first = jnp.where(front, own_border[...], other_border[...])
    second = jnp.where(front, other_border[...], own_border[...])
    upper_rows = lax.broadcasted_iota(jnp.int32, (8, HALF), 0) < 4
    merged = first + (1.0 - jnp.where(upper_rows, first[3:4], first[7:8])) * second
    line = lax.broadcasted_iota(jnp.int32, (QUARTER, COLS), 0)
    lane = lax.broadcasted_iota(jnp.int32, (QUARTER, COLS), 1)
    outer = jnp.logical_or(lane == 0, lane == COLS - 1)
    for r in range(0, HALF, QUARTER):
        for c in range(4):
            near, far_side = merged[c : c + 1, r : r + QUARTER], merged[4 + c : 5 + c, r : r + QUARTER]
            side[c, r : r + QUARTER, :] = jnp.transpose(jnp.where(line == 0, near, far_side))
    for away, dest in ((0, here), (1, plus), (3, minus), (2, far)):
        rows = pl.ds(pl.multiple_of((y + away & 3) * QUARTER, QUARTER), QUARTER)

        def run(first, second):
            done = over([first[c, rows, :] for c in range(4)], [second[c, rows, :] for c in range(4)])
            for c in range(4):
                dest[c, :, :] = jnp.where(outer, side[c, rows, :], done[c])

        pl.when(front)(functools.partial(run, own, other))
        pl.when(jnp.logical_not(front))(functools.partial(run, other, own))


def pair(mask, own, other, own_border, other_border):
    return call(
        pair_kernel,
        [image(4, QUARTER, COLS)] * 4,
        [SMEM] + [VMEM] * 4,
        (mask, own, other, own_border, other_border),
        [pltpu.VMEM((4, HALF, COLS), F32)],
    )


def in_order(parts, ranks, rows):
    loaded = [[part[c, rows, :] for c in range(4)] for part in parts]
    image_so_far = None
    for place in range(4):
        chosen = loaded[0]
        for part in range(1, 4):
            here = ranks[part] == place
            chosen = [jnp.where(here, loaded[part][c], chosen[c]) for c in range(4)]
        image_so_far = chosen if image_so_far is None else over(image_so_far, chosen)
    return image_so_far


def quarter_kernel(mask, own, plus, minus, far, here, one, two, three):
    index = lax.axis_index("gx")
    y = index >> 1 & 3
    z = index >> 3
    key = mask[0] >> 1 & 3
    ranks = [((y + away) & 3) ^ key for away in (0, 3, 1, 2)]
    for flip, dest in enumerate((here, one, two, three)):
        rows = pl.ds(pl.multiple_of((z ^ flip) * TILE, TILE), TILE)
        done = in_order((own, plus, minus, far), ranks, rows)
        for c in range(4):
            dest[c, :, :] = done[c]


def quarter(mask, parts):
    return call(quarter_kernel, [image(4, TILE, COLS)] * 4, [SMEM] + [VMEM] * 4, (mask, *parts), cost=1 << 19)


def tile_kernel(mask, own, one, two, three, out):
    z = lax.axis_index("gx") >> 3
    key = mask[0] >> 3 & 3
    ranks = [(z ^ flip) ^ key for flip in range(4)]
    done = in_order((own, one, two, three), ranks, pl.ds(0, TILE))
    for c in range(4):
        out[c, :, :] = done[c]


def tile(mask, parts):
    return call(tile_kernel, image(4, TILE, COLS), [SMEM] + [VMEM] * 4, (mask, *parts), cost=1 << 18)


def join_kernel(own, one, two, three, out):
    z = lax.axis_index("gx") >> 3
    for flip, part in enumerate((own, one, two, three)):
        out[:, pl.ds(pl.multiple_of((z ^ flip) * TILE, TILE), TILE), :] = part[...]


def join(parts):
    return call(join_kernel, image(4, QUARTER, COLS), [VMEM] * 4, parts, cost=1 << 19)


def frame_kernel(*refs):
    parts, out, sems = refs[:8], refs[8], refs[9]
    index = lax.axis_index("gx")
    copies = []
    for n, part in enumerate(parts):
        half = index & 1 ^ (n >> 2)
        y = (index >> 1) + (0, 3, 1, 2)[n & 3] & 3
        rows = pl.ds(pl.multiple_of(half * HALF + y * QUARTER, QUARTER), QUARTER)
        copies.append(pltpu.make_async_copy(part, out.at[:, rows, :], sems.at[n]))
    for copy in copies:
        copy.start()
    for copy in copies:
        copy.wait()


def frame(parts):
    return pl.pallas_call(
        frame_kernel,
        out_shape=image(4, ROWS, COLS),
        in_specs=[VMEM] * 8,
        out_specs=ANY,
        scratch_shapes=[pltpu.SemaphoreType.DMA((8,))],
        compiler_params=pltpu.CompilerParams(vmem_limit_bytes=BIG),
    )(*parts)


def send(block, target):
    return lax.ppermute(block, "gx", [(i, target(i)) for i in range(32)])


def beside(block, first):
    return lax.ppermute(block, "gy", [swap for i in range(first, 7, 2) for swap in ((i, i + 1), (i + 1, i))])


def flip(bits):
    return lambda i: i ^ bits


def along_y(step):
    return lambda i: i & ~6 | ((i >> 1) + step & 3) << 1


def to_quarters(plus, minus, far):
    return send(plus, along_y(1)), send(minus, along_y(3)), send(far, along_y(2))


def body(tsdf, shift_x, shift_y, frac_x, frac_y, extinction, color_slope, color_offset, view_mask):
    scalars = (shift_x, shift_y, frac_x, frac_y, extinction, color_slope, color_offset)
    cells, columns, to_odd, to_even = edges(tsdf)
    by_even = beside(to_even, 0)
    by_odd = beside(to_odd, 1)
    given, own = render(cells, scalars)
    other = send(given, flip(1))
    own, by_odd, by_even = lax.optimization_barrier((own, by_odd, by_even))
    own_border, given_border = border(columns, by_odd, by_even, scalars)
    other_border = send(given_border, flip(1))
    here, plus, minus, far = pair(view_mask, own, other, own_border, other_border)
    here, one, two, three = quarter(view_mask, (here, *to_quarters(plus, minus, far)))
    mine = tile(view_mask, (here, send(one, flip(8)), send(two, flip(16)), send(three, flip(24))))
    block = join((mine, send(mine, flip(8)), send(mine, flip(16)), send(mine, flip(24))))
    blocks = (block, *to_quarters(block, block, block))
    return frame(blocks + tuple(send(b, flip(1)) for b in blocks))


def solution(mesh):
    in_specs = (P("gx", None, "gy"), P("gx"), P("gx"), P("gx"), P("gx"), P("gx"), P(), P(), P())
    out_specs = P(None, None, "gy")
    return jax.shard_map(body, mesh=mesh, in_specs=in_specs, out_specs=out_specs, check_vma=False)
```

time: 149 us -> 72 us (0.48)
  the two profiles are of different devices: /device:TPU:7 before, /device:TPU:5 now
where the time goes in v2:
time: 72 us; the launch traced here: 71.7 us
  starting transfers between devices  38.6 us (54%)
  waiting for transfers between devices  20.6 us (29%)
  Pallas kernels  11.6 us (16%)
  between operations  0.79 us (1%)
    ppermute x18, starting transfers between devices, send(): return lax.ppermute(block, 'gx', [(i, target(i)) for i in range(32)])  28.9 us
    ppermute x18, waiting for transfers between devices, send(): return lax.ppermute(block, 'gx', [(i, target(i)) for i in range(32)])  20.6 us
    pallas_call x7, Pallas kernels, call(): pl.pallas_call(kernel, out_shape=outs, in_specs=ins, out_specs=jax.tree.m...  10.3 us
    ppermute x2, starting transfers between devices, beside(): lax.ppermute(block, 'gy', [swap for i in range(first, 7, 2) for swap in (...  9.74 us
  transfers between devices with their start and end apart: 20, of which 9 were waited for; matrix products, arithmetic and copies ran while one was open for 0% of the time, Pallas kernels for 9%

profile of v2, /device:TPU:5, one launch (start us, length us, event | category | flops | bytes accessed | tf_op | source)
XLA Modules:
  0.0 71.7 jit_solution(8372465750234472395)
XLA Ops:
  0.0 3.2 %shard_map.91 = (f32[8,1040,128]{2,1,0:T(8,128)S(1)}, f32[4,8,1024]{2,1,0:T(8,128)S(1)}, f32[8,1024]{1,0:T(8,128)S(1)}, f32[8,1024]{1,0:T(8,128)S(1)}) custom-call(f32[8,1024,128]{2,1,0:T(8,128)} %tsdf.1), custom_call_target="tpu_custom_call" | custom-call | flops 1073741824 | bytes 4194304 | tf_op jit(solution)/shard_map/pallas_call | solution.py:27
  3.2 2.2 %collective-permute-start = (f32[8,1024]{1,0:T(8,128)S(1)}, f32[8,1024]{1,0:T(8,128)S(1)}, u32[]{:S(2)}, u32[]{:S(2)}) collective-permute-start(f32[8,1024]{1,0:T(8,128)S(1)} %get-tuple-element.26), channel_id=1, source_target_pairs={{1,2},{2,1},{3,4},{4,3},{5,6},{6,5},{9,10},{10,9},{11,12},{12,11},... | collective-permute-start | bytes 98312 | tf_op jit(solution)/shard_map/ppermute | solution.py:315
  5.4 7.6 %collective-permute-start.1 = (f32[8,1024]{1,0:T(8,128)S(1)}, f32[8,1024]{1,0:T(8,128)S(1)}, u32[]{:S(2)}, u32[]{:S(2)}) collective-permute-start(f32[8,1024]{1,0:T(8,128)S(1)} %get-tuple-element.27), channel_id=1, source_target_pairs={{0,1},{1,0},{2,3},{3,2},{4,5},{5,4},{6,7},{7,6},{8,9},{9,8},{10,11... | collective-permute-start | bytes 98312 | tf_op jit(solution)/shard_map/ppermute | solution.py:315
  13.0 5.4 %shard_map.92 = (f32[4,512,128]{2,1,0:T(8,128)S(1)}, f32[4,512,128]{2,1,0:T(8,128)S(1)}) custom-call(f32[8,1040,128]{2,1,0:T(8,128)S(1)} %get-tuple-element.24.cells, s32[8]{0:T(128)S(1)} %copy-done, s32[8]{0:T(128)S(1)} %copy-done.1, f32[8]{0:T(128)S(1)} %copy-done.2, f32[8]{0:T(128)S(1)} %copy-done.3, f32[8]{0:T(128)S(1)} %copy-done.4, f32[3]{0:T(128)S(1)} %copy-done.5, ...), custom_call_target="tpu_custom_call" | custom-call | flops 5368709120 | bytes 20971520 | tf_op jit(solution)/shard_map/pallas_call | solution.py:27
  18.4 1.3 %collective-permute-start.2 = (f32[4,512,128]{2,1,0:T(8,128)S(1)}, f32[4,512,128]{2,1,0:T(8,128)S(1)}, u32[]{:S(2)}, u32[]{:S(2)}) collective-permute-start(f32[4,512,128]{2,1,0:T(8,128)S(1)} %get-tuple-element.29), channel_id=1, source_target_pairs={{0,8},{8,0},{16,24},{24,16},{32,40},{40,32},{48,56},{56,48},{64,72... | collective-permute-start | bytes 3145736 | tf_op jit(solution)/shard_map/ppermute | solution.py:311
  22.7 1.4 %collective-permute-start.4 = (f32[4,128,128]{2,1,0:T(8,128)S(1)}, f32[4,128,128]{2,1,0:T(8,128)S(1)}, u32[]{:S(2)}, u32[]{:S(2)}) collective-permute-start(f32[4,128,128]{2,1,0:T(8,128)S(1)} %get-tuple-element.36), channel_id=1, source_target_pairs={{0,16},{8,24},{16,32},{24,40},{32,48},{40,56},{48,0},{56,8},{64,80... | collective-permute-start | bytes 786440 | tf_op jit(solution)/shard_map/ppermute | solution.py:311
  24.1 1.5 %collective-permute-start.5 = (f32[4,128,128]{2,1,0:T(8,128)S(1)}, f32[4,128,128]{2,1,0:T(8,128)S(1)}, u32[]{:S(2)}, u32[]{:S(2)}) collective-permute-start(f32[4,128,128]{2,1,0:T(8,128)S(1)} %get-tuple-element.37), channel_id=1, source_target_pairs={{0,48},{8,56},{16,0},{24,8},{32,16},{40,24},{48,32},{56,40},{64,11... | collective-permute-start | bytes 786440 | tf_op jit(solution)/shard_map/ppermute | solution.py:311
  25.6 1.5 %collective-permute-start.6 = (f32[4,128,128]{2,1,0:T(8,128)S(1)}, f32[4,128,128]{2,1,0:T(8,128)S(1)}, u32[]{:S(2)}, u32[]{:S(2)}) collective-permute-start(f32[4,128,128]{2,1,0:T(8,128)S(1)} %get-tuple-element.38), channel_id=1, source_target_pairs={{0,32},{8,40},{16,48},{24,56},{32,0},{40,8},{48,16},{56,24},{64,96... | collective-permute-start | bytes 786440 | tf_op jit(solution)/shard_map/ppermute | solution.py:311
  27.1 4.5 %collective-permute-done.4.plus = f32[4,128,128]{2,1,0:T(8,128)S(1)} collective-permute-done((f32[4,128,128]{2,1,0:T(8,128)S(1)}, f32[4,128,128]{2,1,0:T(8,128)S(1)}, u32[]{:S(2)}, u32[]{:S(2)}) %collective-permute-start.4) | collective-permute-done | bytes 262176 | tf_op jit(solution)/shard_map/ppermute | solution.py:311
  31.6 6.7 %collective-permute-done.6.far = f32[4,128,128]{2,1,0:T(8,128)S(1)} collective-permute-done((f32[4,128,128]{2,1,0:T(8,128)S(1)}, f32[4,128,128]{2,1,0:T(8,128)S(1)}, u32[]{:S(2)}, u32[]{:S(2)}) %collective-permute-start.6) | collective-permute-done | bytes 262176 | tf_op jit(solution)/shard_map/ppermute | solution.py:311
  39.3 1.2 %collective-permute-start.8 = (f32[4,32,128]{2,1,0:T(8,128)S(1)}, f32[4,32,128]{2,1,0:T(8,128)S(1)}, u32[]{:S(2)}, u32[]{:S(2)}) collective-permute-start(f32[4,32,128]{2,1,0:T(8,128)S(1)} %get-tuple-element.41), channel_id=1, source_target_pairs={{0,128},{8,136},{16,144},{24,152},{32,160},{40,168},{48,176},{56,1... | collective-permute-start | bytes 196616 | tf_op jit(solution)/shard_map/ppermute | solution.py:311
  40.5 1.6 %collective-permute-start.9 = (f32[4,32,128]{2,1,0:T(8,128)S(1)}, f32[4,32,128]{2,1,0:T(8,128)S(1)}, u32[]{:S(2)}, u32[]{:S(2)}) collective-permute-start(f32[4,32,128]{2,1,0:T(8,128)S(1)} %get-tuple-element.42), channel_id=1, source_target_pairs={{0,192},{8,200},{16,208},{24,216},{32,224},{40,232},{48,240},{56,2... | collective-permute-start | bytes 196616 | tf_op jit(solution)/shard_map/ppermute | solution.py:311
  42.1 1.8 %collective-permute-done.8.two = f32[4,32,128]{2,1,0:T(8,128)S(1)} collective-permute-done((f32[4,32,128]{2,1,0:T(8,128)S(1)}, f32[4,32,128]{2,1,0:T(8,128)S(1)}, u32[]{:S(2)}, u32[]{:S(2)}) %collective-permute-start.8) | collective-permute-done | bytes 65568 | tf_op jit(solution)/shard_map/ppermute | solution.py:311
  44.0 2.0 %collective-permute-done.9.three = f32[4,32,128]{2,1,0:T(8,128)S(1)} collective-permute-done((f32[4,32,128]{2,1,0:T(8,128)S(1)}, f32[4,32,128]{2,1,0:T(8,128)S(1)}, u32[]{:S(2)}, u32[]{:S(2)}) %collective-permute-start.9) | collective-permute-done | bytes 65568 | tf_op jit(solution)/shard_map/ppermute | solution.py:311
  46.1 1.9 %collective-permute-start.11 = (f32[4,32,128]{2,1,0:T(8,128)S(1)}, f32[4,32,128]{2,1,0:T(8,128)S(1)}, u32[]{:S(2)}, u32[]{:S(2)}) collective-permute-start(f32[4,32,128]{2,1,0:T(8,128)S(1)} %shard_map.96.own), channel_id=1, source_target_pairs={{0,128},{8,136},{16,144},{24,152},{32,160},{40,168},{48,176},{56,1... | collective-permute-start | bytes 196616 | tf_op jit(solution)/shard_map/ppermute | solution.py:311
  48.0 1.7 %collective-permute-start.12 = (f32[4,32,128]{2,1,0:T(8,128)S(1)}, f32[4,32,128]{2,1,0:T(8,128)S(1)}, u32[]{:S(2)}, u32[]{:S(2)}) collective-permute-start(f32[4,32,128]{2,1,0:T(8,128)S(1)} %shard_map.96.own), channel_id=1, source_target_pairs={{0,192},{8,200},{16,208},{24,216},{32,224},{40,232},{48,240},{56,2... | collective-permute-start | bytes 196616 | tf_op jit(solution)/shard_map/ppermute | solution.py:311
  50.2 3.1 %collective-permute-done.12.three = f32[4,32,128]{2,1,0:T(8,128)S(1)} collective-permute-done((f32[4,32,128]{2,1,0:T(8,128)S(1)}, f32[4,32,128]{2,1,0:T(8,128)S(1)}, u32[]{:S(2)}, u32[]{:S(2)}) %collective-permute-start.12) | collective-permute-done | bytes 65568 | tf_op jit(solution)/shard_map/ppermute | solution.py:311
  53.5 2.6 %collective-permute-start.14 = (f32[4,128,128]{2,1,0:T(8,128)S(1)}, f32[4,128,128]{2,1,0:T(8,128)S(1)}, u32[]{:S(2)}, u32[]{:S(2)}) collective-permute-start(f32[4,128,128]{2,1,0:T(8,128)S(1)} %shard_map.97.refs_0_), channel_id=1, source_target_pairs={{0,48},{8,56},{16,0},{24,8},{32,16},{40,24},{48,32},{56,40},{64,11... | collective-permute-start | bytes 786440 | tf_op jit(solution)/shard_map/ppermute | solution.py:311
  56.1 4.4 %collective-permute-start.16 = (f32[4,128,128]{2,1,0:T(8,128)S(1)}, f32[4,128,128]{2,1,0:T(8,128)S(1)}, u32[]{:S(2)}, u32[]{:S(2)}) collective-permute-start(f32[4,128,128]{2,1,0:T(8,128)S(1)} %shard_map.97.refs_0_), channel_id=1, source_target_pairs={{0,8},{8,0},{16,24},{24,16},{32,40},{40,32},{48,56},{56,48},{64,72... | collective-permute-start | bytes 786440 | tf_op jit(solution)/shard_map/ppermute | solution.py:311
  60.6 5.8 %collective-permute-start.17 = (f32[4,128,128]{2,1,0:T(8,128)S(1)}, f32[4,128,128]{2,1,0:T(8,128)S(1)}, u32[]{:S(2)}, u32[]{:S(2)}) collective-permute-start(f32[4,128,128]{2,1,0:T(8,128)S(1)} %collective-permute-done.13.refs_1_), channel_id=1, source_target_pairs={{0,8},{8,0},{16,24},{24,16},{32,40},{40,32},{48,56},{56,48},{64,72... | collective-permute-start | bytes 786440 | tf_op jit(solution)/shard_map/ppermute | solution.py:311
  66.4 1.9 %collective-permute-start.18 = (f32[4,128,128]{2,1,0:T(8,128)S(1)}, f32[4,128,128]{2,1,0:T(8,128)S(1)}, u32[]{:S(2)}, u32[]{:S(2)}) collective-permute-start(f32[4,128,128]{2,1,0:T(8,128)S(1)} %collective-permute-done.14.refs_2_), channel_id=1, source_target_pairs={{0,8},{8,0},{16,24},{24,16},{32,40},{40,32},{48,56},{56,48},{64,72... | collective-permute-start | bytes 786440 | tf_op jit(solution)/shard_map/ppermute | solution.py:311
  68.3 0.9 %collective-permute-start.19 = (f32[4,128,128]{2,1,0:T(8,128)S(1)}, f32[4,128,128]{2,1,0:T(8,128)S(1)}, u32[]{:S(2)}, u32[]{:S(2)}) collective-permute-start(f32[4,128,128]{2,1,0:T(8,128)S(1)} %collective-permute-done.15.refs_3_), channel_id=1, source_target_pairs={{0,8},{8,0},{16,24},{24,16},{32,40},{40,32},{48,56},{56,48},{64,72... | collective-permute-start | bytes 786440 | tf_op jit(solution)/shard_map/ppermute | solution.py:311
  69.4 0.9 %collective-permute-done.19.refs_7_ = f32[4,128,128]{2,1,0:T(8,128)S(1)} collective-permute-done((f32[4,128,128]{2,1,0:T(8,128)S(1)}, f32[4,128,128]{2,1,0:T(8,128)S(1)}, u32[]{:S(2)}, u32[]{:S(2)}) %collective-permute-start.19) | collective-permute-done | bytes 262176 | tf_op jit(solution)/shard_map/ppermute | solution.py:311
  70.3 1.4 %shard_map.98 = f32[4,1024,128]{2,1,0:T(8,128)} custom-call(f32[4,128,128]{2,1,0:T(8,128)S(1)} %shard_map.97.refs_0_, f32[4,128,128]{2,1,0:T(8,128)S(1)} %collective-permute-done.13.refs_1_, f32[4,128,128]{2,1,0:T(8,128)S(1)} %collective-permute-done.14.refs_2_, f32[4,128,128]{2,1,0:T(8,128)S(1)} %collective-permute-done.15.refs_3_, ...), custom_call_target="tpu_custom_call" | custom-call | tf_op jit(solution)/shard_map/pallas_call | solution.py:300
  (38 shorter events, 4.4 us)
Async XLA Ops:
  0.0 13.0 %copy-start = (s32[8]{0:T(128)S(1)}, s32[8]{0:T(128)}, u32[]{:S(2)}) copy-start(s32[8]{0:T(128)} %shift_x.3) | copy-start | bytes 100
  0.0 13.0 %copy-start.1 = (s32[8]{0:T(128)S(1)}, s32[8]{0:T(128)}, u32[]{:S(2)}) copy-start(s32[8]{0:T(128)} %shift_y.3) | copy-start | bytes 100
  0.0 13.0 %copy-start.2 = (f32[8]{0:T(128)S(1)}, f32[8]{0:T(128)}, u32[]{:S(2)}) copy-start(f32[8]{0:T(128)} %frac_x.3) | copy-start | bytes 100
  0.0 13.0 %copy-start.3 = (f32[8]{0:T(128)S(1)}, f32[8]{0:T(128)}, u32[]{:S(2)}) copy-start(f32[8]{0:T(128)} %frac_y.3) | copy-start | bytes 100
  3.2 16.5 %collective-permute-start = (f32[8,1024]{1,0:T(8,128)S(1)}, f32[8,1024]{1,0:T(8,128)S(1)}, u32[]{:S(2)}, u32[]{:S(2)}) collective-permute-start(f32[8,1024]{1,0:T(8,128)S(1)} %get-tuple-element.26), channel_id=1, source_target_pairs={{1,2},{2,1},{3,4},{4,3},{5,6},{6,5},{9,10},{10,9},{11,12},{12,11},... | collective-permute-start | bytes 98312 | tf_op jit(solution)/shard_map/ppermute | solution.py:315
  5.4 14.4 %collective-permute-start.1 = (f32[8,1024]{1,0:T(8,128)S(1)}, f32[8,1024]{1,0:T(8,128)S(1)}, u32[]{:S(2)}, u32[]{:S(2)}) collective-permute-start(f32[8,1024]{1,0:T(8,128)S(1)} %get-tuple-element.27), channel_id=1, source_target_pairs={{0,1},{1,0},{2,3},{3,2},{4,5},{5,4},{6,7},{7,6},{8,9},{9,8},{10,11... | collective-permute-start | bytes 98312 | tf_op jit(solution)/shard_map/ppermute | solution.py:315
  18.4 3.6 %collective-permute-start.2 = (f32[4,512,128]{2,1,0:T(8,128)S(1)}, f32[4,512,128]{2,1,0:T(8,128)S(1)}, u32[]{:S(2)}, u32[]{:S(2)}) collective-permute-start(f32[4,512,128]{2,1,0:T(8,128)S(1)} %get-tuple-element.29), channel_id=1, source_target_pairs={{0,8},{8,0},{16,24},{24,16},{32,40},{40,32},{48,56},{56,48},{64,72... | collective-permute-start | bytes 3145736 | tf_op jit(solution)/shard_map/ppermute | solution.py:311
  20.6 1.5 %collective-permute-start.3 = (f32[8,512]{1,0:T(8,128)S(1)}, f32[8,512]{1,0:T(8,128)S(1)}, u32[]{:S(2)}, u32[]{:S(2)}) collective-permute-start(f32[8,512]{1,0:T(8,128)S(1)} %get-tuple-element.34), channel_id=1, source_target_pairs={{0,8},{8,0},{16,24},{24,16},{32,40},{40,32},{48,56},{56,48},{64,72... | collective-permute-start | bytes 49160 | tf_op jit(solution)/shard_map/ppermute | solution.py:311
  22.7 9.0 %collective-permute-start.4 = (f32[4,128,128]{2,1,0:T(8,128)S(1)}, f32[4,128,128]{2,1,0:T(8,128)S(1)}, u32[]{:S(2)}, u32[]{:S(2)}) collective-permute-start(f32[4,128,128]{2,1,0:T(8,128)S(1)} %get-tuple-element.36), channel_id=1, source_target_pairs={{0,16},{8,24},{16,32},{24,40},{32,48},{40,56},{48,0},{56,8},{64,80... | collective-permute-start | bytes 786440 | tf_op jit(solution)/shard_map/ppermute | solution.py:311
  24.1 7.6 %collective-permute-start.5 = (f32[4,128,128]{2,1,0:T(8,128)S(1)}, f32[4,128,128]{2,1,0:T(8,128)S(1)}, u32[]{:S(2)}, u32[]{:S(2)}) collective-permute-start(f32[4,128,128]{2,1,0:T(8,128)S(1)} %get-tuple-element.37), channel_id=1, source_target_pairs={{0,48},{8,56},{16,0},{24,8},{32,16},{40,24},{48,32},{56,40},{64,11... | collective-permute-start | bytes 786440 | tf_op jit(solution)/shard_map/ppermute | solution.py:311
  25.6 12.8 %collective-permute-start.6 = (f32[4,128,128]{2,1,0:T(8,128)S(1)}, f32[4,128,128]{2,1,0:T(8,128)S(1)}, u32[]{:S(2)}, u32[]{:S(2)}) collective-permute-start(f32[4,128,128]{2,1,0:T(8,128)S(1)} %get-tuple-element.38), channel_id=1, source_target_pairs={{0,32},{8,40},{16,48},{24,56},{32,0},{40,8},{48,16},{56,24},{64,96... | collective-permute-start | bytes 786440 | tf_op jit(solution)/shard_map/ppermute | solution.py:311
  38.5 3.6 %collective-permute-start.7 = (f32[4,32,128]{2,1,0:T(8,128)S(1)}, f32[4,32,128]{2,1,0:T(8,128)S(1)}, u32[]{:S(2)}, u32[]{:S(2)}) collective-permute-start(f32[4,32,128]{2,1,0:T(8,128)S(1)} %get-tuple-element.40), channel_id=1, source_target_pairs={{0,64},{8,72},{16,80},{24,88},{32,96},{40,104},{48,112},{56,120},{... | collective-permute-start | bytes 196616 | tf_op jit(solution)/shard_map/ppermute | solution.py:311
  39.3 4.6 %collective-permute-start.8 = (f32[4,32,128]{2,1,0:T(8,128)S(1)}, f32[4,32,128]{2,1,0:T(8,128)S(1)}, u32[]{:S(2)}, u32[]{:S(2)}) collective-permute-start(f32[4,32,128]{2,1,0:T(8,128)S(1)} %get-tuple-element.41), channel_id=1, source_target_pairs={{0,128},{8,136},{16,144},{24,152},{32,160},{40,168},{48,176},{56,1... | collective-permute-start | bytes 196616 | tf_op jit(solution)/shard_map/ppermute | solution.py:311
  40.5 5.4 %collective-permute-start.9 = (f32[4,32,128]{2,1,0:T(8,128)S(1)}, f32[4,32,128]{2,1,0:T(8,128)S(1)}, u32[]{:S(2)}, u32[]{:S(2)}) collective-permute-start(f32[4,32,128]{2,1,0:T(8,128)S(1)} %get-tuple-element.42), channel_id=1, source_target_pairs={{0,192},{8,200},{16,208},{24,216},{32,224},{40,232},{48,240},{56,2... | collective-permute-start | bytes 196616 | tf_op jit(solution)/shard_map/ppermute | solution.py:311
  46.0 3.6 %collective-permute-start.10 = (f32[4,32,128]{2,1,0:T(8,128)S(1)}, f32[4,32,128]{2,1,0:T(8,128)S(1)}, u32[]{:S(2)}, u32[]{:S(2)}) collective-permute-start(f32[4,32,128]{2,1,0:T(8,128)S(1)} %shard_map.96.own), channel_id=1, source_target_pairs={{0,64},{8,72},{16,80},{24,88},{32,96},{40,104},{48,112},{56,120},{... | collective-permute-start | bytes 196616 | tf_op jit(solution)/shard_map/ppermute | solution.py:311
  46.1 4.1 %collective-permute-start.11 = (f32[4,32,128]{2,1,0:T(8,128)S(1)}, f32[4,32,128]{2,1,0:T(8,128)S(1)}, u32[]{:S(2)}, u32[]{:S(2)}) collective-permute-start(f32[4,32,128]{2,1,0:T(8,128)S(1)} %shard_map.96.own), channel_id=1, source_target_pairs={{0,128},{8,136},{16,144},{24,152},{32,160},{40,168},{48,176},{56,1... | collective-permute-start | bytes 196616 | tf_op jit(solution)/shard_map/ppermute | solution.py:311
  48.0 5.4 %collective-permute-start.12 = (f32[4,32,128]{2,1,0:T(8,128)S(1)}, f32[4,32,128]{2,1,0:T(8,128)S(1)}, u32[]{:S(2)}, u32[]{:S(2)}) collective-permute-start(f32[4,32,128]{2,1,0:T(8,128)S(1)} %shard_map.96.own), channel_id=1, source_target_pairs={{0,192},{8,200},{16,208},{24,216},{32,224},{40,232},{48,240},{56,2... | collective-permute-start | bytes 196616 | tf_op jit(solution)/shard_map/ppermute | solution.py:311
  53.4 7.2 %collective-permute-start.13 = (f32[4,128,128]{2,1,0:T(8,128)S(1)}, f32[4,128,128]{2,1,0:T(8,128)S(1)}, u32[]{:S(2)}, u32[]{:S(2)}) collective-permute-start(f32[4,128,128]{2,1,0:T(8,128)S(1)} %shard_map.97.refs_0_), channel_id=1, source_target_pairs={{0,16},{8,24},{16,32},{24,40},{32,48},{40,56},{48,0},{56,8},{64,80... | collective-permute-start | bytes 786440 | tf_op jit(solution)/shard_map/ppermute | solution.py:311
  53.5 12.8 %collective-permute-start.14 = (f32[4,128,128]{2,1,0:T(8,128)S(1)}, f32[4,128,128]{2,1,0:T(8,128)S(1)}, u32[]{:S(2)}, u32[]{:S(2)}) collective-permute-start(f32[4,128,128]{2,1,0:T(8,128)S(1)} %shard_map.97.refs_0_), channel_id=1, source_target_pairs={{0,48},{8,56},{16,0},{24,8},{32,16},{40,24},{48,32},{56,40},{64,11... | collective-permute-start | bytes 786440 | tf_op jit(solution)/shard_map/ppermute | solution.py:311
  56.1 12.1 %collective-permute-start.15 = (f32[4,128,128]{2,1,0:T(8,128)S(1)}, f32[4,128,128]{2,1,0:T(8,128)S(1)}, u32[]{:S(2)}, u32[]{:S(2)}) collective-permute-start(f32[4,128,128]{2,1,0:T(8,128)S(1)} %shard_map.97.refs_0_), channel_id=1, source_target_pairs={{0,32},{8,40},{16,48},{24,56},{32,0},{40,8},{48,16},{56,24},{64,96... | collective-permute-start | bytes 786440 | tf_op jit(solution)/shard_map/ppermute | solution.py:311
  56.1 13.0 %collective-permute-start.16 = (f32[4,128,128]{2,1,0:T(8,128)S(1)}, f32[4,128,128]{2,1,0:T(8,128)S(1)}, u32[]{:S(2)}, u32[]{:S(2)}) collective-permute-start(f32[4,128,128]{2,1,0:T(8,128)S(1)} %shard_map.97.refs_0_), channel_id=1, source_target_pairs={{0,8},{8,0},{16,24},{24,16},{32,40},{40,32},{48,56},{56,48},{64,72... | collective-permute-start | bytes 786440 | tf_op jit(solution)/shard_map/ppermute | solution.py:311
  60.6 8.6 %collective-permute-start.17 = (f32[4,128,128]{2,1,0:T(8,128)S(1)}, f32[4,128,128]{2,1,0:T(8,128)S(1)}, u32[]{:S(2)}, u32[]{:S(2)}) collective-permute-start(f32[4,128,128]{2,1,0:T(8,128)S(1)} %collective-permute-done.13.refs_1_), channel_id=1, source_target_pairs={{0,8},{8,0},{16,24},{24,16},{32,40},{40,32},{48,56},{56,48},{64,72... | collective-permute-start | bytes 786440 | tf_op jit(solution)/shard_map/ppermute | solution.py:311
  66.4 3.1 %collective-permute-start.18 = (f32[4,128,128]{2,1,0:T(8,128)S(1)}, f32[4,128,128]{2,1,0:T(8,128)S(1)}, u32[]{:S(2)}, u32[]{:S(2)}) collective-permute-start(f32[4,128,128]{2,1,0:T(8,128)S(1)} %collective-permute-done.14.refs_2_), channel_id=1, source_target_pairs={{0,8},{8,0},{16,24},{24,16},{32,40},{40,32},{48,56},{56,48},{64,72... | collective-permute-start | bytes 786440 | tf_op jit(solution)/shard_map/ppermute | solution.py:311
  68.3 2.1 %collective-permute-start.19 = (f32[4,128,128]{2,1,0:T(8,128)S(1)}, f32[4,128,128]{2,1,0:T(8,128)S(1)}, u32[]{:S(2)}, u32[]{:S(2)}) collective-permute-start(f32[4,128,128]{2,1,0:T(8,128)S(1)} %collective-permute-done.15.refs_3_), channel_id=1, source_target_pairs={{0,8},{8,0},{16,24},{24,16},{32,40},{40,32},{48,56},{56,48},{64,72... | collective-permute-start | bytes 786440 | tf_op jit(solution)/shard_map/ppermute | solution.py:311
  (3 other events, 38.9 us)

commit v3 on v2

--- a/solution.py
+++ b/solution.py
@@ -11,9 +11,10 @@
 F32 = jnp.float32
 SLICES, ROWS, COLS = 8, 1024, 128
 HALF, QUARTER, TILE = 512, 128, 32
-STEP = 64
-CHUNK = 128
-AHEAD = 8
+STEP = 512
+AWAY = (0, 1, 3, 2)
+CHUNK = 256
+AHEAD = 4
 PAD = 8
 LOG2E = math.log2(math.e)
 VMEM = pl.BlockSpec(memory_space=pltpu.VMEM)
@@ -192,9 +193,11 @@
     )
 
 
-def pair_kernel(mask, own, other, own_border, other_border, here, plus, minus, far, side):
+def pair_kernel(mask, own, other, own_border, other_border, *refs):
+    dests, side = refs[:8], refs[8]
     index = lax.axis_index("gx")
     y = index >> 1 & 3
+    z = index >> 3
     front = (index ^ mask[0]) & 1 == 0
     first = jnp.where(front, own_border[...], other_border[...])
     second = jnp.where(front, other_border[...], own_border[...])
@@ -207,104 +210,119 @@
         for c in range(4):
             near, far_side = merged[c : c + 1, r : r + QUARTER], merged[4 + c : 5 + c, r : r + QUARTER]
             side[c, r : r + QUARTER, :] = jnp.transpose(jnp.where(line == 0, near, far_side))
-    for away, dest in ((0, here), (1, plus), (3, minus), (2, far)):
-        rows = pl.ds(pl.multiple_of((y + away & 3) * QUARTER, QUARTER), QUARTER)
-
-        def run(first, second):
-            done = over([first[c, rows, :] for c in range(4)], [second[c, rows, :] for c in range(4)])
-            for c in range(4):
-                dest[c, :, :] = jnp.where(outer, side[c, rows, :], done[c])
-
-        pl.when(front)(functools.partial(run, own, other))
-        pl.when(jnp.logical_not(front))(functools.partial(run, other, own))
+    outer = outer[:TILE]
+    for away, rest, single in zip(AWAY, dests[:4], dests[4:]):
+        for bits in range(4):
+            rows = pl.ds(pl.multiple_of((y + away & 3) * QUARTER + (z ^ bits) * TILE, TILE), TILE)
+            dest = rest.at[bits - 1] if bits else single.at[0]
+
+            def run(dest, rows, first, second):
+                done = over([first[c, rows, :] for c in range(4)], [second[c, rows, :] for c in range(4)])
+                for c in range(4):
+                    dest[c, :, :] = jnp.where(outer, side[c, rows, :], done[c])
+
+            pl.when(front)(functools.partial(run, dest, rows, own, other))
+            pl.when(jnp.logical_not(front))(functools.partial(run, dest, rows, other, own))
 
 
 def pair(mask, own, other, own_border, other_border):
     return call(
         pair_kernel,
-        [image(4, QUARTER, COLS)] * 4,
+        [image(3, 4, TILE, COLS)] * 4 + [image(1, 4, TILE, COLS)] * 4,
         [SMEM] + [VMEM] * 4,
         (mask, own, other, own_border, other_border),
         [pltpu.VMEM((4, HALF, COLS), F32)],
     )
 
 
-def in_order(parts, ranks, rows):
-    loaded = [[part[c, rows, :] for c in range(4)] for part in parts]
+def in_order(parts, ranks):
     image_so_far = None
     for place in range(4):
-        chosen = loaded[0]
+        chosen = parts[0]
         for part in range(1, 4):
             here = ranks[part] == place
-            chosen = [jnp.where(here, loaded[part][c], chosen[c]) for c in range(4)]
+            chosen = [jnp.where(here, parts[part][c], chosen[c]) for c in range(4)]
         image_so_far = chosen if image_so_far is None else over(image_so_far, chosen)
     return image_so_far
 
 
-def quarter_kernel(mask, own, plus, minus, far, here, one, two, three):
+def along_y_ranks(mask):
+    y = lax.axis_index("gx") >> 1 & 3
+    return [(y - away & 3) ^ (mask[0] >> 1 & 3) for away in AWAY]
+
+
+def channels(ref):
+    return [ref[c] for c in range(4)]
+
+
+def quarter_kernel(mask, *refs):
+    ranks = along_y_ranks(mask)
+    outs = refs[4:]
+    for n, out in enumerate(outs):
+        done = in_order([channels(ref.at[n]) for ref in refs[:4]], ranks)
+        for c in range(4):
+            out[c, :, :] = done[c]
+
+
+def quarter(mask, parts, cost):
+    tiles = parts[0].shape[0]
+    return call(
+        quarter_kernel, [image(4, TILE, COLS)] * tiles, [SMEM] + [VMEM] * 4, (mask, *parts), cost=cost
+    )
+
+
+def tile_kernel(mask, *refs):
+    z = lax.axis_index("gx") >> 3
+    ranks = [(z ^ bits) ^ (mask[0] >> 3 & 3) for bits in (0, 2, 3, 1)]
+    done = in_order([channels(ref) for ref in refs[:4]], ranks)
+    for c in range(4):
+        refs[4][c, :, :] = done[c]
+
+
+def tile(mask, parts):
+    return call(tile_kernel, image(4, TILE, COLS), [SMEM] + [VMEM] * 4, (mask, *parts))
+
+
+def join_kernel(*refs):
+    for n, part in enumerate(refs[:-1]):
+        refs[-1][n] = part[...]
+
+
+def join(*parts):
+    return call(join_kernel, image(len(parts), 4, TILE, COLS), [VMEM] * len(parts), parts, cost=256 << 20)
+
+
+def frame_kernel(places, *refs):
+    parts, out, sems = refs[: len(places)], refs[-2], refs[-1]
     index = lax.axis_index("gx")
-    y = index >> 1 & 3
-    z = index >> 3
-    key = mask[0] >> 1 & 3
-    ranks = [((y + away) & 3) ^ key for away in (0, 3, 1, 2)]
-    for flip, dest in enumerate((here, one, two, three)):
-        rows = pl.ds(pl.multiple_of((z ^ flip) * TILE, TILE), TILE)
-        done = in_order((own, plus, minus, far), ranks, rows)
-        for c in range(4):
-            dest[c, :, :] = done[c]
-
-
-def quarter(mask, parts):
-    return call(quarter_kernel, [image(4, TILE, COLS)] * 4, [SMEM] + [VMEM] * 4, (mask, *parts), cost=1 << 19)
-
-
-def tile_kernel(mask, own, one, two, three, out):
-    z = lax.axis_index("gx") >> 3
-    key = mask[0] >> 3 & 3
-    ranks = [(z ^ flip) ^ key for flip in range(4)]
-    done = in_order((own, one, two, three), ranks, pl.ds(0, TILE))
-    for c in range(4):
-        out[c, :, :] = done[c]
-
-
-def tile(mask, parts):
-    return call(tile_kernel, image(4, TILE, COLS), [SMEM] + [VMEM] * 4, (mask, *parts), cost=1 << 18)
-
-
-def join_kernel(own, one, two, three, out):
-    z = lax.axis_index("gx") >> 3
-    for flip, part in enumerate((own, one, two, three)):
-        out[:, pl.ds(pl.multiple_of((z ^ flip) * TILE, TILE), TILE), :] = part[...]
-
-
-def join(parts):
-    return call(join_kernel, image(4, QUARTER, COLS), [VMEM] * 4, parts, cost=1 << 19)
-
-
-def frame_kernel(*refs):
-    parts, out, sems = refs[:8], refs[8], refs[9]
-    index = lax.axis_index("gx")
+
+    def put(source, side, n, bits):
+        y = (index >> 1) - AWAY[n] & 3
+        row = (index & 1 ^ side) * HALF + y * QUARTER + (index >> 3 ^ bits) * TILE
+        rows = pl.ds(pl.multiple_of(row, TILE), TILE)
+        copies.append(pltpu.make_async_copy(source, out.at[:, rows, :], sems.at[len(copies)]))
+
     copies = []
-    for n, part in enumerate(parts):
-        half = index & 1 ^ (n >> 2)
-        y = (index >> 1) + (0, 3, 1, 2)[n & 3] & 3
-        rows = pl.ds(pl.multiple_of(half * HALF + y * QUARTER, QUARTER), QUARTER)
-        copies.append(pltpu.make_async_copy(part, out.at[:, rows, :], sems.at[n]))
+    for part, (side, n) in zip(parts, places):
+        for m in range(part.shape[0]):
+            put(part.at[m], side, *((m, 0) if n is None else (n, (2, 3, 1)[m])))
     for copy in copies:
         copy.start()
     for copy in copies:
         copy.wait()
 
 
-def frame(parts):
+def frame(places, parts, begun=()):
+    count = sum(part.shape[0] for part in parts)
     return pl.pallas_call(
-        frame_kernel,
+        functools.partial(frame_kernel, places),
         out_shape=image(4, ROWS, COLS),
-        in_specs=[VMEM] * 8,
+        in_specs=[VMEM] * len(parts) + [ANY] * len(begun),
         out_specs=ANY,
-        scratch_shapes=[pltpu.SemaphoreType.DMA((8,))],
+        scratch_shapes=[pltpu.SemaphoreType.DMA((count,))],
+        input_output_aliases={len(parts): 0} if begun else {},
         compiler_params=pltpu.CompilerParams(vmem_limit_bytes=BIG),
-    )(*parts)
+    )(*parts, *begun)
 
 
 def send(block, target):
@@ -321,6 +339,11 @@
 
 def along_y(step):
     return lambda i: i & ~6 | ((i >> 1) + step & 3) << 1
+
+
+def along_z(one, two, three):
+    two, three, one = send(two, flip(16)), send(three, flip(24)), send(one, flip(8))
+    return two, three, one
 
 
 def to_quarters(plus, minus, far):
@@ -334,15 +357,24 @@
     by_odd = beside(to_odd, 1)
     given, own = render(cells, scalars)
     other = send(given, flip(1))
-    own, by_odd, by_even = lax.optimization_barrier((own, by_odd, by_even))
+    by_odd, by_even, own = lax.optimization_barrier((by_odd, by_even, own))
     own_border, given_border = border(columns, by_odd, by_even, scalars)
     other_border = send(given_border, flip(1))
-    here, plus, minus, far = pair(view_mask, own, other, own_border, other_border)
-    here, one, two, three = quarter(view_mask, (here, *to_quarters(plus, minus, far)))
-    mine = tile(view_mask, (here, send(one, flip(8)), send(two, flip(16)), send(three, flip(24))))
-    block = join((mine, send(mine, flip(8)), send(mine, flip(16)), send(mine, flip(24))))
-    blocks = (block, *to_quarters(block, block, block))
-    return frame(blocks + tuple(send(b, flip(1)) for b in blocks))
+    pieces = pair(view_mask, own, other, own_border, other_border)
+    rests, singles = pieces[:4], pieces[4:]
+    came = to_quarters(*rests[1:])
+    came_first, *singles = lax.optimization_barrier((came[0], *singles))
+    one, two, three = quarter(view_mask, (rests[0], came_first, *came[1:]), 1 << 20)
+    over_z = along_z(one, two, three)
+    (mine,) = quarter(view_mask, (singles[0], *to_quarters(*singles[1:])), 256 << 20)
+    mine = tile(view_mask, (mine, *over_z))
+    rest = join(*along_z(mine, mine, mine))
+    singles = join(mine, *to_quarters(mine, mine, mine))
+    blocks = (singles, rest, *to_quarters(rest, rest, rest))
+    others = tuple(send(block, flip(1)) for block in blocks)
+    places = [(side, n) for side in range(2) for n in (None, 0, 1, 2, 3)]
+    begun = frame(places[:7], blocks + others[:2])
+    return frame(places[7:], others[2:], (begun,))
 
 
 def solution(mesh):

time: 72 us -> 67.1 us (0.932)
  waiting for transfers between devices: 20.6 us -> 10.7 us
  starting transfers between devices: 38.6 us -> 43.4 us
    ppermute x18 -> x25, waiting for transfers between devices: 20.6 us -> 10.7 us  [send(): return lax.ppermute(block, 'gx', [(i, target(i)) for i in range(32)])]
    ppermute x18 -> x25, starting transfers between devices: 28.9 us -> 33.7 us  [send(): return lax.ppermute(block, 'gx', [(i, target(i)) for i in range(32)])]
    pallas_call x7 -> x9, Pallas kernels: 10.3 us -> 9.26 us  [call(): pl.pallas_call(kernel, out_shape=outs, in_specs=ins, out_specs=jax.tree.m...]
    pallas_call x1 -> x2, Pallas kernels: 1.37 us -> 2.19 us  [frame(): pl.pallas_call(functools.partial(frame_kernel, places), out_shape=image(4...]
  transfers between devices with their start and end apart: 20 -> 27, of which waited for: 9 -> 8; matrix products, arithmetic and copies ran while one was open for 0% -> 0% of each run, Pallas kernels for 9% -> 10%
where the time goes in v3:
time: 67.1 us; the launch traced here: 66.6 us
  starting transfers between devices  43.4 us (65%)
  Pallas kernels  11.5 us (17%)
  waiting for transfers between devices  10.7 us (16%)
  between operations  0.99 us (1%)
    ppermute x25, starting transfers between devices, send(): return lax.ppermute(block, 'gx', [(i, target(i)) for i in range(32)])  33.7 us
    ppermute x25, waiting for transfers between devices, send(): return lax.ppermute(block, 'gx', [(i, target(i)) for i in range(32)])  10.7 us
    ppermute x2, starting transfers between devices, beside(): lax.ppermute(block, 'gy', [swap for i in range(first, 7, 2) for swap in (...  9.74 us
    pallas_call x9, Pallas kernels, call(): pl.pallas_call(kernel, out_shape=outs, in_specs=ins, out_specs=jax.tree.m...  9.26 us
    pallas_call x2, Pallas kernels, frame(): pl.pallas_call(functools.partial(frame_kernel, places), out_shape=image(4...  2.19 us
  transfers between devices with their start and end apart: 27, of which 8 were waited for; matrix products, arithmetic and copies ran while one was open for 0% of the time, Pallas kernels for 10%

profile of v3, /device:TPU:5, one launch (start us, length us, event | category | flops | bytes accessed | tf_op | source)
XLA Modules:
  0.0 66.6 jit_solution(11553284184198127229)
XLA Ops:
  0.0 3.0 %shard_map.91 = (f32[8,1040,128]{2,1,0:T(8,128)S(1)}, f32[4,8,1024]{2,1,0:T(8,128)S(1)}, f32[8,1024]{1,0:T(8,128)S(1)}, f32[8,1024]{1,0:T(8,128)S(1)}) custom-call(f32[8,1024,128]{2,1,0:T(8,128)} %tsdf.1), custom_call_target="tpu_custom_call" | custom-call | flops 1073741824 | bytes 4194304 | tf_op jit(solution)/shard_map/pallas_call | solution.py:28
  3.1 2.2 %collective-permute-start = (f32[8,1024]{1,0:T(8,128)S(1)}, f32[8,1024]{1,0:T(8,128)S(1)}, u32[]{:S(2)}, u32[]{:S(2)}) collective-permute-start(f32[8,1024]{1,0:T(8,128)S(1)} %get-tuple-element.32), channel_id=1, source_target_pairs={{1,2},{2,1},{3,4},{4,3},{5,6},{6,5},{9,10},{10,9},{11,12},{12,11},... | collective-permute-start | bytes 98312 | tf_op jit(solution)/shard_map/ppermute | solution.py:333
  5.2 7.6 %collective-permute-start.1 = (f32[8,1024]{1,0:T(8,128)S(1)}, f32[8,1024]{1,0:T(8,128)S(1)}, u32[]{:S(2)}, u32[]{:S(2)}) collective-permute-start(f32[8,1024]{1,0:T(8,128)S(1)} %get-tuple-element.33), channel_id=1, source_target_pairs={{0,1},{1,0},{2,3},{3,2},{4,5},{5,4},{6,7},{7,6},{8,9},{9,8},{10,11... | collective-permute-start | bytes 98312 | tf_op jit(solution)/shard_map/ppermute | solution.py:333
  12.9 4.5 %shard_map.92 = (f32[4,512,128]{2,1,0:T(8,128)S(1)}, f32[4,512,128]{2,1,0:T(8,128)S(1)}) custom-call(f32[8,1040,128]{2,1,0:T(8,128)S(1)} %get-tuple-element.34.cells, s32[8]{0:T(128)S(1)} %copy-done, s32[8]{0:T(128)S(1)} %copy-done.1, f32[8]{0:T(128)S(1)} %copy-done.2, f32[8]{0:T(128)S(1)} %copy-done.3, f32[8]{0:T(128)S(1)} %copy-done.4, f32[3]{0:T(128)S(1)} %copy-done.5, ...), custom_call_target="tpu_custom_call" | custom-call | flops 5368709120 | bytes 20971520 | tf_op jit(solution)/shard_map/pallas_call | solution.py:28
  17.4 1.3 %collective-permute-start.2 = (f32[4,512,128]{2,1,0:T(8,128)S(1)}, f32[4,512,128]{2,1,0:T(8,128)S(1)}, u32[]{:S(2)}, u32[]{:S(2)}) collective-permute-start(f32[4,512,128]{2,1,0:T(8,128)S(1)} %get-tuple-element.37), channel_id=1, source_target_pairs={{0,8},{8,0},{16,24},{24,16},{32,40},{40,32},{48,56},{56,48},{64,72... | collective-permute-start | bytes 3145736 | tf_op jit(solution)/shard_map/ppermute | solution.py:329
  21.7 1.4 %collective-permute-start.4 = (f32[3,4,32,128]{3,2,1,0:T(8,128)S(1)}, f32[3,4,32,128]{3,2,1,0:T(8,128)S(1)}, u32[]{:S(2)}, u32[]{:S(2)}) collective-permute-start(f32[3,4,32,128]{3,2,1,0:T(8,128)S(1)} %get-tuple-element.43), channel_id=1, source_target_pairs={{0,16},{8,24},{16,32},{24,40},{32,48},{40,56},{48,0},{56,8},{64,80... | collective-permute-start | bytes 589832 | tf_op jit(solution)/shard_map/ppermute | solution.py:329
  23.0 1.5 %collective-permute-start.8 = (f32[3,4,32,128]{3,2,1,0:T(8,128)S(1)}, f32[3,4,32,128]{3,2,1,0:T(8,128)S(1)}, u32[]{:S(2)}, u32[]{:S(2)}) collective-permute-start(f32[3,4,32,128]{3,2,1,0:T(8,128)S(1)} %get-tuple-element.54), channel_id=1, source_target_pairs={{0,48},{8,56},{16,0},{24,8},{32,16},{40,24},{48,32},{56,40},{64,11... | collective-permute-start | bytes 589832 | tf_op jit(solution)/shard_map/ppermute | solution.py:329
  24.5 1.6 %collective-permute-start.9 = (f32[3,4,32,128]{3,2,1,0:T(8,128)S(1)}, f32[3,4,32,128]{3,2,1,0:T(8,128)S(1)}, u32[]{:S(2)}, u32[]{:S(2)}) collective-permute-start(f32[3,4,32,128]{3,2,1,0:T(8,128)S(1)} %get-tuple-element.55), channel_id=1, source_target_pairs={{0,32},{8,40},{16,48},{24,56},{32,0},{40,8},{48,16},{56,24},{64,96... | collective-permute-start | bytes 589832 | tf_op jit(solution)/shard_map/ppermute | solution.py:329
  26.1 3.1 %collective-permute-done.4.refs_1_ = f32[3,4,32,128]{3,2,1,0:T(8,128)S(1)} collective-permute-done((f32[3,4,32,128]{3,2,1,0:T(8,128)S(1)}, f32[3,4,32,128]{3,2,1,0:T(8,128)S(1)}, u32[]{:S(2)}, u32[]{:S(2)}) %collective-permute-start.4) | collective-permute-done | bytes 196640 | tf_op jit(solution)/shard_map/ppermute | solution.py:329
  29.2 2.7 %collective-permute-start.6 = (f32[1,4,32,128]{3,2,1,0:T(8,128)S(1)}, f32[1,4,32,128]{3,2,1,0:T(8,128)S(1)}, u32[]{:S(2)}, u32[]{:S(2)}) collective-permute-start(f32[1,4,32,128]{3,2,1,0:T(8,128)S(1)} %get-tuple-element.50), channel_id=1, source_target_pairs={{0,48},{8,56},{16,0},{24,8},{32,16},{40,24},{48,32},{56,40},{64,11... | collective-permute-start | bytes 196616 | tf_op jit(solution)/shard_map/ppermute | solution.py:329
  32.3 2.2 %collective-permute-done.9.refs_3_ = f32[3,4,32,128]{3,2,1,0:T(8,128)S(1)} collective-permute-done((f32[3,4,32,128]{3,2,1,0:T(8,128)S(1)}, f32[3,4,32,128]{3,2,1,0:T(8,128)S(1)}, u32[]{:S(2)}, u32[]{:S(2)}) %collective-permute-start.9) | collective-permute-done | bytes 196640 | tf_op jit(solution)/shard_map/ppermute | solution.py:329
  34.6 1.3 %collective-permute-start.10 = (f32[4,32,128]{2,1,0:T(8,128)S(1)}, f32[4,32,128]{2,1,0:T(8,128)S(1)}, u32[]{:S(2)}, u32[]{:S(2)}) collective-permute-start(f32[4,32,128]{2,1,0:T(8,128)S(1)} %get-tuple-element.56), channel_id=1, source_target_pairs={{0,128},{8,136},{16,144},{24,152},{32,160},{40,168},{48,176},{56,1... | collective-permute-start | bytes 196616 | tf_op jit(solution)/shard_map/ppermute | solution.py:329
  35.9 1.6 %collective-permute-start.11 = (f32[4,32,128]{2,1,0:T(8,128)S(1)}, f32[4,32,128]{2,1,0:T(8,128)S(1)}, u32[]{:S(2)}, u32[]{:S(2)}) collective-permute-start(f32[4,32,128]{2,1,0:T(8,128)S(1)} %get-tuple-element.57), channel_id=1, source_target_pairs={{0,192},{8,200},{16,208},{24,216},{32,224},{40,232},{48,240},{56,2... | collective-permute-start | bytes 196616 | tf_op jit(solution)/shard_map/ppermute | solution.py:329
  37.9 1.5 %collective-permute-done.10.refs_1_ = f32[4,32,128]{2,1,0:T(8,128)S(1)} collective-permute-done((f32[4,32,128]{2,1,0:T(8,128)S(1)}, f32[4,32,128]{2,1,0:T(8,128)S(1)}, u32[]{:S(2)}, u32[]{:S(2)}) %collective-permute-start.10) | collective-permute-done | bytes 65568 | tf_op jit(solution)/shard_map/ppermute | solution.py:329
  39.4 1.5 %collective-permute-done.11.refs_2_ = f32[4,32,128]{2,1,0:T(8,128)S(1)} collective-permute-done((f32[4,32,128]{2,1,0:T(8,128)S(1)}, f32[4,32,128]{2,1,0:T(8,128)S(1)}, u32[]{:S(2)}, u32[]{:S(2)}) %collective-permute-start.11) | collective-permute-done | bytes 65568 | tf_op jit(solution)/shard_map/ppermute | solution.py:329
  41.0 1.1 %collective-permute-done.12.refs_3_ = f32[4,32,128]{2,1,0:T(8,128)S(1)} collective-permute-done((f32[4,32,128]{2,1,0:T(8,128)S(1)}, f32[4,32,128]{2,1,0:T(8,128)S(1)}, u32[]{:S(2)}, u32[]{:S(2)}) %collective-permute-start.12) | collective-permute-done | bytes 65568 | tf_op jit(solution)/shard_map/ppermute | solution.py:329
  45.6 2.0 %collective-permute-start.23 = (f32[4,32,128]{2,1,0:T(8,128)S(1)}, f32[4,32,128]{2,1,0:T(8,128)S(1)}, u32[]{:S(2)}, u32[]{:S(2)}) collective-permute-start(f32[4,32,128]{2,1,0:T(8,128)S(1)} %shard_map.97.refs_0_), channel_id=1, source_target_pairs={{0,48},{8,56},{16,0},{24,8},{32,16},{40,24},{48,32},{56,40},{64,11... | collective-permute-start | bytes 196616 | tf_op jit(solution)/shard_map/ppermute | solution.py:329
  48.5 2.2 %collective-permute-start.18 = (f32[3,4,32,128]{3,2,1,0:T(8,128)S(1)}, f32[3,4,32,128]{3,2,1,0:T(8,128)S(1)}, u32[]{:S(2)}, u32[]{:S(2)}) collective-permute-start(f32[3,4,32,128]{3,2,1,0:T(8,128)S(1)} %shard_map.98.refs_1_), channel_id=1, source_target_pairs={{0,48},{8,56},{16,0},{24,8},{32,16},{40,24},{48,32},{56,40},{64,11... | collective-permute-start | bytes 589832 | tf_op jit(solution)/shard_map/ppermute | solution.py:329
  50.8 1.4 %collective-permute-start.20 = (f32[3,4,32,128]{3,2,1,0:T(8,128)S(1)}, f32[3,4,32,128]{3,2,1,0:T(8,128)S(1)}, u32[]{:S(2)}, u32[]{:S(2)}) collective-permute-start(f32[3,4,32,128]{3,2,1,0:T(8,128)S(1)} %shard_map.98.refs_1_), channel_id=1, source_target_pairs={{0,32},{8,40},{16,48},{24,56},{32,0},{40,8},{48,16},{56,24},{64,96... | collective-permute-start | bytes 589832 | tf_op jit(solution)/shard_map/ppermute | solution.py:329
  52.3 6.3 %collective-permute-start.25 = (f32[4,4,32,128]{3,2,1,0:T(8,128)S(1)}, f32[4,4,32,128]{3,2,1,0:T(8,128)S(1)}, u32[]{:S(2)}, u32[]{:S(2)}) collective-permute-start(f32[4,4,32,128]{3,2,1,0:T(8,128)S(1)} %shard_map.99.refs_0_), channel_id=1, source_target_pairs={{0,8},{8,0},{16,24},{24,16},{32,40},{40,32},{48,56},{56,48},{64,72... | collective-permute-start | bytes 786440 | tf_op jit(solution)/shard_map/ppermute | solution.py:329
  58.7 1.9 %collective-permute-start.17 = (f32[3,4,32,128]{3,2,1,0:T(8,128)S(1)}, f32[3,4,32,128]{3,2,1,0:T(8,128)S(1)}, u32[]{:S(2)}, u32[]{:S(2)}) collective-permute-start(f32[3,4,32,128]{3,2,1,0:T(8,128)S(1)} %collective-permute-done.16.refs_2_), channel_id=1, source_target_pairs={{0,8},{8,0},{16,24},{24,16},{32,40},{40,32},{48,56},{56,48},{64,72... | collective-permute-start | bytes 589832 | tf_op jit(solution)/shard_map/ppermute | solution.py:329
  60.7 1.6 %collective-permute-start.19 = (f32[3,4,32,128]{3,2,1,0:T(8,128)S(1)}, f32[3,4,32,128]{3,2,1,0:T(8,128)S(1)}, u32[]{:S(2)}, u32[]{:S(2)}) collective-permute-start(f32[3,4,32,128]{3,2,1,0:T(8,128)S(1)} %collective-permute-done.18.refs_3_), channel_id=1, source_target_pairs={{0,8},{8,0},{16,24},{24,16},{32,40},{40,32},{48,56},{56,48},{64,72... | collective-permute-start | bytes 589832 | tf_op jit(solution)/shard_map/ppermute | solution.py:329
  62.3 1.9 %collective-permute-start.21 = (f32[3,4,32,128]{3,2,1,0:T(8,128)S(1)}, f32[3,4,32,128]{3,2,1,0:T(8,128)S(1)}, u32[]{:S(2)}, u32[]{:S(2)}) collective-permute-start(f32[3,4,32,128]{3,2,1,0:T(8,128)S(1)} %collective-permute-done.20.refs_4_), channel_id=1, source_target_pairs={{0,8},{8,0},{16,24},{24,16},{32,40},{40,32},{48,56},{56,48},{64,72... | collective-permute-start | bytes 589832 | tf_op jit(solution)/shard_map/ppermute | solution.py:329
  64.2 1.3 %shard_map.100.refs_3_ = f32[4,1024,128]{2,1,0:T(8,128)} custom-call(f32[4,4,32,128]{3,2,1,0:T(8,128)S(1)} %shard_map.99.refs_0_, f32[3,4,32,128]{3,2,1,0:T(8,128)S(1)} %shard_map.98.refs_1_, f32[3,4,32,128]{3,2,1,0:T(8,128)S(1)} %collective-permute-done.16.refs_2_, f32[3,4,32,128]{3,2,1,0:T(8,128)S(1)} %collective-permute-done.18.refs_3_, ...), custom_call_target="tpu_custom_call" | custom-call | tf_op jit(solution)/shard_map/pallas_call | solution.py:317
  (55 shorter events, 8.8 us)
Async XLA Ops:
  3.1 15.7 %collective-permute-start = (f32[8,1024]{1,0:T(8,128)S(1)}, f32[8,1024]{1,0:T(8,128)S(1)}, u32[]{:S(2)}, u32[]{:S(2)}) collective-permute-start(f32[8,1024]{1,0:T(8,128)S(1)} %get-tuple-element.32), channel_id=1, source_target_pairs={{1,2},{2,1},{3,4},{4,3},{5,6},{6,5},{9,10},{10,9},{11,12},{12,11},... | collective-permute-start | bytes 98312 | tf_op jit(solution)/shard_map/ppermute | solution.py:333
  5.2 13.5 %collective-permute-start.1 = (f32[8,1024]{1,0:T(8,128)S(1)}, f32[8,1024]{1,0:T(8,128)S(1)}, u32[]{:S(2)}, u32[]{:S(2)}) collective-permute-start(f32[8,1024]{1,0:T(8,128)S(1)} %get-tuple-element.33), channel_id=1, source_target_pairs={{0,1},{1,0},{2,3},{3,2},{4,5},{5,4},{6,7},{7,6},{8,9},{9,8},{10,11... | collective-permute-start | bytes 98312 | tf_op jit(solution)/shard_map/ppermute | solution.py:333
  21.7 7.5 %collective-permute-start.4 = (f32[3,4,32,128]{3,2,1,0:T(8,128)S(1)}, f32[3,4,32,128]{3,2,1,0:T(8,128)S(1)}, u32[]{:S(2)}, u32[]{:S(2)}) collective-permute-start(f32[3,4,32,128]{3,2,1,0:T(8,128)S(1)} %get-tuple-element.43), channel_id=1, source_target_pairs={{0,16},{8,24},{16,32},{24,40},{32,48},{40,56},{48,0},{56,8},{64,80... | collective-permute-start | bytes 589832 | tf_op jit(solution)/shard_map/ppermute | solution.py:329
  23.0 9.3 %collective-permute-start.8 = (f32[3,4,32,128]{3,2,1,0:T(8,128)S(1)}, f32[3,4,32,128]{3,2,1,0:T(8,128)S(1)}, u32[]{:S(2)}, u32[]{:S(2)}) collective-permute-start(f32[3,4,32,128]{3,2,1,0:T(8,128)S(1)} %get-tuple-element.54), channel_id=1, source_target_pairs={{0,48},{8,56},{16,0},{24,8},{32,16},{40,24},{48,32},{56,40},{64,11... | collective-permute-start | bytes 589832 | tf_op jit(solution)/shard_map/ppermute | solution.py:329
  24.5 10.0 %collective-permute-start.9 = (f32[3,4,32,128]{3,2,1,0:T(8,128)S(1)}, f32[3,4,32,128]{3,2,1,0:T(8,128)S(1)}, u32[]{:S(2)}, u32[]{:S(2)}) collective-permute-start(f32[3,4,32,128]{3,2,1,0:T(8,128)S(1)} %get-tuple-element.55), channel_id=1, source_target_pairs={{0,32},{8,40},{16,48},{24,56},{32,0},{40,8},{48,16},{56,24},{64,96... | collective-permute-start | bytes 589832 | tf_op jit(solution)/shard_map/ppermute | solution.py:329
  29.2 8.4 %collective-permute-start.5 = (f32[1,4,32,128]{3,2,1,0:T(8,128)S(1)}, f32[1,4,32,128]{3,2,1,0:T(8,128)S(1)}, u32[]{:S(2)}, u32[]{:S(2)}) collective-permute-start(f32[1,4,32,128]{3,2,1,0:T(8,128)S(1)} %get-tuple-element.49), channel_id=1, source_target_pairs={{0,16},{8,24},{16,32},{24,40},{32,48},{40,56},{48,0},{56,8},{64,80... | collective-permute-start | bytes 196616 | tf_op jit(solution)/shard_map/ppermute | solution.py:329
  29.2 8.7 %collective-permute-start.6 = (f32[1,4,32,128]{3,2,1,0:T(8,128)S(1)}, f32[1,4,32,128]{3,2,1,0:T(8,128)S(1)}, u32[]{:S(2)}, u32[]{:S(2)}) collective-permute-start(f32[1,4,32,128]{3,2,1,0:T(8,128)S(1)} %get-tuple-element.50), channel_id=1, source_target_pairs={{0,48},{8,56},{16,0},{24,8},{32,16},{40,24},{48,32},{56,40},{64,11... | collective-permute-start | bytes 196616 | tf_op jit(solution)/shard_map/ppermute | solution.py:329
  31.8 6.0 %collective-permute-start.7 = (f32[1,4,32,128]{3,2,1,0:T(8,128)S(1)}, f32[1,4,32,128]{3,2,1,0:T(8,128)S(1)}, u32[]{:S(2)}, u32[]{:S(2)}) collective-permute-start(f32[1,4,32,128]{3,2,1,0:T(8,128)S(1)} %get-tuple-element.51), channel_id=1, source_target_pairs={{0,32},{8,40},{16,48},{24,56},{32,0},{40,8},{48,16},{56,24},{64,96... | collective-permute-start | bytes 196616 | tf_op jit(solution)/shard_map/ppermute | solution.py:329
  34.6 4.8 %collective-permute-start.10 = (f32[4,32,128]{2,1,0:T(8,128)S(1)}, f32[4,32,128]{2,1,0:T(8,128)S(1)}, u32[]{:S(2)}, u32[]{:S(2)}) collective-permute-start(f32[4,32,128]{2,1,0:T(8,128)S(1)} %get-tuple-element.56), channel_id=1, source_target_pairs={{0,128},{8,136},{16,144},{24,152},{32,160},{40,168},{48,176},{56,1... | collective-permute-start | bytes 196616 | tf_op jit(solution)/shard_map/ppermute | solution.py:329
  35.9 5.1 %collective-permute-start.11 = (f32[4,32,128]{2,1,0:T(8,128)S(1)}, f32[4,32,128]{2,1,0:T(8,128)S(1)}, u32[]{:S(2)}, u32[]{:S(2)}) collective-permute-start(f32[4,32,128]{2,1,0:T(8,128)S(1)} %get-tuple-element.57), channel_id=1, source_target_pairs={{0,192},{8,200},{16,208},{24,216},{32,224},{40,232},{48,240},{56,2... | collective-permute-start | bytes 196616 | tf_op jit(solution)/shard_map/ppermute | solution.py:329
  37.5 4.6 %collective-permute-start.12 = (f32[4,32,128]{2,1,0:T(8,128)S(1)}, f32[4,32,128]{2,1,0:T(8,128)S(1)}, u32[]{:S(2)}, u32[]{:S(2)}) collective-permute-start(f32[4,32,128]{2,1,0:T(8,128)S(1)} %get-tuple-element.58), channel_id=1, source_target_pairs={{0,64},{8,72},{16,80},{24,88},{32,96},{40,104},{48,112},{56,120},{... | collective-permute-start | bytes 196616 | tf_op jit(solution)/shard_map/ppermute | solution.py:329
  42.2 5.4 %collective-permute-start.13 = (f32[4,32,128]{2,1,0:T(8,128)S(1)}, f32[4,32,128]{2,1,0:T(8,128)S(1)}, u32[]{:S(2)}, u32[]{:S(2)}) collective-permute-start(f32[4,32,128]{2,1,0:T(8,128)S(1)} %shard_map.97.refs_0_), channel_id=1, source_target_pairs={{0,128},{8,136},{16,144},{24,152},{32,160},{40,168},{48,176},{56,1... | collective-permute-start | bytes 196616 | tf_op jit(solution)/shard_map/ppermute | solution.py:329
  43.0 5.0 %collective-permute-start.14 = (f32[4,32,128]{2,1,0:T(8,128)S(1)}, f32[4,32,128]{2,1,0:T(8,128)S(1)}, u32[]{:S(2)}, u32[]{:S(2)}) collective-permute-start(f32[4,32,128]{2,1,0:T(8,128)S(1)} %shard_map.97.refs_0_), channel_id=1, source_target_pairs={{0,192},{8,200},{16,208},{24,216},{32,224},{40,232},{48,240},{56,2... | collective-permute-start | bytes 196616 | tf_op jit(solution)/shard_map/ppermute | solution.py:329
  44.0 4.0 %collective-permute-start.15 = (f32[4,32,128]{2,1,0:T(8,128)S(1)}, f32[4,32,128]{2,1,0:T(8,128)S(1)}, u32[]{:S(2)}, u32[]{:S(2)}) collective-permute-start(f32[4,32,128]{2,1,0:T(8,128)S(1)} %shard_map.97.refs_0_), channel_id=1, source_target_pairs={{0,64},{8,72},{16,80},{24,88},{32,96},{40,104},{48,112},{56,120},{... | collective-permute-start | bytes 196616 | tf_op jit(solution)/shard_map/ppermute | solution.py:329
  44.9 5.9 %collective-permute-start.22 = (f32[4,32,128]{2,1,0:T(8,128)S(1)}, f32[4,32,128]{2,1,0:T(8,128)S(1)}, u32[]{:S(2)}, u32[]{:S(2)}) collective-permute-start(f32[4,32,128]{2,1,0:T(8,128)S(1)} %shard_map.97.refs_0_), channel_id=1, source_target_pairs={{0,16},{8,24},{16,32},{24,40},{32,48},{40,56},{48,0},{56,8},{64,80... | collective-permute-start | bytes 196616 | tf_op jit(solution)/shard_map/ppermute | solution.py:329
  45.6 6.6 %collective-permute-start.23 = (f32[4,32,128]{2,1,0:T(8,128)S(1)}, f32[4,32,128]{2,1,0:T(8,128)S(1)}, u32[]{:S(2)}, u32[]{:S(2)}) collective-permute-start(f32[4,32,128]{2,1,0:T(8,128)S(1)} %shard_map.97.refs_0_), channel_id=1, source_target_pairs={{0,48},{8,56},{16,0},{24,8},{32,16},{40,24},{48,32},{56,40},{64,11... | collective-permute-start | bytes 196616 | tf_op jit(solution)/shard_map/ppermute | solution.py:329
  47.6 4.7 %collective-permute-start.24 = (f32[4,32,128]{2,1,0:T(8,128)S(1)}, f32[4,32,128]{2,1,0:T(8,128)S(1)}, u32[]{:S(2)}, u32[]{:S(2)}) collective-permute-start(f32[4,32,128]{2,1,0:T(8,128)S(1)} %shard_map.97.refs_0_), channel_id=1, source_target_pairs={{0,32},{8,40},{16,48},{24,56},{32,0},{40,8},{48,16},{56,24},{64,96... | collective-permute-start | bytes 196616 | tf_op jit(solution)/shard_map/ppermute | solution.py:329
  48.0 10.7 %collective-permute-start.16 = (f32[3,4,32,128]{3,2,1,0:T(8,128)S(1)}, f32[3,4,32,128]{3,2,1,0:T(8,128)S(1)}, u32[]{:S(2)}, u32[]{:S(2)}) collective-permute-start(f32[3,4,32,128]{3,2,1,0:T(8,128)S(1)} %shard_map.98.refs_1_), channel_id=1, source_target_pairs={{0,16},{8,24},{16,32},{24,40},{32,48},{40,56},{48,0},{56,8},{64,80... | collective-permute-start | bytes 589832 | tf_op jit(solution)/shard_map/ppermute | solution.py:329
  48.5 12.1 %collective-permute-start.18 = (f32[3,4,32,128]{3,2,1,0:T(8,128)S(1)}, f32[3,4,32,128]{3,2,1,0:T(8,128)S(1)}, u32[]{:S(2)}, u32[]{:S(2)}) collective-permute-start(f32[3,4,32,128]{3,2,1,0:T(8,128)S(1)} %shard_map.98.refs_1_), channel_id=1, source_target_pairs={{0,48},{8,56},{16,0},{24,8},{32,16},{40,24},{48,32},{56,40},{64,11... | collective-permute-start | bytes 589832 | tf_op jit(solution)/shard_map/ppermute | solution.py:329
  50.8 11.6 %collective-permute-start.20 = (f32[3,4,32,128]{3,2,1,0:T(8,128)S(1)}, f32[3,4,32,128]{3,2,1,0:T(8,128)S(1)}, u32[]{:S(2)}, u32[]{:S(2)}) collective-permute-start(f32[3,4,32,128]{3,2,1,0:T(8,128)S(1)} %shard_map.98.refs_1_), channel_id=1, source_target_pairs={{0,32},{8,40},{16,48},{24,56},{32,0},{40,8},{48,16},{56,24},{64,96... | collective-permute-start | bytes 589832 | tf_op jit(solution)/shard_map/ppermute | solution.py:329
  52.3 11.9 %collective-permute-start.25 = (f32[4,4,32,128]{3,2,1,0:T(8,128)S(1)}, f32[4,4,32,128]{3,2,1,0:T(8,128)S(1)}, u32[]{:S(2)}, u32[]{:S(2)}) collective-permute-start(f32[4,4,32,128]{3,2,1,0:T(8,128)S(1)} %shard_map.99.refs_0_), channel_id=1, source_target_pairs={{0,8},{8,0},{16,24},{24,16},{32,40},{40,32},{48,56},{56,48},{64,72... | collective-permute-start | bytes 786440 | tf_op jit(solution)/shard_map/ppermute | solution.py:329
  58.6 5.6 %collective-permute-start.26 = (f32[3,4,32,128]{3,2,1,0:T(8,128)S(1)}, f32[3,4,32,128]{3,2,1,0:T(8,128)S(1)}, u32[]{:S(2)}, u32[]{:S(2)}) collective-permute-start(f32[3,4,32,128]{3,2,1,0:T(8,128)S(1)} %shard_map.98.refs_1_), channel_id=1, source_target_pairs={{0,8},{8,0},{16,24},{24,16},{32,40},{40,32},{48,56},{56,48},{64,72... | collective-permute-start | bytes 589832 | tf_op jit(solution)/shard_map/ppermute | solution.py:329
  58.7 6.8 %collective-permute-start.17 = (f32[3,4,32,128]{3,2,1,0:T(8,128)S(1)}, f32[3,4,32,128]{3,2,1,0:T(8,128)S(1)}, u32[]{:S(2)}, u32[]{:S(2)}) collective-permute-start(f32[3,4,32,128]{3,2,1,0:T(8,128)S(1)} %collective-permute-done.16.refs_2_), channel_id=1, source_target_pairs={{0,8},{8,0},{16,24},{24,16},{32,40},{40,32},{48,56},{56,48},{64,72... | collective-permute-start | bytes 589832 | tf_op jit(solution)/shard_map/ppermute | solution.py:329
  60.7 4.9 %collective-permute-start.19 = (f32[3,4,32,128]{3,2,1,0:T(8,128)S(1)}, f32[3,4,32,128]{3,2,1,0:T(8,128)S(1)}, u32[]{:S(2)}, u32[]{:S(2)}) collective-permute-start(f32[3,4,32,128]{3,2,1,0:T(8,128)S(1)} %collective-permute-done.18.refs_3_), channel_id=1, source_target_pairs={{0,8},{8,0},{16,24},{24,16},{32,40},{40,32},{48,56},{56,48},{64,72... | collective-permute-start | bytes 589832 | tf_op jit(solution)/shard_map/ppermute | solution.py:329
  (10 other events, 98.0 us)

commit v4 on v3

--- a/solution.py
+++ b/solution.py
@@ -12,6 +12,8 @@
 SLICES, ROWS, COLS = 8, 1024, 128
 HALF, QUARTER, TILE = 512, 128, 32
 STEP = 512
+COST_A = 1 << 16
+COST_B = 1 << 16
 AWAY = (0, 1, 3, 2)
 CHUNK = 256
 AHEAD = 4
@@ -211,10 +213,10 @@
             near, far_side = merged[c : c + 1, r : r + QUARTER], merged[4 + c : 5 + c, r : r + QUARTER]
             side[c, r : r + QUARTER, :] = jnp.transpose(jnp.where(line == 0, near, far_side))
     outer = outer[:TILE]
-    for away, rest, single in zip(AWAY, dests[:4], dests[4:]):
+    for away, early, late in zip(AWAY, dests[:4], dests[4:]):
         for bits in range(4):
             rows = pl.ds(pl.multiple_of((y + away & 3) * QUARTER + (z ^ bits) * TILE, TILE), TILE)
-            dest = rest.at[bits - 1] if bits else single.at[0]
+            dest = (early if bits > 1 else late).at[bits & 1]
 
             def run(dest, rows, first, second):
                 done = over([first[c, rows, :] for c in range(4)], [second[c, rows, :] for c in range(4)])
@@ -228,7 +230,7 @@
 def pair(mask, own, other, own_border, other_border):
     return call(
         pair_kernel,
-        [image(3, 4, TILE, COLS)] * 4 + [image(1, 4, TILE, COLS)] * 4,
+        [image(2, 4, TILE, COLS)] * 8,
         [SMEM] + [VMEM] * 4,
         (mask, own, other, own_border, other_border),
         [pltpu.VMEM((4, HALF, COLS), F32)],
@@ -284,12 +286,19 @@
 
 
 def join_kernel(*refs):
-    for n, part in enumerate(refs[:-1]):
-        refs[-1][n] = part[...]
+    begin = 0
+    for part in refs[:-1]:
+        if len(part.shape) == 3:
+            refs[-1][begin] = part[...]
+            begin += 1
+        else:
+            refs[-1][begin : begin + part.shape[0]] = part[...]
+            begin += part.shape[0]
 
 
 def join(*parts):
-    return call(join_kernel, image(len(parts), 4, TILE, COLS), [VMEM] * len(parts), parts, cost=256 << 20)
+    count = sum(part.shape[0] if part.ndim == 4 else 1 for part in parts)
+    return call(join_kernel, image(count, 4, TILE, COLS), [VMEM] * len(parts), parts, cost=256 << 20)
 
 
 def frame_kernel(places, *refs):
@@ -303,9 +312,9 @@
         copies.append(pltpu.make_async_copy(source, out.at[:, rows, :], sems.at[len(copies)]))
 
     copies = []
-    for part, (side, n) in zip(parts, places):
+    for part, (side, upper, n) in zip(parts, places):
         for m in range(part.shape[0]):
-            put(part.at[m], side, *((m, 0) if n is None else (n, (2, 3, 1)[m])))
+            put(part.at[m], side, n, upper + m)
     for copy in copies:
         copy.start()
     for copy in copies:
@@ -341,11 +350,6 @@
     return lambda i: i & ~6 | ((i >> 1) + step & 3) << 1
 
 
-def along_z(one, two, three):
-    two, three, one = send(two, flip(16)), send(three, flip(24)), send(one, flip(8))
-    return two, three, one
-
-
 def to_quarters(plus, minus, far):
     return send(plus, along_y(1)), send(minus, along_y(3)), send(far, along_y(2))
 
@@ -361,20 +365,19 @@
     own_border, given_border = border(columns, by_odd, by_even, scalars)
     other_border = send(given_border, flip(1))
     pieces = pair(view_mask, own, other, own_border, other_border)
-    rests, singles = pieces[:4], pieces[4:]
-    came = to_quarters(*rests[1:])
-    came_first, *singles = lax.optimization_barrier((came[0], *singles))
-    one, two, three = quarter(view_mask, (rests[0], came_first, *came[1:]), 1 << 20)
-    over_z = along_z(one, two, three)
-    (mine,) = quarter(view_mask, (singles[0], *to_quarters(*singles[1:])), 256 << 20)
-    mine = tile(view_mask, (mine, *over_z))
-    rest = join(*along_z(mine, mine, mine))
-    singles = join(mine, *to_quarters(mine, mine, mine))
-    blocks = (singles, rest, *to_quarters(rest, rest, rest))
+    early, late = pieces[:4], pieces[4:]
+    two, three = quarter(view_mask, (early[0], *to_quarters(*early[1:])), COST_A)
+    two, three = send(two, flip(16)), send(three, flip(24))
+    mine, one = quarter(view_mask, (late[0], *to_quarters(*late[1:])), COST_B)
+    one = send(one, flip(8))
+    mine = tile(view_mask, (mine, two, three, one))
+    near = join(mine, send(mine, flip(8)))
+    far = join(send(mine, flip(16)), send(mine, flip(24)))
+    blocks = (near, *to_quarters(near, near, near), far, *to_quarters(far, far, far))
     others = tuple(send(block, flip(1)) for block in blocks)
-    places = [(side, n) for side in range(2) for n in (None, 0, 1, 2, 3)]
-    begun = frame(places[:7], blocks + others[:2])
-    return frame(places[7:], others[2:], (begun,))
+    places = [(side, upper, n) for side in range(2) for upper in (0, 2) for n in range(4)]
+    begun = frame(places[:13], blocks + others[:5])
+    return frame(places[13:], others[5:], (begun,))
 
 
 def solution(mesh):

time: 67.1 us -> 66 us (0.984)
  starting transfers between devices: 43.4 us -> 41.7 us
  waiting for transfers between devices: 10.7 us -> 11.7 us
    ppermute x25 -> x28, starting transfers between devices: 33.7 us -> 32 us  [send(): return lax.ppermute(block, 'gx', [(i, target(i)) for i in range(32)])]
    ppermute x25 -> x28, waiting for transfers between devices: 10.7 us -> 11.7 us  [send(): return lax.ppermute(block, 'gx', [(i, target(i)) for i in range(32)])]
  transfers between devices with their start and end apart: 27 -> 30, of which waited for: 8 -> 7; matrix products, arithmetic and copies ran while one was open for 0% -> 0% of each run, Pallas kernels for 10% -> 11%
where the time goes in v4:
time: 66 us; the launch traced here: 65.9 us
  starting transfers between devices  41.7 us (63%)
  waiting for transfers between devices  11.7 us (18%)
  Pallas kernels  11.4 us (17%)
  between operations  1 us (2%)
    ppermute x28, starting transfers between devices, send(): return lax.ppermute(block, 'gx', [(i, target(i)) for i in range(32)])  32 us
    ppermute x28, waiting for transfers between devices, send(): return lax.ppermute(block, 'gx', [(i, target(i)) for i in range(32)])  11.7 us
    ppermute x2, starting transfers between devices, beside(): lax.ppermute(block, 'gy', [swap for i in range(first, 7, 2) for swap in (...  9.74 us
    pallas_call x9, Pallas kernels, call(): pl.pallas_call(kernel, out_shape=outs, in_specs=ins, out_specs=jax.tree.m...  9.24 us
    pallas_call x2, Pallas kernels, frame(): pl.pallas_call(functools.partial(frame_kernel, places), out_shape=image(4...  2.19 us
  transfers between devices with their start and end apart: 30, of which 7 were waited for; matrix products, arithmetic and copies ran while one was open for 0% of the time, Pallas kernels for 11%

profile of v4, /device:TPU:5, one launch (start us, length us, event | category | flops | bytes accessed | tf_op | source)
XLA Modules:
  0.0 65.9 jit_solution(7246638053425507601)
XLA Ops:
  0.0 3.0 %shard_map.91 = (f32[8,1040,128]{2,1,0:T(8,128)S(1)}, f32[4,8,1024]{2,1,0:T(8,128)S(1)}, f32[8,1024]{1,0:T(8,128)S(1)}, f32[8,1024]{1,0:T(8,128)S(1)}) custom-call(f32[8,1024,128]{2,1,0:T(8,128)} %tsdf.1), custom_call_target="tpu_custom_call" | custom-call | flops 1073741824 | bytes 4194304 | tf_op jit(solution)/shard_map/pallas_call | solution.py:30
  3.1 2.2 %collective-permute-start = (f32[8,1024]{1,0:T(8,128)S(1)}, f32[8,1024]{1,0:T(8,128)S(1)}, u32[]{:S(2)}, u32[]{:S(2)}) collective-permute-start(f32[8,1024]{1,0:T(8,128)S(1)} %get-tuple-element.28), channel_id=1, source_target_pairs={{1,2},{2,1},{3,4},{4,3},{5,6},{6,5},{9,10},{10,9},{11,12},{12,11},... | collective-permute-start | bytes 98312 | tf_op jit(solution)/shard_map/ppermute | solution.py:342
  5.2 7.6 %collective-permute-start.1 = (f32[8,1024]{1,0:T(8,128)S(1)}, f32[8,1024]{1,0:T(8,128)S(1)}, u32[]{:S(2)}, u32[]{:S(2)}) collective-permute-start(f32[8,1024]{1,0:T(8,128)S(1)} %get-tuple-element.29), channel_id=1, source_target_pairs={{0,1},{1,0},{2,3},{3,2},{4,5},{5,4},{6,7},{7,6},{8,9},{9,8},{10,11... | collective-permute-start | bytes 98312 | tf_op jit(solution)/shard_map/ppermute | solution.py:342
  12.9 4.5 %shard_map.92 = (f32[4,512,128]{2,1,0:T(8,128)S(1)}, f32[4,512,128]{2,1,0:T(8,128)S(1)}) custom-call(f32[8,1040,128]{2,1,0:T(8,128)S(1)} %get-tuple-element.30.cells, s32[8]{0:T(128)S(1)} %copy-done, s32[8]{0:T(128)S(1)} %copy-done.1, f32[8]{0:T(128)S(1)} %copy-done.2, f32[8]{0:T(128)S(1)} %copy-done.3, f32[8]{0:T(128)S(1)} %copy-done.4, f32[3]{0:T(128)S(1)} %copy-done.5, ...), custom_call_target="tpu_custom_call" | custom-call | flops 5368709120 | bytes 20971520 | tf_op jit(solution)/shard_map/pallas_call | solution.py:30
  17.4 1.3 %collective-permute-start.2 = (f32[4,512,128]{2,1,0:T(8,128)S(1)}, f32[4,512,128]{2,1,0:T(8,128)S(1)}, u32[]{:S(2)}, u32[]{:S(2)}) collective-permute-start(f32[4,512,128]{2,1,0:T(8,128)S(1)} %get-tuple-element.33), channel_id=1, source_target_pairs={{0,8},{8,0},{16,24},{24,16},{32,40},{40,32},{48,56},{56,48},{64,72... | collective-permute-start | bytes 3145736 | tf_op jit(solution)/shard_map/ppermute | solution.py:338
  21.6 1.4 %collective-permute-start.7 = (f32[2,4,32,128]{3,2,1,0:T(8,128)S(1)}, f32[2,4,32,128]{3,2,1,0:T(8,128)S(1)}, u32[]{:S(2)}, u32[]{:S(2)}) collective-permute-start(f32[2,4,32,128]{3,2,1,0:T(8,128)S(1)} %get-tuple-element.45), channel_id=1, source_target_pairs={{0,16},{8,24},{16,32},{24,40},{32,48},{40,56},{48,0},{56,8},{64,80... | collective-permute-start | bytes 393224 | tf_op jit(solution)/shard_map/ppermute | solution.py:338
  23.0 1.5 %collective-permute-start.8 = (f32[2,4,32,128]{3,2,1,0:T(8,128)S(1)}, f32[2,4,32,128]{3,2,1,0:T(8,128)S(1)}, u32[]{:S(2)}, u32[]{:S(2)}) collective-permute-start(f32[2,4,32,128]{3,2,1,0:T(8,128)S(1)} %get-tuple-element.46), channel_id=1, source_target_pairs={{0,48},{8,56},{16,0},{24,8},{32,16},{40,24},{48,32},{56,40},{64,11... | collective-permute-start | bytes 393224 | tf_op jit(solution)/shard_map/ppermute | solution.py:338
  24.5 1.6 %collective-permute-start.9 = (f32[2,4,32,128]{3,2,1,0:T(8,128)S(1)}, f32[2,4,32,128]{3,2,1,0:T(8,128)S(1)}, u32[]{:S(2)}, u32[]{:S(2)}) collective-permute-start(f32[2,4,32,128]{3,2,1,0:T(8,128)S(1)} %get-tuple-element.47), channel_id=1, source_target_pairs={{0,32},{8,40},{16,48},{24,56},{32,0},{40,8},{48,16},{56,24},{64,96... | collective-permute-start | bytes 393224 | tf_op jit(solution)/shard_map/ppermute | solution.py:338
  26.5 2.3 %collective-permute-start.5 = (f32[2,4,32,128]{3,2,1,0:T(8,128)S(1)}, f32[2,4,32,128]{3,2,1,0:T(8,128)S(1)}, u32[]{:S(2)}, u32[]{:S(2)}) collective-permute-start(f32[2,4,32,128]{3,2,1,0:T(8,128)S(1)} %get-tuple-element.41), channel_id=1, source_target_pairs={{0,48},{8,56},{16,0},{24,8},{32,16},{40,24},{48,32},{56,40},{64,11... | collective-permute-start | bytes 393224 | tf_op jit(solution)/shard_map/ppermute | solution.py:338
  29.4 2.4 %collective-permute-done.9.refs_3_ = f32[2,4,32,128]{3,2,1,0:T(8,128)S(1)} collective-permute-done((f32[2,4,32,128]{3,2,1,0:T(8,128)S(1)}, f32[2,4,32,128]{3,2,1,0:T(8,128)S(1)}, u32[]{:S(2)}, u32[]{:S(2)}) %collective-permute-start.9) | collective-permute-done | bytes 131104 | tf_op jit(solution)/shard_map/ppermute | solution.py:338
  31.8 1.3 %collective-permute-start.10 = (f32[4,32,128]{2,1,0:T(8,128)S(1)}, f32[4,32,128]{2,1,0:T(8,128)S(1)}, u32[]{:S(2)}, u32[]{:S(2)}) collective-permute-start(f32[4,32,128]{2,1,0:T(8,128)S(1)} %get-tuple-element.48), channel_id=1, source_target_pairs={{0,128},{8,136},{16,144},{24,152},{32,160},{40,168},{48,176},{56,1... | collective-permute-start | bytes 196616 | tf_op jit(solution)/shard_map/ppermute | solution.py:338
  33.1 1.6 %collective-permute-start.11 = (f32[4,32,128]{2,1,0:T(8,128)S(1)}, f32[4,32,128]{2,1,0:T(8,128)S(1)}, u32[]{:S(2)}, u32[]{:S(2)}) collective-permute-start(f32[4,32,128]{2,1,0:T(8,128)S(1)} %get-tuple-element.49), channel_id=1, source_target_pairs={{0,192},{8,200},{16,208},{24,216},{32,224},{40,232},{48,240},{56,2... | collective-permute-start | bytes 196616 | tf_op jit(solution)/shard_map/ppermute | solution.py:338
  34.9 2.4 %collective-permute-done.6.refs_3_ = f32[2,4,32,128]{3,2,1,0:T(8,128)S(1)} collective-permute-done((f32[2,4,32,128]{3,2,1,0:T(8,128)S(1)}, f32[2,4,32,128]{3,2,1,0:T(8,128)S(1)}, u32[]{:S(2)}, u32[]{:S(2)}) %collective-permute-start.6) | collective-permute-done | bytes 131104 | tf_op jit(solution)/shard_map/ppermute | solution.py:338
  38.3 3.1 %collective-permute-done.12.refs_3_ = f32[4,32,128]{2,1,0:T(8,128)S(1)} collective-permute-done((f32[4,32,128]{2,1,0:T(8,128)S(1)}, f32[4,32,128]{2,1,0:T(8,128)S(1)}, u32[]{:S(2)}, u32[]{:S(2)}) %collective-permute-start.12) | collective-permute-done | bytes 65568 | tf_op jit(solution)/shard_map/ppermute | solution.py:338
  41.5 1.9 %collective-permute-start.13 = (f32[4,32,128]{2,1,0:T(8,128)S(1)}, f32[4,32,128]{2,1,0:T(8,128)S(1)}, u32[]{:S(2)}, u32[]{:S(2)}) collective-permute-start(f32[4,32,128]{2,1,0:T(8,128)S(1)} %shard_map.97.refs_0_), channel_id=1, source_target_pairs={{0,128},{8,136},{16,144},{24,152},{32,160},{40,168},{48,176},{56,1... | collective-permute-start | bytes 196616 | tf_op jit(solution)/shard_map/ppermute | solution.py:338
  43.4 1.6 %collective-permute-start.14 = (f32[4,32,128]{2,1,0:T(8,128)S(1)}, f32[4,32,128]{2,1,0:T(8,128)S(1)}, u32[]{:S(2)}, u32[]{:S(2)}) collective-permute-start(f32[4,32,128]{2,1,0:T(8,128)S(1)} %shard_map.97.refs_0_), channel_id=1, source_target_pairs={{0,192},{8,200},{16,208},{24,216},{32,224},{40,232},{48,240},{56,2... | collective-permute-start | bytes 196616 | tf_op jit(solution)/shard_map/ppermute | solution.py:338
  45.2 2.7 %collective-permute-start.23 = (f32[2,4,32,128]{3,2,1,0:T(8,128)S(1)}, f32[2,4,32,128]{3,2,1,0:T(8,128)S(1)}, u32[]{:S(2)}, u32[]{:S(2)}) collective-permute-start(f32[2,4,32,128]{3,2,1,0:T(8,128)S(1)} %shard_map.99.refs_0_), channel_id=1, source_target_pairs={{0,48},{8,56},{16,0},{24,8},{32,16},{40,24},{48,32},{56,40},{64,11... | collective-permute-start | bytes 393224 | tf_op jit(solution)/shard_map/ppermute | solution.py:338
  47.8 3.6 %collective-permute-start.25 = (f32[2,4,32,128]{3,2,1,0:T(8,128)S(1)}, f32[2,4,32,128]{3,2,1,0:T(8,128)S(1)}, u32[]{:S(2)}, u32[]{:S(2)}) collective-permute-start(f32[2,4,32,128]{3,2,1,0:T(8,128)S(1)} %shard_map.99.refs_0_), channel_id=1, source_target_pairs={{0,8},{8,0},{16,24},{24,16},{32,40},{40,32},{48,56},{56,48},{64,72... | collective-permute-start | bytes 393224 | tf_op jit(solution)/shard_map/ppermute | solution.py:338
  52.2 2.0 %collective-permute-start.17 = (f32[2,4,32,128]{3,2,1,0:T(8,128)S(1)}, f32[2,4,32,128]{3,2,1,0:T(8,128)S(1)}, u32[]{:S(2)}, u32[]{:S(2)}) collective-permute-start(f32[2,4,32,128]{3,2,1,0:T(8,128)S(1)} %shard_map.98.refs_4_), channel_id=1, source_target_pairs={{0,48},{8,56},{16,0},{24,8},{32,16},{40,24},{48,32},{56,40},{64,11... | collective-permute-start | bytes 393224 | tf_op jit(solution)/shard_map/ppermute | solution.py:338
  54.2 1.5 %collective-permute-start.19 = (f32[2,4,32,128]{3,2,1,0:T(8,128)S(1)}, f32[2,4,32,128]{3,2,1,0:T(8,128)S(1)}, u32[]{:S(2)}, u32[]{:S(2)}) collective-permute-start(f32[2,4,32,128]{3,2,1,0:T(8,128)S(1)} %shard_map.98.refs_4_), channel_id=1, source_target_pairs={{0,32},{8,40},{16,48},{24,56},{32,0},{40,8},{48,16},{56,24},{64,96... | collective-permute-start | bytes 393224 | tf_op jit(solution)/shard_map/ppermute | solution.py:338
  55.7 2.4 %collective-permute-start.29 = (f32[2,4,32,128]{3,2,1,0:T(8,128)S(1)}, f32[2,4,32,128]{3,2,1,0:T(8,128)S(1)}, u32[]{:S(2)}, u32[]{:S(2)}) collective-permute-start(f32[2,4,32,128]{3,2,1,0:T(8,128)S(1)} %shard_map.98.refs_4_), channel_id=1, source_target_pairs={{0,8},{8,0},{16,24},{24,16},{32,40},{40,32},{48,56},{56,48},{64,72... | collective-permute-start | bytes 393224 | tf_op jit(solution)/shard_map/ppermute | solution.py:338
  58.1 1.8 %collective-permute-done.15.refs_5_ = f32[2,4,32,128]{3,2,1,0:T(8,128)S(1)} collective-permute-done((f32[2,4,32,128]{3,2,1,0:T(8,128)S(1)}, f32[2,4,32,128]{3,2,1,0:T(8,128)S(1)}, u32[]{:S(2)}, u32[]{:S(2)}) %collective-permute-start.15) | collective-permute-done | bytes 131104 | tf_op jit(solution)/shard_map/ppermute | solution.py:338
  61.7 1.2 %collective-permute-start.16 = (f32[2,4,32,128]{3,2,1,0:T(8,128)S(1)}, f32[2,4,32,128]{3,2,1,0:T(8,128)S(1)}, u32[]{:S(2)}, u32[]{:S(2)}) collective-permute-start(f32[2,4,32,128]{3,2,1,0:T(8,128)S(1)} %collective-permute-done.15.refs_5_), channel_id=1, source_target_pairs={{0,8},{8,0},{16,24},{24,16},{32,40},{40,32},{48,56},{56,48},{64,72... | collective-permute-start | bytes 393224 | tf_op jit(solution)/shard_map/ppermute | solution.py:338
  63.5 1.4 %shard_map.100.refs_3_ = f32[4,1024,128]{2,1,0:T(8,128)} custom-call(f32[2,4,32,128]{3,2,1,0:T(8,128)S(1)} %shard_map.99.refs_0_, f32[2,4,32,128]{3,2,1,0:T(8,128)S(1)} %collective-permute-done.22.refs_1_, f32[2,4,32,128]{3,2,1,0:T(8,128)S(1)} %collective-permute-done.23.refs_2_, f32[2,4,32,128]{3,2,1,0:T(8,128)S(1)} %collective-permute-done.24.refs_3_, ...), custom_call_target="tpu_custom_call" | custom-call | tf_op jit(solution)/shard_map/pallas_call | solution.py:326
  (61 shorter events, 8.7 us)
Async XLA Ops:
  3.1 15.6 %collective-permute-start = (f32[8,1024]{1,0:T(8,128)S(1)}, f32[8,1024]{1,0:T(8,128)S(1)}, u32[]{:S(2)}, u32[]{:S(2)}) collective-permute-start(f32[8,1024]{1,0:T(8,128)S(1)} %get-tuple-element.28), channel_id=1, source_target_pairs={{1,2},{2,1},{3,4},{4,3},{5,6},{6,5},{9,10},{10,9},{11,12},{12,11},... | collective-permute-start | bytes 98312 | tf_op jit(solution)/shard_map/ppermute | solution.py:342
  5.2 13.5 %collective-permute-start.1 = (f32[8,1024]{1,0:T(8,128)S(1)}, f32[8,1024]{1,0:T(8,128)S(1)}, u32[]{:S(2)}, u32[]{:S(2)}) collective-permute-start(f32[8,1024]{1,0:T(8,128)S(1)} %get-tuple-element.29), channel_id=1, source_target_pairs={{0,1},{1,0},{2,3},{3,2},{4,5},{5,4},{6,7},{7,6},{8,9},{9,8},{10,11... | collective-permute-start | bytes 98312 | tf_op jit(solution)/shard_map/ppermute | solution.py:342
  17.4 3.6 %collective-permute-start.2 = (f32[4,512,128]{2,1,0:T(8,128)S(1)}, f32[4,512,128]{2,1,0:T(8,128)S(1)}, u32[]{:S(2)}, u32[]{:S(2)}) collective-permute-start(f32[4,512,128]{2,1,0:T(8,128)S(1)} %get-tuple-element.33), channel_id=1, source_target_pairs={{0,8},{8,0},{16,24},{24,16},{32,40},{40,32},{48,56},{56,48},{64,72... | collective-permute-start | bytes 3145736 | tf_op jit(solution)/shard_map/ppermute | solution.py:338
  21.6 7.1 %collective-permute-start.7 = (f32[2,4,32,128]{3,2,1,0:T(8,128)S(1)}, f32[2,4,32,128]{3,2,1,0:T(8,128)S(1)}, u32[]{:S(2)}, u32[]{:S(2)}) collective-permute-start(f32[2,4,32,128]{3,2,1,0:T(8,128)S(1)} %get-tuple-element.45), channel_id=1, source_target_pairs={{0,16},{8,24},{16,32},{24,40},{32,48},{40,56},{48,0},{56,8},{64,80... | collective-permute-start | bytes 393224 | tf_op jit(solution)/shard_map/ppermute | solution.py:338
  23.0 6.3 %collective-permute-start.8 = (f32[2,4,32,128]{3,2,1,0:T(8,128)S(1)}, f32[2,4,32,128]{3,2,1,0:T(8,128)S(1)}, u32[]{:S(2)}, u32[]{:S(2)}) collective-permute-start(f32[2,4,32,128]{3,2,1,0:T(8,128)S(1)} %get-tuple-element.46), channel_id=1, source_target_pairs={{0,48},{8,56},{16,0},{24,8},{32,16},{40,24},{48,32},{56,40},{64,11... | collective-permute-start | bytes 393224 | tf_op jit(solution)/shard_map/ppermute | solution.py:338
  24.5 7.2 %collective-permute-start.9 = (f32[2,4,32,128]{3,2,1,0:T(8,128)S(1)}, f32[2,4,32,128]{3,2,1,0:T(8,128)S(1)}, u32[]{:S(2)}, u32[]{:S(2)}) collective-permute-start(f32[2,4,32,128]{3,2,1,0:T(8,128)S(1)} %get-tuple-element.47), channel_id=1, source_target_pairs={{0,32},{8,40},{16,48},{24,56},{32,0},{40,8},{48,16},{56,24},{64,96... | collective-permute-start | bytes 393224 | tf_op jit(solution)/shard_map/ppermute | solution.py:338
  26.1 8.8 %collective-permute-start.4 = (f32[2,4,32,128]{3,2,1,0:T(8,128)S(1)}, f32[2,4,32,128]{3,2,1,0:T(8,128)S(1)}, u32[]{:S(2)}, u32[]{:S(2)}) collective-permute-start(f32[2,4,32,128]{3,2,1,0:T(8,128)S(1)} %get-tuple-element.40), channel_id=1, source_target_pairs={{0,16},{8,24},{16,32},{24,40},{32,48},{40,56},{48,0},{56,8},{64,80... | collective-permute-start | bytes 393224 | tf_op jit(solution)/shard_map/ppermute | solution.py:338
  26.5 8.4 %collective-permute-start.5 = (f32[2,4,32,128]{3,2,1,0:T(8,128)S(1)}, f32[2,4,32,128]{3,2,1,0:T(8,128)S(1)}, u32[]{:S(2)}, u32[]{:S(2)}) collective-permute-start(f32[2,4,32,128]{3,2,1,0:T(8,128)S(1)} %get-tuple-element.41), channel_id=1, source_target_pairs={{0,48},{8,56},{16,0},{24,8},{32,16},{40,24},{48,32},{56,40},{64,11... | collective-permute-start | bytes 393224 | tf_op jit(solution)/shard_map/ppermute | solution.py:338
  28.8 8.6 %collective-permute-start.6 = (f32[2,4,32,128]{3,2,1,0:T(8,128)S(1)}, f32[2,4,32,128]{3,2,1,0:T(8,128)S(1)}, u32[]{:S(2)}, u32[]{:S(2)}) collective-permute-start(f32[2,4,32,128]{3,2,1,0:T(8,128)S(1)} %get-tuple-element.42), channel_id=1, source_target_pairs={{0,32},{8,40},{16,48},{24,56},{32,0},{40,8},{48,16},{56,24},{64,96... | collective-permute-start | bytes 393224 | tf_op jit(solution)/shard_map/ppermute | solution.py:338
  31.8 6.4 %collective-permute-start.10 = (f32[4,32,128]{2,1,0:T(8,128)S(1)}, f32[4,32,128]{2,1,0:T(8,128)S(1)}, u32[]{:S(2)}, u32[]{:S(2)}) collective-permute-start(f32[4,32,128]{2,1,0:T(8,128)S(1)} %get-tuple-element.48), channel_id=1, source_target_pairs={{0,128},{8,136},{16,144},{24,152},{32,160},{40,168},{48,176},{56,1... | collective-permute-start | bytes 196616 | tf_op jit(solution)/shard_map/ppermute | solution.py:338
  33.1 5.1 %collective-permute-start.11 = (f32[4,32,128]{2,1,0:T(8,128)S(1)}, f32[4,32,128]{2,1,0:T(8,128)S(1)}, u32[]{:S(2)}, u32[]{:S(2)}) collective-permute-start(f32[4,32,128]{2,1,0:T(8,128)S(1)} %get-tuple-element.49), channel_id=1, source_target_pairs={{0,192},{8,200},{16,208},{24,216},{32,224},{40,232},{48,240},{56,2... | collective-permute-start | bytes 196616 | tf_op jit(solution)/shard_map/ppermute | solution.py:338
  37.4 3.9 %collective-permute-start.12 = (f32[4,32,128]{2,1,0:T(8,128)S(1)}, f32[4,32,128]{2,1,0:T(8,128)S(1)}, u32[]{:S(2)}, u32[]{:S(2)}) collective-permute-start(f32[4,32,128]{2,1,0:T(8,128)S(1)} %get-tuple-element.50), channel_id=1, source_target_pairs={{0,64},{8,72},{16,80},{24,88},{32,96},{40,104},{48,112},{56,120},{... | collective-permute-start | bytes 196616 | tf_op jit(solution)/shard_map/ppermute | solution.py:338
  41.4 3.6 %collective-permute-start.21 = (f32[4,32,128]{2,1,0:T(8,128)S(1)}, f32[4,32,128]{2,1,0:T(8,128)S(1)}, u32[]{:S(2)}, u32[]{:S(2)}) collective-permute-start(f32[4,32,128]{2,1,0:T(8,128)S(1)} %shard_map.97.refs_0_), channel_id=1, source_target_pairs={{0,64},{8,72},{16,80},{24,88},{32,96},{40,104},{48,112},{56,120},{... | collective-permute-start | bytes 196616 | tf_op jit(solution)/shard_map/ppermute | solution.py:338
  41.5 6.3 %collective-permute-start.13 = (f32[4,32,128]{2,1,0:T(8,128)S(1)}, f32[4,32,128]{2,1,0:T(8,128)S(1)}, u32[]{:S(2)}, u32[]{:S(2)}) collective-permute-start(f32[4,32,128]{2,1,0:T(8,128)S(1)} %shard_map.97.refs_0_), channel_id=1, source_target_pairs={{0,128},{8,136},{16,144},{24,152},{32,160},{40,168},{48,176},{56,1... | collective-permute-start | bytes 196616 | tf_op jit(solution)/shard_map/ppermute | solution.py:338
  43.4 8.0 %collective-permute-start.14 = (f32[4,32,128]{2,1,0:T(8,128)S(1)}, f32[4,32,128]{2,1,0:T(8,128)S(1)}, u32[]{:S(2)}, u32[]{:S(2)}) collective-permute-start(f32[4,32,128]{2,1,0:T(8,128)S(1)} %shard_map.97.refs_0_), channel_id=1, source_target_pairs={{0,192},{8,200},{16,208},{24,216},{32,224},{40,232},{48,240},{56,2... | collective-permute-start | bytes 196616 | tf_op jit(solution)/shard_map/ppermute | solution.py:338
  45.1 7.1 %collective-permute-start.22 = (f32[2,4,32,128]{3,2,1,0:T(8,128)S(1)}, f32[2,4,32,128]{3,2,1,0:T(8,128)S(1)}, u32[]{:S(2)}, u32[]{:S(2)}) collective-permute-start(f32[2,4,32,128]{3,2,1,0:T(8,128)S(1)} %shard_map.99.refs_0_), channel_id=1, source_target_pairs={{0,16},{8,24},{16,32},{24,40},{32,48},{40,56},{48,0},{56,8},{64,80... | collective-permute-start | bytes 393224 | tf_op jit(solution)/shard_map/ppermute | solution.py:338
  45.2 9.0 %collective-permute-start.23 = (f32[2,4,32,128]{3,2,1,0:T(8,128)S(1)}, f32[2,4,32,128]{3,2,1,0:T(8,128)S(1)}, u32[]{:S(2)}, u32[]{:S(2)}) collective-permute-start(f32[2,4,32,128]{3,2,1,0:T(8,128)S(1)} %shard_map.99.refs_0_), channel_id=1, source_target_pairs={{0,48},{8,56},{16,0},{24,8},{32,16},{40,24},{48,32},{56,40},{64,11... | collective-permute-start | bytes 393224 | tf_op jit(solution)/shard_map/ppermute | solution.py:338
  47.8 7.9 %collective-permute-start.24 = (f32[2,4,32,128]{3,2,1,0:T(8,128)S(1)}, f32[2,4,32,128]{3,2,1,0:T(8,128)S(1)}, u32[]{:S(2)}, u32[]{:S(2)}) collective-permute-start(f32[2,4,32,128]{3,2,1,0:T(8,128)S(1)} %shard_map.99.refs_0_), channel_id=1, source_target_pairs={{0,32},{8,40},{16,48},{24,56},{32,0},{40,8},{48,16},{56,24},{64,96... | collective-permute-start | bytes 393224 | tf_op jit(solution)/shard_map/ppermute | solution.py:338
  47.8 10.3 %collective-permute-start.25 = (f32[2,4,32,128]{3,2,1,0:T(8,128)S(1)}, f32[2,4,32,128]{3,2,1,0:T(8,128)S(1)}, u32[]{:S(2)}, u32[]{:S(2)}) collective-permute-start(f32[2,4,32,128]{3,2,1,0:T(8,128)S(1)} %shard_map.99.refs_0_), channel_id=1, source_target_pairs={{0,8},{8,0},{16,24},{24,16},{32,40},{40,32},{48,56},{56,48},{64,72... | collective-permute-start | bytes 393224 | tf_op jit(solution)/shard_map/ppermute | solution.py:338
  51.4 8.5 %collective-permute-start.15 = (f32[2,4,32,128]{3,2,1,0:T(8,128)S(1)}, f32[2,4,32,128]{3,2,1,0:T(8,128)S(1)}, u32[]{:S(2)}, u32[]{:S(2)}) collective-permute-start(f32[2,4,32,128]{3,2,1,0:T(8,128)S(1)} %shard_map.98.refs_4_), channel_id=1, source_target_pairs={{0,16},{8,24},{16,32},{24,40},{32,48},{40,56},{48,0},{56,8},{64,80... | collective-permute-start | bytes 393224 | tf_op jit(solution)/shard_map/ppermute | solution.py:338
  52.2 8.5 %collective-permute-start.17 = (f32[2,4,32,128]{3,2,1,0:T(8,128)S(1)}, f32[2,4,32,128]{3,2,1,0:T(8,128)S(1)}, u32[]{:S(2)}, u32[]{:S(2)}) collective-permute-start(f32[2,4,32,128]{3,2,1,0:T(8,128)S(1)} %shard_map.98.refs_4_), channel_id=1, source_target_pairs={{0,48},{8,56},{16,0},{24,8},{32,16},{40,24},{48,32},{56,40},{64,11... | collective-permute-start | bytes 393224 | tf_op jit(solution)/shard_map/ppermute | solution.py:338
  54.2 7.6 %collective-permute-start.19 = (f32[2,4,32,128]{3,2,1,0:T(8,128)S(1)}, f32[2,4,32,128]{3,2,1,0:T(8,128)S(1)}, u32[]{:S(2)}, u32[]{:S(2)}) collective-permute-start(f32[2,4,32,128]{3,2,1,0:T(8,128)S(1)} %shard_map.98.refs_4_), channel_id=1, source_target_pairs={{0,32},{8,40},{16,48},{24,56},{32,0},{40,8},{48,16},{56,24},{64,96... | collective-permute-start | bytes 393224 | tf_op jit(solution)/shard_map/ppermute | solution.py:338
  55.7 7.3 %collective-permute-start.29 = (f32[2,4,32,128]{3,2,1,0:T(8,128)S(1)}, f32[2,4,32,128]{3,2,1,0:T(8,128)S(1)}, u32[]{:S(2)}, u32[]{:S(2)}) collective-permute-start(f32[2,4,32,128]{3,2,1,0:T(8,128)S(1)} %shard_map.98.refs_4_), channel_id=1, source_target_pairs={{0,8},{8,0},{16,24},{24,16},{32,40},{40,32},{48,56},{56,48},{64,72... | collective-permute-start | bytes 393224 | tf_op jit(solution)/shard_map/ppermute | solution.py:338
  58.1 4.8 %collective-permute-start.26 = (f32[2,4,32,128]{3,2,1,0:T(8,128)S(1)}, f32[2,4,32,128]{3,2,1,0:T(8,128)S(1)}, u32[]{:S(2)}, u32[]{:S(2)}) collective-permute-start(f32[2,4,32,128]{3,2,1,0:T(8,128)S(1)} %collective-permute-done.22.refs_1_), channel_id=1, source_target_pairs={{0,8},{8,0},{16,24},{24,16},{32,40},{40,32},{48,56},{56,48},{64,72... | collective-permute-start | bytes 393224 | tf_op jit(solution)/shard_map/ppermute | solution.py:338
  (13 other events, 104.4 us)

commit v5 on v4

--- a/solution.py
+++ b/solution.py
@@ -296,9 +296,9 @@
             begin += part.shape[0]
 
 
-def join(*parts):
+def join(*parts, cost=256 << 20):
     count = sum(part.shape[0] if part.ndim == 4 else 1 for part in parts)
-    return call(join_kernel, image(count, 4, TILE, COLS), [VMEM] * len(parts), parts, cost=256 << 20)
+    return call(join_kernel, image(count, 4, TILE, COLS), [VMEM] * len(parts), parts, cost=cost)
 
 
 def frame_kernel(places, *refs):
@@ -373,11 +373,13 @@
     mine = tile(view_mask, (mine, two, three, one))
     near = join(mine, send(mine, flip(8)))
     far = join(send(mine, flip(16)), send(mine, flip(24)))
-    blocks = (near, *to_quarters(near, near, near), far, *to_quarters(far, far, far))
+    own = join(near, far, cost=1 << 10)
+    plus, minus, opposite = to_quarters(far, far, far)
+    blocks = (own, *to_quarters(near, near, near), plus, opposite, minus)
     others = tuple(send(block, flip(1)) for block in blocks)
-    places = [(side, upper, n) for side in range(2) for upper in (0, 2) for n in range(4)]
-    begun = frame(places[:13], blocks + others[:5])
-    return frame(places[13:], others[5:], (begun,))
+    places = [(side, upper, n) for side in range(2) for upper, n in ((0, 0), (0, 1), (0, 2), (0, 3), (2, 1), (2, 3), (2, 2))]
+    begun = frame(places[:11], blocks + others[:4])
+    return frame(places[11:], others[4:], (begun,))
 
 
 def solution(mesh):

time: 66 us -> 65.8 us (level)
  waiting for transfers between devices: 11.7 us -> 9.84 us
  starting transfers between devices: 41.7 us -> 43.3 us
    ppermute x28 -> x27, waiting for transfers between devices: 11.7 us -> 9.83 us  [send(): return lax.ppermute(block, 'gx', [(i, target(i)) for i in range(32)])]
    ppermute x28 -> x27, starting transfers between devices: 32 us -> 33.6 us  [send(): return lax.ppermute(block, 'gx', [(i, target(i)) for i in range(32)])]
    pallas_call x9 -> x10, Pallas kernels: 9.24 us -> 9.27 us  [call(): pl.pallas_call(kernel, out_shape=outs, in_specs=ins, out_specs=jax.tree.m...]
  transfers between devices with their start and end apart: 30 -> 29, of which waited for: 7 -> 6; matrix products, arithmetic and copies ran while one was open for 0% -> 0% of each run, Pallas kernels for 11% -> 11%
where the time goes in v5:
time: 65.8 us; the launch traced here: 65.6 us
  starting transfers between devices  43.3 us (66%)
  Pallas kernels  11.5 us (17%)
  waiting for transfers between devices  9.84 us (15%)
  between operations  1 us (2%)
    ppermute x27, starting transfers between devices, send(): return lax.ppermute(block, 'gx', [(i, target(i)) for i in range(32)])  33.6 us
    ppermute x27, waiting for transfers between devices, send(): return lax.ppermute(block, 'gx', [(i, target(i)) for i in range(32)])  9.83 us
    ppermute x2, starting transfers between devices, beside(): lax.ppermute(block, 'gy', [swap for i in range(first, 7, 2) for swap in (...  9.74 us
    pallas_call x10, Pallas kernels, call(): pl.pallas_call(kernel, out_shape=outs, in_specs=ins, out_specs=jax.tree.m...  9.27 us
    pallas_call x2, Pallas kernels, frame(): pl.pallas_call(functools.partial(frame_kernel, places), out_shape=image(4...  2.19 us
  transfers between devices with their start and end apart: 29, of which 6 were waited for; matrix products, arithmetic and copies ran while one was open for 0% of the time, Pallas kernels for 11%

profile of v5, /device:TPU:5, one launch (start us, length us, event | category | flops | bytes accessed | tf_op | source)
XLA Modules:
  0.0 65.6 jit_solution(1446515814050802438)
XLA Ops:
  0.0 3.0 %shard_map.91 = (f32[8,1040,128]{2,1,0:T(8,128)S(1)}, f32[4,8,1024]{2,1,0:T(8,128)S(1)}, f32[8,1024]{1,0:T(8,128)S(1)}, f32[8,1024]{1,0:T(8,128)S(1)}) custom-call(f32[8,1024,128]{2,1,0:T(8,128)} %tsdf.1), custom_call_target="tpu_custom_call" | custom-call | flops 1073741824 | bytes 4194304 | tf_op jit(solution)/shard_map/pallas_call | solution.py:30
  3.1 2.2 %collective-permute-start = (f32[8,1024]{1,0:T(8,128)S(1)}, f32[8,1024]{1,0:T(8,128)S(1)}, u32[]{:S(2)}, u32[]{:S(2)}) collective-permute-start(f32[8,1024]{1,0:T(8,128)S(1)} %get-tuple-element.28), channel_id=1, source_target_pairs={{1,2},{2,1},{3,4},{4,3},{5,6},{6,5},{9,10},{10,9},{11,12},{12,11},... | collective-permute-start | bytes 98312 | tf_op jit(solution)/shard_map/ppermute | solution.py:342
  5.2 7.6 %collective-permute-start.1 = (f32[8,1024]{1,0:T(8,128)S(1)}, f32[8,1024]{1,0:T(8,128)S(1)}, u32[]{:S(2)}, u32[]{:S(2)}) collective-permute-start(f32[8,1024]{1,0:T(8,128)S(1)} %get-tuple-element.29), channel_id=1, source_target_pairs={{0,1},{1,0},{2,3},{3,2},{4,5},{5,4},{6,7},{7,6},{8,9},{9,8},{10,11... | collective-permute-start | bytes 98312 | tf_op jit(solution)/shard_map/ppermute | solution.py:342
  12.9 4.5 %shard_map.92 = (f32[4,512,128]{2,1,0:T(8,128)S(1)}, f32[4,512,128]{2,1,0:T(8,128)S(1)}) custom-call(f32[8,1040,128]{2,1,0:T(8,128)S(1)} %get-tuple-element.30.cells, s32[8]{0:T(128)S(1)} %copy-done, s32[8]{0:T(128)S(1)} %copy-done.1, f32[8]{0:T(128)S(1)} %copy-done.2, f32[8]{0:T(128)S(1)} %copy-done.3, f32[8]{0:T(128)S(1)} %copy-done.4, f32[3]{0:T(128)S(1)} %copy-done.5, ...), custom_call_target="tpu_custom_call" | custom-call | flops 5368709120 | bytes 20971520 | tf_op jit(solution)/shard_map/pallas_call | solution.py:30
  17.4 1.3 %collective-permute-start.2 = (f32[4,512,128]{2,1,0:T(8,128)S(1)}, f32[4,512,128]{2,1,0:T(8,128)S(1)}, u32[]{:S(2)}, u32[]{:S(2)}) collective-permute-start(f32[4,512,128]{2,1,0:T(8,128)S(1)} %get-tuple-element.33), channel_id=1, source_target_pairs={{0,8},{8,0},{16,24},{24,16},{32,40},{40,32},{48,56},{56,48},{64,72... | collective-permute-start | bytes 3145736 | tf_op jit(solution)/shard_map/ppermute | solution.py:338
  21.6 1.4 %collective-permute-start.7 = (f32[2,4,32,128]{3,2,1,0:T(8,128)S(1)}, f32[2,4,32,128]{3,2,1,0:T(8,128)S(1)}, u32[]{:S(2)}, u32[]{:S(2)}) collective-permute-start(f32[2,4,32,128]{3,2,1,0:T(8,128)S(1)} %get-tuple-element.45), channel_id=1, source_target_pairs={{0,16},{8,24},{16,32},{24,40},{32,48},{40,56},{48,0},{56,8},{64,80... | collective-permute-start | bytes 393224 | tf_op jit(solution)/shard_map/ppermute | solution.py:338
  23.0 1.5 %collective-permute-start.8 = (f32[2,4,32,128]{3,2,1,0:T(8,128)S(1)}, f32[2,4,32,128]{3,2,1,0:T(8,128)S(1)}, u32[]{:S(2)}, u32[]{:S(2)}) collective-permute-start(f32[2,4,32,128]{3,2,1,0:T(8,128)S(1)} %get-tuple-element.46), channel_id=1, source_target_pairs={{0,48},{8,56},{16,0},{24,8},{32,16},{40,24},{48,32},{56,40},{64,11... | collective-permute-start | bytes 393224 | tf_op jit(solution)/shard_map/ppermute | solution.py:338
  24.6 1.5 %collective-permute-start.9 = (f32[2,4,32,128]{3,2,1,0:T(8,128)S(1)}, f32[2,4,32,128]{3,2,1,0:T(8,128)S(1)}, u32[]{:S(2)}, u32[]{:S(2)}) collective-permute-start(f32[2,4,32,128]{3,2,1,0:T(8,128)S(1)} %get-tuple-element.47), channel_id=1, source_target_pairs={{0,32},{8,40},{16,48},{24,56},{32,0},{40,8},{48,16},{56,24},{64,96... | collective-permute-start | bytes 393224 | tf_op jit(solution)/shard_map/ppermute | solution.py:338
  26.5 2.3 %collective-permute-start.5 = (f32[2,4,32,128]{3,2,1,0:T(8,128)S(1)}, f32[2,4,32,128]{3,2,1,0:T(8,128)S(1)}, u32[]{:S(2)}, u32[]{:S(2)}) collective-permute-start(f32[2,4,32,128]{3,2,1,0:T(8,128)S(1)} %get-tuple-element.41), channel_id=1, source_target_pairs={{0,48},{8,56},{16,0},{24,8},{32,16},{40,24},{48,32},{56,40},{64,11... | collective-permute-start | bytes 393224 | tf_op jit(solution)/shard_map/ppermute | solution.py:338
  29.3 2.4 %collective-permute-done.9.refs_3_ = f32[2,4,32,128]{3,2,1,0:T(8,128)S(1)} collective-permute-done((f32[2,4,32,128]{3,2,1,0:T(8,128)S(1)}, f32[2,4,32,128]{3,2,1,0:T(8,128)S(1)}, u32[]{:S(2)}, u32[]{:S(2)}) %collective-permute-start.9) | collective-permute-done | bytes 131104 | tf_op jit(solution)/shard_map/ppermute | solution.py:338
  31.8 1.3 %collective-permute-start.10 = (f32[4,32,128]{2,1,0:T(8,128)S(1)}, f32[4,32,128]{2,1,0:T(8,128)S(1)}, u32[]{:S(2)}, u32[]{:S(2)}) collective-permute-start(f32[4,32,128]{2,1,0:T(8,128)S(1)} %get-tuple-element.48), channel_id=1, source_target_pairs={{0,128},{8,136},{16,144},{24,152},{32,160},{40,168},{48,176},{56,1... | collective-permute-start | bytes 196616 | tf_op jit(solution)/shard_map/ppermute | solution.py:338
  33.1 1.6 %collective-permute-start.11 = (f32[4,32,128]{2,1,0:T(8,128)S(1)}, f32[4,32,128]{2,1,0:T(8,128)S(1)}, u32[]{:S(2)}, u32[]{:S(2)}) collective-permute-start(f32[4,32,128]{2,1,0:T(8,128)S(1)} %get-tuple-element.49), channel_id=1, source_target_pairs={{0,192},{8,200},{16,208},{24,216},{32,224},{40,232},{48,240},{56,2... | collective-permute-start | bytes 196616 | tf_op jit(solution)/shard_map/ppermute | solution.py:338
  34.7 2.6 %collective-permute-done.6.refs_3_ = f32[2,4,32,128]{3,2,1,0:T(8,128)S(1)} collective-permute-done((f32[2,4,32,128]{3,2,1,0:T(8,128)S(1)}, f32[2,4,32,128]{3,2,1,0:T(8,128)S(1)}, u32[]{:S(2)}, u32[]{:S(2)}) %collective-permute-start.6) | collective-permute-done | bytes 131104 | tf_op jit(solution)/shard_map/ppermute | solution.py:338
  38.2 3.1 %collective-permute-done.12.refs_3_ = f32[4,32,128]{2,1,0:T(8,128)S(1)} collective-permute-done((f32[4,32,128]{2,1,0:T(8,128)S(1)}, f32[4,32,128]{2,1,0:T(8,128)S(1)}, u32[]{:S(2)}, u32[]{:S(2)}) %collective-permute-start.12) | collective-permute-done | bytes 65568 | tf_op jit(solution)/shard_map/ppermute | solution.py:338
  41.5 1.9 %collective-permute-start.13 = (f32[4,32,128]{2,1,0:T(8,128)S(1)}, f32[4,32,128]{2,1,0:T(8,128)S(1)}, u32[]{:S(2)}, u32[]{:S(2)}) collective-permute-start(f32[4,32,128]{2,1,0:T(8,128)S(1)} %shard_map.97.refs_0_), channel_id=1, source_target_pairs={{0,128},{8,136},{16,144},{24,152},{32,160},{40,168},{48,176},{56,1... | collective-permute-start | bytes 196616 | tf_op jit(solution)/shard_map/ppermute | solution.py:338
  43.4 1.6 %collective-permute-start.14 = (f32[4,32,128]{2,1,0:T(8,128)S(1)}, f32[4,32,128]{2,1,0:T(8,128)S(1)}, u32[]{:S(2)}, u32[]{:S(2)}) collective-permute-start(f32[4,32,128]{2,1,0:T(8,128)S(1)} %shard_map.97.refs_0_), channel_id=1, source_target_pairs={{0,192},{8,200},{16,208},{24,216},{32,224},{40,232},{48,240},{56,2... | collective-permute-start | bytes 196616 | tf_op jit(solution)/shard_map/ppermute | solution.py:338
  45.1 2.7 %collective-permute-start.23 = (f32[2,4,32,128]{3,2,1,0:T(8,128)S(1)}, f32[2,4,32,128]{3,2,1,0:T(8,128)S(1)}, u32[]{:S(2)}, u32[]{:S(2)}) collective-permute-start(f32[2,4,32,128]{3,2,1,0:T(8,128)S(1)} %shard_map.99.refs_0_), channel_id=1, source_target_pairs={{0,48},{8,56},{16,0},{24,8},{32,16},{40,24},{48,32},{56,40},{64,11... | collective-permute-start | bytes 393224 | tf_op jit(solution)/shard_map/ppermute | solution.py:338
  48.6 2.7 %collective-permute-start.17 = (f32[2,4,32,128]{3,2,1,0:T(8,128)S(1)}, f32[2,4,32,128]{3,2,1,0:T(8,128)S(1)}, u32[]{:S(2)}, u32[]{:S(2)}) collective-permute-start(f32[2,4,32,128]{3,2,1,0:T(8,128)S(1)} %shard_map.98.refs_1_), channel_id=1, source_target_pairs={{0,32},{8,40},{16,48},{24,56},{32,0},{40,8},{48,16},{56,24},{64,96... | collective-permute-start | bytes 393224 | tf_op jit(solution)/shard_map/ppermute | solution.py:338
  51.4 1.7 %collective-permute-start.19 = (f32[2,4,32,128]{3,2,1,0:T(8,128)S(1)}, f32[2,4,32,128]{3,2,1,0:T(8,128)S(1)}, u32[]{:S(2)}, u32[]{:S(2)}) collective-permute-start(f32[2,4,32,128]{3,2,1,0:T(8,128)S(1)} %shard_map.98.refs_1_), channel_id=1, source_target_pairs={{0,48},{8,56},{16,0},{24,8},{32,16},{40,24},{48,32},{56,40},{64,11... | collective-permute-start | bytes 393224 | tf_op jit(solution)/shard_map/ppermute | solution.py:338
  53.1 4.2 %collective-permute-start.25 = (f32[4,4,32,128]{3,2,1,0:T(8,128)S(1)}, f32[4,4,32,128]{3,2,1,0:T(8,128)S(1)}, u32[]{:S(2)}, u32[]{:S(2)}) collective-permute-start(f32[4,4,32,128]{3,2,1,0:T(8,128)S(1)} %shard_map.100.refs_0_), channel_id=1, source_target_pairs={{0,8},{8,0},{16,24},{24,16},{32,40},{40,32},{48,56},{56,48},{64,72... | collective-permute-start | bytes 786440 | tf_op jit(solution)/shard_map/ppermute | solution.py:338
  57.2 1.6 %collective-permute-start.26 = (f32[2,4,32,128]{3,2,1,0:T(8,128)S(1)}, f32[2,4,32,128]{3,2,1,0:T(8,128)S(1)}, u32[]{:S(2)}, u32[]{:S(2)}) collective-permute-start(f32[2,4,32,128]{3,2,1,0:T(8,128)S(1)} %collective-permute-done.22.refs_1_), channel_id=1, source_target_pairs={{0,8},{8,0},{16,24},{24,16},{32,40},{40,32},{48,56},{56,48},{64,72... | collective-permute-start | bytes 393224 | tf_op jit(solution)/shard_map/ppermute | solution.py:338
  58.9 2.0 %collective-permute-start.27 = (f32[2,4,32,128]{3,2,1,0:T(8,128)S(1)}, f32[2,4,32,128]{3,2,1,0:T(8,128)S(1)}, u32[]{:S(2)}, u32[]{:S(2)}) collective-permute-start(f32[2,4,32,128]{3,2,1,0:T(8,128)S(1)} %collective-permute-done.23.refs_2_), channel_id=1, source_target_pairs={{0,8},{8,0},{16,24},{24,16},{32,40},{40,32},{48,56},{56,48},{64,72... | collective-permute-start | bytes 393224 | tf_op jit(solution)/shard_map/ppermute | solution.py:338
  60.8 1.4 %collective-permute-start.28 = (f32[2,4,32,128]{3,2,1,0:T(8,128)S(1)}, f32[2,4,32,128]{3,2,1,0:T(8,128)S(1)}, u32[]{:S(2)}, u32[]{:S(2)}) collective-permute-start(f32[2,4,32,128]{3,2,1,0:T(8,128)S(1)} %collective-permute-done.24.refs_3_), channel_id=1, source_target_pairs={{0,8},{8,0},{16,24},{24,16},{32,40},{40,32},{48,56},{56,48},{64,72... | collective-permute-start | bytes 393224 | tf_op jit(solution)/shard_map/ppermute | solution.py:338
  63.2 1.4 %shard_map.101.refs_3_ = f32[4,1024,128]{2,1,0:T(8,128)} custom-call(f32[4,4,32,128]{3,2,1,0:T(8,128)S(1)} %shard_map.100.refs_0_, f32[2,4,32,128]{3,2,1,0:T(8,128)S(1)} %collective-permute-done.22.refs_1_, f32[2,4,32,128]{3,2,1,0:T(8,128)S(1)} %collective-permute-done.23.refs_2_, f32[2,4,32,128]{3,2,1,0:T(8,128)S(1)} %collective-permute-done.24.refs_3_, ...), custom_call_target="tpu_custom_call" | custom-call | tf_op jit(solution)/shard_map/pallas_call | solution.py:326
  (60 shorter events, 7.2 us)
Async XLA Ops:
  3.1 15.6 %collective-permute-start = (f32[8,1024]{1,0:T(8,128)S(1)}, f32[8,1024]{1,0:T(8,128)S(1)}, u32[]{:S(2)}, u32[]{:S(2)}) collective-permute-start(f32[8,1024]{1,0:T(8,128)S(1)} %get-tuple-element.28), channel_id=1, source_target_pairs={{1,2},{2,1},{3,4},{4,3},{5,6},{6,5},{9,10},{10,9},{11,12},{12,11},... | collective-permute-start | bytes 98312 | tf_op jit(solution)/shard_map/ppermute | solution.py:342
  5.2 13.5 %collective-permute-start.1 = (f32[8,1024]{1,0:T(8,128)S(1)}, f32[8,1024]{1,0:T(8,128)S(1)}, u32[]{:S(2)}, u32[]{:S(2)}) collective-permute-start(f32[8,1024]{1,0:T(8,128)S(1)} %get-tuple-element.29), channel_id=1, source_target_pairs={{0,1},{1,0},{2,3},{3,2},{4,5},{5,4},{6,7},{7,6},{8,9},{9,8},{10,11... | collective-permute-start | bytes 98312 | tf_op jit(solution)/shard_map/ppermute | solution.py:342
  17.4 3.6 %collective-permute-start.2 = (f32[4,512,128]{2,1,0:T(8,128)S(1)}, f32[4,512,128]{2,1,0:T(8,128)S(1)}, u32[]{:S(2)}, u32[]{:S(2)}) collective-permute-start(f32[4,512,128]{2,1,0:T(8,128)S(1)} %get-tuple-element.33), channel_id=1, source_target_pairs={{0,8},{8,0},{16,24},{24,16},{32,40},{40,32},{48,56},{56,48},{64,72... | collective-permute-start | bytes 3145736 | tf_op jit(solution)/shard_map/ppermute | solution.py:338
  21.6 7.1 %collective-permute-start.7 = (f32[2,4,32,128]{3,2,1,0:T(8,128)S(1)}, f32[2,4,32,128]{3,2,1,0:T(8,128)S(1)}, u32[]{:S(2)}, u32[]{:S(2)}) collective-permute-start(f32[2,4,32,128]{3,2,1,0:T(8,128)S(1)} %get-tuple-element.45), channel_id=1, source_target_pairs={{0,16},{8,24},{16,32},{24,40},{32,48},{40,56},{48,0},{56,8},{64,80... | collective-permute-start | bytes 393224 | tf_op jit(solution)/shard_map/ppermute | solution.py:338
  23.0 6.3 %collective-permute-start.8 = (f32[2,4,32,128]{3,2,1,0:T(8,128)S(1)}, f32[2,4,32,128]{3,2,1,0:T(8,128)S(1)}, u32[]{:S(2)}, u32[]{:S(2)}) collective-permute-start(f32[2,4,32,128]{3,2,1,0:T(8,128)S(1)} %get-tuple-element.46), channel_id=1, source_target_pairs={{0,48},{8,56},{16,0},{24,8},{32,16},{40,24},{48,32},{56,40},{64,11... | collective-permute-start | bytes 393224 | tf_op jit(solution)/shard_map/ppermute | solution.py:338
  24.6 7.2 %collective-permute-start.9 = (f32[2,4,32,128]{3,2,1,0:T(8,128)S(1)}, f32[2,4,32,128]{3,2,1,0:T(8,128)S(1)}, u32[]{:S(2)}, u32[]{:S(2)}) collective-permute-start(f32[2,4,32,128]{3,2,1,0:T(8,128)S(1)} %get-tuple-element.47), channel_id=1, source_target_pairs={{0,32},{8,40},{16,48},{24,56},{32,0},{40,8},{48,16},{56,24},{64,96... | collective-permute-start | bytes 393224 | tf_op jit(solution)/shard_map/ppermute | solution.py:338
  26.1 8.6 %collective-permute-start.4 = (f32[2,4,32,128]{3,2,1,0:T(8,128)S(1)}, f32[2,4,32,128]{3,2,1,0:T(8,128)S(1)}, u32[]{:S(2)}, u32[]{:S(2)}) collective-permute-start(f32[2,4,32,128]{3,2,1,0:T(8,128)S(1)} %get-tuple-element.40), channel_id=1, source_target_pairs={{0,16},{8,24},{16,32},{24,40},{32,48},{40,56},{48,0},{56,8},{64,80... | collective-permute-start | bytes 393224 | tf_op jit(solution)/shard_map/ppermute | solution.py:338
  26.5 8.2 %collective-permute-start.5 = (f32[2,4,32,128]{3,2,1,0:T(8,128)S(1)}, f32[2,4,32,128]{3,2,1,0:T(8,128)S(1)}, u32[]{:S(2)}, u32[]{:S(2)}) collective-permute-start(f32[2,4,32,128]{3,2,1,0:T(8,128)S(1)} %get-tuple-element.41), channel_id=1, source_target_pairs={{0,48},{8,56},{16,0},{24,8},{32,16},{40,24},{48,32},{56,40},{64,11... | collective-permute-start | bytes 393224 | tf_op jit(solution)/shard_map/ppermute | solution.py:338
  28.8 8.6 %collective-permute-start.6 = (f32[2,4,32,128]{3,2,1,0:T(8,128)S(1)}, f32[2,4,32,128]{3,2,1,0:T(8,128)S(1)}, u32[]{:S(2)}, u32[]{:S(2)}) collective-permute-start(f32[2,4,32,128]{3,2,1,0:T(8,128)S(1)} %get-tuple-element.42), channel_id=1, source_target_pairs={{0,32},{8,40},{16,48},{24,56},{32,0},{40,8},{48,16},{56,24},{64,96... | collective-permute-start | bytes 393224 | tf_op jit(solution)/shard_map/ppermute | solution.py:338
  31.8 6.4 %collective-permute-start.10 = (f32[4,32,128]{2,1,0:T(8,128)S(1)}, f32[4,32,128]{2,1,0:T(8,128)S(1)}, u32[]{:S(2)}, u32[]{:S(2)}) collective-permute-start(f32[4,32,128]{2,1,0:T(8,128)S(1)} %get-tuple-element.48), channel_id=1, source_target_pairs={{0,128},{8,136},{16,144},{24,152},{32,160},{40,168},{48,176},{56,1... | collective-permute-start | bytes 196616 | tf_op jit(solution)/shard_map/ppermute | solution.py:338
  33.1 5.2 %collective-permute-start.11 = (f32[4,32,128]{2,1,0:T(8,128)S(1)}, f32[4,32,128]{2,1,0:T(8,128)S(1)}, u32[]{:S(2)}, u32[]{:S(2)}) collective-permute-start(f32[4,32,128]{2,1,0:T(8,128)S(1)} %get-tuple-element.49), channel_id=1, source_target_pairs={{0,192},{8,200},{16,208},{24,216},{32,224},{40,232},{48,240},{56,2... | collective-permute-start | bytes 196616 | tf_op jit(solution)/shard_map/ppermute | solution.py:338
  37.4 3.9 %collective-permute-start.12 = (f32[4,32,128]{2,1,0:T(8,128)S(1)}, f32[4,32,128]{2,1,0:T(8,128)S(1)}, u32[]{:S(2)}, u32[]{:S(2)}) collective-permute-start(f32[4,32,128]{2,1,0:T(8,128)S(1)} %get-tuple-element.50), channel_id=1, source_target_pairs={{0,64},{8,72},{16,80},{24,88},{32,96},{40,104},{48,112},{56,120},{... | collective-permute-start | bytes 196616 | tf_op jit(solution)/shard_map/ppermute | solution.py:338
  41.4 3.6 %collective-permute-start.21 = (f32[4,32,128]{2,1,0:T(8,128)S(1)}, f32[4,32,128]{2,1,0:T(8,128)S(1)}, u32[]{:S(2)}, u32[]{:S(2)}) collective-permute-start(f32[4,32,128]{2,1,0:T(8,128)S(1)} %shard_map.97.refs_0_), channel_id=1, source_target_pairs={{0,64},{8,72},{16,80},{24,88},{32,96},{40,104},{48,112},{56,120},{... | collective-permute-start | bytes 196616 | tf_op jit(solution)/shard_map/ppermute | solution.py:338
  41.5 6.3 %collective-permute-start.13 = (f32[4,32,128]{2,1,0:T(8,128)S(1)}, f32[4,32,128]{2,1,0:T(8,128)S(1)}, u32[]{:S(2)}, u32[]{:S(2)}) collective-permute-start(f32[4,32,128]{2,1,0:T(8,128)S(1)} %shard_map.97.refs_0_), channel_id=1, source_target_pairs={{0,128},{8,136},{16,144},{24,152},{32,160},{40,168},{48,176},{56,1... | collective-permute-start | bytes 196616 | tf_op jit(solution)/shard_map/ppermute | solution.py:338
  43.4 5.0 %collective-permute-start.14 = (f32[4,32,128]{2,1,0:T(8,128)S(1)}, f32[4,32,128]{2,1,0:T(8,128)S(1)}, u32[]{:S(2)}, u32[]{:S(2)}) collective-permute-start(f32[4,32,128]{2,1,0:T(8,128)S(1)} %shard_map.97.refs_0_), channel_id=1, source_target_pairs={{0,192},{8,200},{16,208},{24,216},{32,224},{40,232},{48,240},{56,2... | collective-permute-start | bytes 196616 | tf_op jit(solution)/shard_map/ppermute | solution.py:338
  45.0 6.3 %collective-permute-start.22 = (f32[2,4,32,128]{3,2,1,0:T(8,128)S(1)}, f32[2,4,32,128]{3,2,1,0:T(8,128)S(1)}, u32[]{:S(2)}, u32[]{:S(2)}) collective-permute-start(f32[2,4,32,128]{3,2,1,0:T(8,128)S(1)} %shard_map.99.refs_0_), channel_id=1, source_target_pairs={{0,16},{8,24},{16,32},{24,40},{32,48},{40,56},{48,0},{56,8},{64,80... | collective-permute-start | bytes 393224 | tf_op jit(solution)/shard_map/ppermute | solution.py:338
  45.1 7.9 %collective-permute-start.23 = (f32[2,4,32,128]{3,2,1,0:T(8,128)S(1)}, f32[2,4,32,128]{3,2,1,0:T(8,128)S(1)}, u32[]{:S(2)}, u32[]{:S(2)}) collective-permute-start(f32[2,4,32,128]{3,2,1,0:T(8,128)S(1)} %shard_map.99.refs_0_), channel_id=1, source_target_pairs={{0,48},{8,56},{16,0},{24,8},{32,16},{40,24},{48,32},{56,40},{64,11... | collective-permute-start | bytes 393224 | tf_op jit(solution)/shard_map/ppermute | solution.py:338
  47.8 9.5 %collective-permute-start.24 = (f32[2,4,32,128]{3,2,1,0:T(8,128)S(1)}, f32[2,4,32,128]{3,2,1,0:T(8,128)S(1)}, u32[]{:S(2)}, u32[]{:S(2)}) collective-permute-start(f32[2,4,32,128]{3,2,1,0:T(8,128)S(1)} %shard_map.99.refs_0_), channel_id=1, source_target_pairs={{0,32},{8,40},{16,48},{24,56},{32,0},{40,8},{48,16},{56,24},{64,96... | collective-permute-start | bytes 393224 | tf_op jit(solution)/shard_map/ppermute | solution.py:338
  48.4 10.5 %collective-permute-start.15 = (f32[2,4,32,128]{3,2,1,0:T(8,128)S(1)}, f32[2,4,32,128]{3,2,1,0:T(8,128)S(1)}, u32[]{:S(2)}, u32[]{:S(2)}) collective-permute-start(f32[2,4,32,128]{3,2,1,0:T(8,128)S(1)} %shard_map.98.refs_1_), channel_id=1, source_target_pairs={{0,16},{8,24},{16,32},{24,40},{32,48},{40,56},{48,0},{56,8},{64,80... | collective-permute-start | bytes 393224 | tf_op jit(solution)/shard_map/ppermute | solution.py:338
  48.6 12.2 %collective-permute-start.17 = (f32[2,4,32,128]{3,2,1,0:T(8,128)S(1)}, f32[2,4,32,128]{3,2,1,0:T(8,128)S(1)}, u32[]{:S(2)}, u32[]{:S(2)}) collective-permute-start(f32[2,4,32,128]{3,2,1,0:T(8,128)S(1)} %shard_map.98.refs_1_), channel_id=1, source_target_pairs={{0,32},{8,40},{16,48},{24,56},{32,0},{40,8},{48,16},{56,24},{64,96... | collective-permute-start | bytes 393224 | tf_op jit(solution)/shard_map/ppermute | solution.py:338
  51.4 10.9 %collective-permute-start.19 = (f32[2,4,32,128]{3,2,1,0:T(8,128)S(1)}, f32[2,4,32,128]{3,2,1,0:T(8,128)S(1)}, u32[]{:S(2)}, u32[]{:S(2)}) collective-permute-start(f32[2,4,32,128]{3,2,1,0:T(8,128)S(1)} %shard_map.98.refs_1_), channel_id=1, source_target_pairs={{0,48},{8,56},{16,0},{24,8},{32,16},{40,24},{48,32},{56,40},{64,11... | collective-permute-start | bytes 393224 | tf_op jit(solution)/shard_map/ppermute | solution.py:338
  53.1 10.2 %collective-permute-start.25 = (f32[4,4,32,128]{3,2,1,0:T(8,128)S(1)}, f32[4,4,32,128]{3,2,1,0:T(8,128)S(1)}, u32[]{:S(2)}, u32[]{:S(2)}) collective-permute-start(f32[4,4,32,128]{3,2,1,0:T(8,128)S(1)} %shard_map.100.refs_0_), channel_id=1, source_target_pairs={{0,8},{8,0},{16,24},{24,16},{32,40},{40,32},{48,56},{56,48},{64,72... | collective-permute-start | bytes 786440 | tf_op jit(solution)/shard_map/ppermute | solution.py:338
  57.2 5.0 %collective-permute-start.26 = (f32[2,4,32,128]{3,2,1,0:T(8,128)S(1)}, f32[2,4,32,128]{3,2,1,0:T(8,128)S(1)}, u32[]{:S(2)}, u32[]{:S(2)}) collective-permute-start(f32[2,4,32,128]{3,2,1,0:T(8,128)S(1)} %collective-permute-done.22.refs_1_), channel_id=1, source_target_pairs={{0,8},{8,0},{16,24},{24,16},{32,40},{40,32},{48,56},{56,48},{64,72... | collective-permute-start | bytes 393224 | tf_op jit(solution)/shard_map/ppermute | solution.py:338
  58.9 3.9 %collective-permute-start.27 = (f32[2,4,32,128]{3,2,1,0:T(8,128)S(1)}, f32[2,4,32,128]{3,2,1,0:T(8,128)S(1)}, u32[]{:S(2)}, u32[]{:S(2)}) collective-permute-start(f32[2,4,32,128]{3,2,1,0:T(8,128)S(1)} %collective-permute-done.23.refs_2_), channel_id=1, source_target_pairs={{0,8},{8,0},{16,24},{24,16},{32,40},{40,32},{48,56},{56,48},{64,72... | collective-permute-start | bytes 393224 | tf_op jit(solution)/shard_map/ppermute | solution.py:338
  (12 other events, 100.2 us)
